TPU v7x, 512 devices: a whole 4x8x8 slice. The times are simulated.
512 devices in a mesh: ctx: 64 (over y_hi, x, z), tp: 4 (over y_lo), dp: 2 (over core).
Axes of the slice: x: 4, y: 8 (y_hi: 2, y_lo: 4; y = y_hi * 4 + y_lo), z: 8, core: 2. Of those that a mesh axis runs over, the one named last changes fastest.
Arguments:
- gate_query: bfloat16 [2, 8192, 8192], P('dp', 'ctx', 'tp'), may hold values from -6 to 6
- gate_key: bfloat16 [2, 8192, 8192], P('dp', 'ctx', 'tp'), may hold values from -6 to 6
- input_value: bfloat16 [2, 8192, 8192], P('dp', 'ctx', 'tp'), may hold values from -6 to 6
- out_grad: bfloat16 [2, 8192, 8192], P('dp', 'ctx', 'tp'), may hold values from -16 to 16
- short_taps: float32 [7, 8192], P(None, 'tp'), may hold values from -2 to 2
- long_taps: bfloat16 [128, 8192], P(None, 'tp'), may hold values from -0.5 to 0.5
Outputs:
- query_grad: bfloat16 [2, 8192, 8192], P('dp', 'ctx', 'tp')
- key_grad: bfloat16 [2, 8192, 8192], P('dp', 'ctx', 'tp')
- value_grad: bfloat16 [2, 8192, 8192], P('dp', 'ctx', 'tp')
- long_grad: bfloat16 [128, 8192], P(None, 'tp')
- short_grad: bfloat16 [7, 8192], P(None, 'tp')
All inputs are finite; a program needn't handle non-finite values.
Results may differ from a plain program's by a relative error of at most 0.013.
Values may be sent and summed in bfloat16 or wider, within the bound.
No kernel may reach another device: no remote copies, remote signals or barrier semaphores. Data moves between devices by JAX's collectives and lax.ppermute only.
A program may use at most 64 MiB of HBM per device.

v0:
```python
import math

import jax
import jax.numpy as jnp
from jax import lax
from jax.sharding import PartitionSpec as P

table_precision = lax.Precision.HIGH


def shifted(value, axis, by):
    devices = lax.axis_size(axis)
    pairs = [(i, i + by) for i in range(devices) if 0 <= i + by < devices]
    return lax.ppermute(value, axis, pairs)


def forward_table(period, count):
    half_len = period // 2 + 1
    frequency = lax.iota(jnp.int32, half_len)[:, None]
    places = lax.iota(jnp.int32, count)[None, :]
    angles = (frequency * places % period).astype(jnp.float32) * (2.0 * math.pi / period)
    return jnp.concatenate([jnp.cos(angles), -jnp.sin(angles)], axis=0)


def inverse_table(period, first, count):
    half_len = period // 2 + 1
    frequency = lax.iota(jnp.int32, half_len)[None, :]
    places = lax.iota(jnp.int32, count)[:, None] + first
    angles = (frequency * places % period).astype(jnp.float32) * (2.0 * math.pi / period)
    edge = (frequency == 0) | (frequency == period // 2)
    weight = jnp.where(edge, 1.0, 2.0).astype(jnp.float32) / period
    return jnp.concatenate([weight * jnp.cos(angles), -weight * jnp.sin(angles)], axis=1)


def apply_table(table, signal):
    return jnp.dot(table, signal.astype(jnp.float32), precision=table_precision)


def spectral_product(first_spec, second_spec, conjugate):
    half_len = first_spec.shape[0] // 2
    real_a = first_spec[:half_len]
    imag_a = first_spec[half_len:]
    real_b = second_spec[:half_len]
    imag_b = second_spec[half_len:]
    if conjugate:
        imag_b = -imag_b
    return jnp.concatenate(
        [real_a * real_b - imag_a * imag_b, real_a * imag_b + imag_a * real_b], axis=0
    )


def short_causal(extended, taps, tok_rows):
    short_len = taps.shape[0]
    total = jnp.zeros((tok_rows, taps.shape[1]), jnp.float32)
    for lag in range(short_len):
        total = total + taps[lag] * extended[
            short_len - 1 - lag : short_len - 1 - lag + tok_rows
        ].astype(jnp.float32)
    return total


def short_anti(extended, taps, tok_rows):
    short_len = taps.shape[0]
    total = jnp.zeros((tok_rows, taps.shape[1]), jnp.float32)
    for lag in range(short_len):
        total = total + taps[lag] * extended[lag : lag + tok_rows].astype(jnp.float32)
    return total


def on_device(gate_query, gate_key, input_value, out_grad, short_taps, long_taps):
    query_rows = gate_query[0]
    key_rows = gate_key[0]
    value_rows = input_value[0]
    grad_rows = out_grad[0]
    tok_rows = query_rows.shape[0]
    chan_width = query_rows.shape[1]
    short_len = short_taps.shape[0]
    long_len = long_taps.shape[0]
    period = tok_rows + long_len
    span_len = tok_rows + long_len - 1
    value_rim = shifted(value_rows[tok_rows - short_len + 1 :], "ctx", 1)
    value_ext = jnp.concatenate([value_rim, value_rows], axis=0)
    mixed_value = short_causal(value_ext, short_taps, tok_rows).astype(jnp.bfloat16)
    gated = (key_rows.astype(jnp.float32) * mixed_value.astype(jnp.float32)).astype(jnp.bfloat16)
    gated_rim = shifted(gated[tok_rows - long_len + 1 :], "ctx", 1)
    gated_ext = jnp.concatenate([gated_rim, gated], axis=0)
    mid_grad = (grad_rows.astype(jnp.float32) * query_rows.astype(jnp.float32)).astype(jnp.bfloat16)
    whole_table = forward_table(period, period)
    taps_spec = apply_table(whole_table[:, :long_len], long_taps)
    placed_spec = apply_table(whole_table[:, long_len - 1 : long_len - 1 + tok_rows], mid_grad)
    gated_spec = apply_table(whole_table[:, :span_len], gated_ext)
    long_out = apply_table(
        inverse_table(period, long_len - 1, tok_rows),
        spectral_product(gated_spec, taps_spec, False),
    )
    query_grad = (grad_rows.astype(jnp.float32) * long_out).astype(jnp.bfloat16)
    long_sum = apply_table(
        inverse_table(period, 0, long_len), spectral_product(placed_spec, gated_spec, True)
    )
    mid_rim = shifted(mid_grad[: long_len - 1], "ctx", -1)
    mid_ext = jnp.concatenate([mid_grad, mid_rim], axis=0)
    ext_spec = apply_table(whole_table[:, :span_len], mid_ext)
    gated_grad = apply_table(
        inverse_table(period, 0, tok_rows), spectral_product(ext_spec, taps_spec, True)
    )
    key_grad = (gated_grad * mixed_value.astype(jnp.float32)).astype(jnp.bfloat16)
    mixed_grad = (gated_grad * key_rows.astype(jnp.float32)).astype(jnp.bfloat16)
    mixed_rim = shifted(mixed_grad[: short_len - 1], "ctx", -1)
    mixed_ext = jnp.concatenate([mixed_grad, mixed_rim], axis=0)
    value_grad = short_anti(mixed_ext, short_taps, tok_rows).astype(jnp.bfloat16)
    mixed_wide = mixed_grad.astype(jnp.float32)
    short_sum = jnp.stack(
        [
            jnp.sum(
                mixed_wide
                * value_ext[short_len - 1 - lag : short_len - 1 - lag + tok_rows].astype(
                    jnp.float32
                ),
                axis=0,
            )
            for lag in range(short_len)
        ],
        axis=0,
    )
    limit = math.sqrt((long_len + short_len) * chan_width * lax.axis_size("tp"))
    long_total, short_total = lax.psum((long_sum, short_sum), ("ctx", "dp"))
    local_sq = jnp.sum(long_total * long_total) + jnp.sum(short_total * short_total)
    norm_sq = lax.psum(local_sq, "tp")
    factor = limit / jnp.sqrt(norm_sq + 1e-06)
    long_grad = (factor * long_total).astype(jnp.bfloat16)
    short_grad = (factor * short_total).astype(jnp.bfloat16)
    return (query_grad[None], key_grad[None], value_grad[None], long_grad, short_grad)


def solution(mesh):
    in_specs = (
        P("dp", "ctx", "tp"),
        P("dp", "ctx", "tp"),
        P("dp", "ctx", "tp"),
        P("dp", "ctx", "tp"),
        P(None, "tp"),
        P(None, "tp"),
    )
    out_specs = (
        P("dp", "ctx", "tp"),
        P("dp", "ctx", "tp"),
        P("dp", "ctx", "tp"),
        P(None, "tp"),
        P(None, "tp"),
    )
    return jax.shard_map(
        on_device, mesh=mesh, in_specs=in_specs, out_specs=out_specs, check_vma=False
    )
```

profile of v0, /device:TPU:1, one launch (start us, length us, event | category | flops | bytes accessed | tf_op | source)
XLA Modules:
  0.0 1649.8 jit_solution(10436581971909227488)
XLA Ops:
  7.2 0.0 copy-start
  7.2 0.0 all-reduce.2.cloned.1.call-start
  7.2 0.8 slice_bitcast_fusion
  8.0 4.8 collective-permute-start
  12.9 1.3 fusion.21
  14.2 1.3 collective-permute-start.2
  15.5 0.6 sine_negate_fusion
  16.1 0.0 copy-done
  16.1 0.0 copy-start.8
  16.1 0.7 fusion.69
  16.8 1.8 cosine_multiply_fusion.1
  18.6 0.0 copy-done.8
  18.7 0.0 copy-start.3
  18.7 0.0 copy-start.4
  18.7 0.0 copy-start.5
  18.7 0.0 copy-start.6
  18.7 0.0 copy-start.7
  18.7 8.7 collective-permute-done.2
  27.5 0.7 fusion.42
  28.2 0.5 multiply_subtract_fusion.1
  28.7 0.0 copy-start.1
  28.7 1.2 fusion.5
  29.9 0.0 collective-permute-done
  29.9 0.0 copy-done.3
  29.9 0.0 copy-done.4
  29.9 0.0 copy-done.5
  29.9 0.0 copy-done.6
  29.9 0.0 copy-done.7
  29.9 0.0 copy-done.1
  29.9 0.0 copy-start.2
  30.0 1.8 fusion.46
  31.7 0.0 copy-done.2
  31.7 1.3 fusion.37
  33.1 0.1 slice.170
  33.2 6.1 collective-permute-start.1
  39.3 0.8 fusion.71
  40.1 8.8 collective-permute-done.1
  49.0 0.8 fusion.38
  49.8 0.9 multiply_subtract_fusion
  50.7 2.2 fusion.9
  52.9 0.0 all-reduce.2.cloned.1.call-update
  52.9 0.6 slice.180
  53.5 1.3 collective-permute-start.3
  54.8 0.1 stack.31
  54.9 804.2 %psum.22 = f32[7,2048]{1,0:T(8,128)S(1)} all-reduce(f32[7,2048]{1,0:T(8,128)S(1)} %stack.31), channel_id=1, replica_groups=mesh['ctx'=64,'tp'=4,'dp'=2] {'ctx','dp'}, use_global_device_ids=true, to_apply=%region_9.10 | all-reduce | flops 14336 | bytes 114688 | tf_op jit(solution)/shard_map/psum | solution.py:126
  859.1 0.6 multiply_reduce_fusion.1
  859.7 0.0 collective-permute-done.3
  859.7 2.7 fusion.57
  862.5 762.6 %all-reduce.2.cloned.1.call-done = f32[128,2048]{1,0:T(8,128)} async-done(((f32[128,2048]{1,0:T(8,128)}), f32[128,2048]{1,0:T(8,128)}) %all-reduce.2.cloned.1.call-update) | async-done | bytes 1048592 | tf_op jit(solution)/shard_map/psum | solution.py:126
  1625.0 2.1 multiply_reduce_fusion
  1628.4 3.0 fusion.1
  1631.4 8.1 psum.23
  1640.2 0.6 multiply_convert_fusion.1
  1640.8 2.1 multiply_convert_fusion
  (3 shorter events, 0.0 us)
Async XLA Ops:
  7.2 8.9 copy-start
  7.2 1617.9 %all-reduce.2.cloned.1.call-start = ((), (), s32[]{:S(2)}) async-start(), calls=%async_computation | async-start | bytes 2097152 | tf_op jit(solution)/shard_map/psum | solution.py:126
  8.0 21.8 %collective-permute-start = (bf16[6,2048]{1,0:T(8,128)(2,1)S(1)}, bf16[6,2048]{1,0:T(8,128)(2,1)S(1)}, u32[]{:S(2)}, u32[]{:S(2)}) collective-permute-start(bf16[6,2048]{1,0:T(8,128)(2,1)S(1)} %slice_bitcast_fusion), channel_id=1, source_target_pairs={{0,8},{8,16},{16,24},{24,32},{32,40},{40,48},{48,56},{56,64},{64,7... | collective-permute-start | bytes 73736 | tf_op jit(solution)/shard_map/ppermute | solution.py:14
  14.2 13.2 collective-permute-start.2
  16.1 2.5 copy-start.8
  18.7 11.2 copy-start.3
  18.7 11.2 copy-start.4
  18.7 11.2 copy-start.5
  18.7 11.2 copy-start.6
  18.7 11.2 copy-start.7
  28.7 1.2 copy-start.1
  29.9 1.8 copy-start.2
  33.2 15.7 collective-permute-start.1
  53.5 806.2 %collective-permute-start.3 = (bf16[6,2048]{1,0:T(8,128)(2,1)}, bf16[6,2048]{1,0:T(8,128)(2,1)}, u32[]{:S(2)}, u32[]{:S(2)}) collective-permute-start(bf16[6,2048]{1,0:T(8,128)(2,1)} %slice.180), channel_id=1, source_target_pairs={{8,0},{16,8},{24,16},{32,24},{40,32},{48,40},{56,48},{64,56},{72,6... | collective-permute-start | bytes 73736 | tf_op jit(solution)/shard_map/ppermute | solution.py:14
Sparse Core Ops, SparseCore 0:
  53.0 1571.9 all-reduce.1
where the time goes:
time: 1660 us; the launch traced here: 1650 us
  blocking collectives  812 us (49%)
  waiting for transfers between devices  780 us (47%)
    psum x1, blocking collectives, on_device(): long_total, short_total = lax.psum((long_sum, short_sum), ('ctx', 'dp'))  804 us
    psum x1, waiting for transfers between devices, on_device(): long_total, short_total = lax.psum((long_sum, short_sum), ('ctx', 'dp'))  763 us
  transfers between devices with their start and end apart: 5, of which 3 were waited for; matrix products, arithmetic and copies ran while one was open for 1% of the time, Pallas kernels for 0%

commit v1 on v0

v1 whole, which is shorter than its diff:
```python
import math

import jax
import jax.numpy as jnp
import numpy as np
from jax import lax
from jax.experimental import pallas as pl
from jax.experimental.pallas import tpu as pltpu
from jax.sharding import PartitionSpec as P

BF = jnp.bfloat16
F32 = jnp.float32
ROWS = 128
PIECES = 64
WIDTH = 512
VMEM = 48 * 1024 * 1024


def split_table(table):
    high = table.astype(np.float32).astype(jnp.bfloat16)
    low = (table - high.astype(np.float64)).astype(np.float32).astype(jnp.bfloat16)
    return high, low


def tables():
    freq = np.arange(128)[:, None]
    place = np.arange(256)[None, :]
    angle = (freq * place % 256) * (2.0 * np.pi / 256)
    fwd = np.concatenate([np.cos(angle), -np.sin(angle)], axis=0)
    fwd[128] = 1.0 - 2.0 * (np.arange(256) % 2)
    weight = np.full((256,), 2.0 / 256)
    weight[0] = weight[128] = 1.0 / 256
    inv = (fwd * weight[:, None]).T[:ROWS]
    fwd_hi, fwd_lo = split_table(fwd)
    inv_hi, inv_lo = split_table(inv)
    near = np.concatenate([fwd_hi[:, :128], fwd_lo[:, :128]], axis=1)
    far = np.concatenate([fwd_hi[:, 128:], fwd_lo[:, 128:]], axis=1)
    inv_both = np.concatenate([inv_hi, inv_lo], axis=0)
    return fwd_hi, fwd_lo, near, far, inv_both


def half_of(slot, core):
    return jnp.where(core == 0, 1 - slot, slot)


def gate_kernel(core_ref, query_ref, key_ref, value_ref, grad_ref, taps_ref, mid_ref, gated_ref, mixed_ref, wide_ref):
    short_len = taps_ref.shape[0]
    mid_ref[0] = (grad_ref[...].astype(F32) * query_ref[...].astype(F32)).astype(BF)
    wide_ref[0:8, :] = jnp.zeros((8, wide_ref.shape[1]), F32)
    wide_ref[8:, :] = value_ref[...].astype(F32)
    total = taps_ref[0:1, :] * wide_ref[8 : 8 + ROWS, :]
    for lag in range(1, short_len):
        total = total + taps_ref[lag : lag + 1, :] * wide_ref[8 - lag : 8 - lag + ROWS, :]
    mixed = total.astype(BF)
    mixed_ref[0] = mixed
    gated_ref[0] = (key_ref[...].astype(F32) * mixed.astype(F32)).astype(BF)


def head_kernel(core_ref, rim_ref, value_ref, key_ref, taps_ref, mixed_ref, gated_ref, wide_ref):
    short_len = taps_ref.shape[0]
    wide_ref[0:8, :] = rim_ref[...].astype(F32)
    wide_ref[8:, :] = value_ref[...].astype(F32)
    total = taps_ref[0:1, :] * wide_ref[8:24, :]
    for lag in range(1, short_len):
        total = total + taps_ref[lag : lag + 1, :] * wide_ref[8 - lag : 24 - lag, :]
    mixed = total.astype(BF)
    mixed_ref[0] = mixed
    gated_ref[0] = (key_ref[...].astype(F32) * mixed.astype(F32)).astype(BF)


def dot(left, right):
    return jnp.dot(left, right, preferred_element_type=F32)


def product(first, second, conjugate):
    first_re, first_im = first[:128], first[128:]
    second_re, second_im = second[:128], second[128:]
    edge = lax.broadcasted_iota(jnp.int32, first_re.shape, 0) == 0
    cross = first_im * second_im
    inner = jnp.where(edge, 0.0, cross)
    if conjugate:
        real = first_re * second_re + inner
        imag = first_im * second_re - first_re * second_im
    else:
        real = first_re * second_re - inner
        imag = first_re * second_im + first_im * second_re
    return jnp.concatenate([real, jnp.where(edge, cross, imag)], axis=0)


def inverse(inv_ref, spec):
    high = spec.astype(BF)
    low = (spec - high.astype(F32)).astype(BF)
    both = dot(inv_ref[...], high)
    return both[:ROWS] + both[ROWS:] + dot(inv_ref[0:ROWS, :], low)


def filter_kernel(
    core_ref, gated_ref, gated_head_ref, prev_ref, prev_head_ref, mid_ref, next_ref, mixed_ref, mixed_head_ref,
    key_ref, value_ref, rim_ref, grad_ref, short_ref, long_ref, hi_ref, lo_ref, near_ref, far_ref, inv_ref, *rest,
):
    query_out, key_out, value_out, top_out, end_out, part_ref, wide_ref, mixed_grad_ref = rest[-8:]
    short_len = short_ref.shape[0]
    width = wide_ref.shape[1]
    gated = jnp.concatenate([gated_head_ref[0], gated_ref[0, 16:], prev_head_ref[0], prev_ref[0, 16:]], axis=0)
    mid = mid_ref[0]
    ahead = next_ref[0]
    taps = long_ref[...]
    gated_spec = dot(hi_ref[...], gated) + dot(lo_ref[...], gated)
    mid_spec = dot(near_ref[...], jnp.concatenate([mid, mid], axis=0))
    both_spec = mid_spec + dot(far_ref[...], jnp.concatenate([ahead, ahead], axis=0))
    taps_spec = dot(near_ref[...], jnp.concatenate([taps, taps], axis=0))
    long_sum = inverse(inv_ref, product(mid_spec, gated_spec, True))
    gated_grad = inverse(inv_ref, product(both_spec, taps_spec, True))
    long_out = inverse(inv_ref, product(gated_spec, taps_spec, False))
    query_out[...] = (grad_ref[...].astype(F32) * long_out).astype(BF)
    mixed = jnp.concatenate([mixed_head_ref[0], mixed_ref[0, 16:]], axis=0)
    key_out[...] = (gated_grad * mixed.astype(F32)).astype(BF)
    mixed_grad = (gated_grad * key_ref[...].astype(F32)).astype(BF)
    top_out[...] = mixed_grad[0:16]
    end_out[...] = mixed_grad[ROWS - 16 :]
    mixed_grad = mixed_grad.astype(F32)
    mixed_grad_ref[0:ROWS, :] = mixed_grad
    mixed_grad_ref[ROWS:, :] = jnp.zeros((8, width), F32)
    wide_ref[0:8, :] = rim_ref[...].astype(F32)
    wide_ref[8:, :] = value_ref[...].astype(F32)
    total = short_ref[0:1, :] * mixed_grad
    sums = [jnp.sum(mixed_grad * wide_ref[8 : 8 + ROWS, :], axis=0, keepdims=True)]
    for lag in range(1, short_len):
        total = total + short_ref[lag : lag + 1, :] * mixed_grad_ref[lag : lag + ROWS, :]
        sums.append(jnp.sum(mixed_grad * wide_ref[8 - lag : 8 - lag + ROWS, :], axis=0, keepdims=True))
    value_out[...] = total.astype(BF)
    short_sum = jnp.concatenate(sums + [jnp.zeros((16 - short_len, width), F32)], axis=0)
    for block in range(width // 128):
        lanes = slice(block * 128, block * 128 + 128)
        part_ref[block, 0:ROWS, :] = long_sum[:, lanes].astype(part_ref.dtype)
        part_ref[block, ROWS : ROWS + 16, :] = short_sum[:, lanes].astype(part_ref.dtype)


def tail_kernel(end_ref, rim_ref, taps_ref, old_ref, out_ref, wide_ref):
    short_len = taps_ref.shape[0]
    wide_ref[0:16, :] = end_ref[...].astype(F32)
    wide_ref[16:, :] = rim_ref[...].astype(F32)
    total = taps_ref[0:1, :] * wide_ref[0:16, :]
    for lag in range(1, short_len):
        total = total + taps_ref[lag : lag + 1, :] * wide_ref[lag : lag + 16, :]
    out_ref[...] = total.astype(BF)


def params():
    return pltpu.CompilerParams(vmem_limit_bytes=VMEM)


def shifted(value, by):
    devices = lax.axis_size("ctx")
    return lax.ppermute(value, "ctx", [(i, i + by) for i in range(devices) if 0 <= i + by < devices])


def on_device(gate_query, gate_key, input_value, out_grad, short_taps, long_taps):
    query_rows, key_rows, value_rows, grad_rows = gate_query[0], gate_key[0], input_value[0], out_grad[0]
    chan_width = query_rows.shape[1]
    half_width = chan_width // 2
    short_len, long_len = short_taps.shape[0], long_taps.shape[0]
    core = lax.axis_index("dp").astype(jnp.int32).reshape(1)
    devices = lax.axis_size("ctx")
    per_half = half_width // WIDTH
    struct = jax.ShapeDtypeStruct

    value_rim = shifted(value_rows[ROWS - 8 :], 1)

    def slot_map(i, core):
        return (half_of(i // per_half, core[0]), 0, i % per_half)

    whole = pl.BlockSpec((ROWS, WIDTH), lambda i, core: (0, i))
    by_slot = pl.BlockSpec((1, ROWS, WIDTH), slot_map)
    halves = struct((2, ROWS, half_width), BF)
    mid, gated, mixed = pl.pallas_call(
        gate_kernel,
        out_shape=(halves, halves, halves),
        grid_spec=pltpu.PrefetchScalarGridSpec(
            num_scalar_prefetch=1,
            grid=(chan_width // WIDTH,),
            in_specs=[whole, whole, whole, whole, pl.BlockSpec((short_len, WIDTH), lambda i, core: (0, i))],
            out_specs=[by_slot, by_slot, by_slot],
            scratch_shapes=[pltpu.VMEM((ROWS + 8, WIDTH), F32)],
        ),
        compiler_params=params(),
        name="gates",
    )(core, query_rows, key_rows, value_rows, grad_rows, short_taps)

    prev_parts = [shifted(gated[slot], 1) for slot in range(2)]
    next_parts = [shifted(mid[slot], -1) for slot in range(2)]

    head_in = pl.BlockSpec((16, WIDTH), lambda i, core: (0, i))
    head_out = pl.BlockSpec((1, 16, WIDTH), slot_map)
    heads = struct((2, 16, half_width), BF)
    mixed_head, gated_head = pl.pallas_call(
        head_kernel,
        out_shape=(heads, heads),
        grid_spec=pltpu.PrefetchScalarGridSpec(
            num_scalar_prefetch=1,
            grid=(chan_width // WIDTH,),
            in_specs=[
                pl.BlockSpec((8, WIDTH), lambda i, core: (0, i)),
                head_in,
                head_in,
                pl.BlockSpec((short_len, WIDTH), lambda i, core: (0, i)),
            ],
            out_specs=[head_out, head_out],
            scratch_shapes=[pltpu.VMEM((24, WIDTH), F32)],
        ),
        compiler_params=params(),
        name="head",
    )(core, value_rim, value_rows, key_rows, short_taps)
    prev_head = shifted(gated_head, 1)

    fwd_hi, fwd_lo, near, far, inv_both = (jnp.asarray(t) for t in tables())

    def run_filter(slot, kept):
        def chan(rows):
            return pl.BlockSpec((rows, WIDTH), lambda i, core: (0, half_of(slot, core[0]) * per_half + i))

        def held(rows):
            return pl.BlockSpec((1, rows, WIDTH), lambda i, core: (slot, 0, i))

        sent = pl.BlockSpec((1, ROWS, WIDTH), lambda i, core: (0, 0, i))
        table = pl.BlockSpec((256, 256), lambda i, core: (0, 0))
        wide = struct((ROWS, chan_width), BF)
        rim = struct((16, chan_width), BF)
        part = struct((half_width // 128, ROWS + 16, 128), BF if slot == 0 else F32)
        in_specs = [
            held(ROWS), held(16), sent, held(16), held(ROWS), sent, held(ROWS), held(16),
            chan(ROWS), chan(ROWS), chan(8), chan(ROWS), chan(short_len), chan(long_len),
            table, table, table, table, table,
        ]
        first = 1 + len(in_specs)
        return pl.pallas_call(
            filter_kernel,
            out_shape=(wide, wide, wide, rim, rim, part),
            grid_spec=pltpu.PrefetchScalarGridSpec(
                num_scalar_prefetch=1,
                grid=(per_half,),
                in_specs=in_specs + [pl.BlockSpec(memory_space=pl.ANY)] * len(kept),
                out_specs=[
                    chan(ROWS), chan(ROWS), chan(ROWS), chan(16), chan(16),
                    pl.BlockSpec((WIDTH // 128, ROWS + 16, 128), lambda i, core: (i, 0, 0)),
                ],
                scratch_shapes=[pltpu.VMEM((ROWS + 8, WIDTH), F32), pltpu.VMEM((ROWS + 8, WIDTH), F32)],
            ),
            input_output_aliases={first + k: k for k in range(len(kept))},
            compiler_params=params(),
            name=f"filters_{slot}",
        )(
            core, gated, gated_head, prev_parts[slot][None], prev_head, mid, next_parts[slot][None], mixed, mixed_head,
            key_rows, value_rows, value_rim, grad_rows, short_taps, long_taps, fwd_hi, fwd_lo, near, far, inv_both, *kept,
        )

    *kept, part_sent = run_filter(0, ())
    part_got = lax.ppermute(part_sent, "dp", [(0, 1), (1, 0)])
    query_grad, key_grad, value_grad, mixed_top, mixed_end, part_own = run_filter(1, tuple(kept))

    blocks = half_width // 128
    groups = PIECES // blocks
    total = part_own + part_got.astype(F32)
    long_part = total[:, :ROWS].reshape(blocks, groups, ROWS // groups, 128)
    short_part = total[:, ROWS : ROWS + groups].reshape(blocks, groups, 1, 128)
    pieces = jnp.concatenate([long_part, short_part], axis=2).astype(BF)
    depth = pieces.shape[2]
    owned = PIECES // devices
    arrived = lax.all_to_all(pieces.reshape(PIECES, depth, 128), "ctx", 0, 0, tiled=True)
    summed = jnp.sum(arrived.reshape(devices, owned, depth, 128).astype(F32), axis=0)
    square = jnp.sum(summed * summed, axis=(1, 2), keepdims=True)
    high = square.astype(BF)
    low = (square - high.astype(F32)).astype(BF)
    line = (owned, 1, 128)
    message = jnp.concatenate([summed.astype(BF), jnp.broadcast_to(high, line), jnp.broadcast_to(low, line)], axis=1)
    spread = jnp.broadcast_to(message[None], (devices,) + message.shape).reshape(PIECES, depth + 2, 128)
    gathered = lax.all_to_all(spread, "ctx", 0, 0, tiled=True)
    gathered = lax.all_gather(gathered, "dp")
    gathered = gathered.reshape(2, blocks, groups, depth + 2, 128)
    local_sq = jnp.sum(gathered[:, :, :, depth:, 0].astype(F32))
    ways = lax.axis_size("tp")
    norms = lax.all_to_all(jnp.full((ways, 8, 128), local_sq, F32), "tp", 0, 0, tiled=True)
    norm_sq = jnp.sum(norms[:, 0, 0])
    limit = math.sqrt((long_len + short_len) * chan_width * ways)
    factor = limit / jnp.sqrt(norm_sq + 1e-06)
    long_total = gathered[:, :, :, : depth - 1].transpose(2, 3, 0, 1, 4).reshape(long_len, chan_width)
    short_total = gathered[:, :, :, depth - 1].transpose(2, 0, 1, 3).reshape(groups, chan_width)[:short_len]
    long_grad = (factor * long_total.astype(F32)).astype(BF)
    short_grad = (factor * short_total.astype(F32)).astype(BF)

    mixed_rim = shifted(mixed_top, -1)
    value_grad = pl.pallas_call(
        tail_kernel,
        out_shape=struct((ROWS, chan_width), BF),
        grid=(1,),
        in_specs=[
            pl.BlockSpec((16, chan_width), lambda i: (0, 0)),
            pl.BlockSpec((16, chan_width), lambda i: (0, 0)),
            pl.BlockSpec((short_len, chan_width), lambda i: (0, 0)),
            pl.BlockSpec(memory_space=pl.ANY),
        ],
        out_specs=pl.BlockSpec((16, chan_width), lambda i: (ROWS // 16 - 1, 0)),
        scratch_shapes=[pltpu.VMEM((32, chan_width), F32)],
        input_output_aliases={3: 0},
        compiler_params=params(),
        name="tail",
    )(mixed_end, mixed_rim, short_taps, value_grad)
    return (query_grad[None], key_grad[None], value_grad[None], long_grad, short_grad)


def solution(mesh):
    split = P("dp", "ctx", "tp")
    taps = P(None, "tp")
    return jax.shard_map(
        on_device,
        mesh=mesh,
        in_specs=(split, split, split, split, taps, taps),
        out_specs=(split, split, split, taps, taps),
        check_vma=False,
    )
```

time: 1660 us -> 163 us (0.10)
  blocking collectives: 812 us -> 59 us
  waiting for transfers between devices: 780 us -> 28.9 us
  starting transfers between devices: 13.5 us -> 47.6 us
    psum x2 -> x0, blocking collectives: 812 us -> none  [the longest x1 804 us: on_device(): long_total, short_total = lax.psum((long_sum, short_sum), ('ctx', 'dp'))]
    psum x1 -> x0, waiting for transfers between devices: 763 us -> none  [on_device(): long_total, short_total = lax.psum((long_sum, short_sum), ('ctx', 'dp'))]
    all_to_all x0 -> x1, blocking collectives: none -> 54.7 us  [on_device(): lax.all_to_all(pieces.reshape(PIECES, depth, 128), 'ctx', 0, 0, tiled=True)]
    all_to_all x0 -> x2, starting transfers between devices: none -> 19.4 us  [the longest x1 9.81 us: on_device(): gathered = lax.all_to_all(spread, 'ctx', 0, 0, tiled=True)]
  transfers between devices with their start and end apart: 5 -> 10, of which waited for: 3 -> 7; matrix products, arithmetic and copies ran while one was open for 1% -> 0% of each run, Pallas kernels for 0% -> 3%
where the time goes in v1:
time: 163 us; the launch traced here: 162 us
  blocking collectives  59 us (36%)
  starting transfers between devices  47.6 us (29%)
  waiting for transfers between devices  28.9 us (18%)
  Pallas kernels  12.2 us (7%)
  local copies, waits for them, and re-layouts  8.54 us (5%)
  between operations  2.95 us (2%)
  other arithmetic  2.91 us (2%)
    all_to_all x1, blocking collectives, on_device(): lax.all_to_all(pieces.reshape(PIECES, depth, 128), 'ctx', 0, 0, tiled=True)  54.7 us
    ppermute x7, starting transfers between devices, shifted(): lax.ppermute(value, 'ctx', [(i, i + by) for i in range(devices) if 0 <= i...  21.6 us
    ppermute x7, waiting for transfers between devices, shifted(): lax.ppermute(value, 'ctx', [(i, i + by) for i in range(devices) if 0 <= i...  17.6 us
    all_to_all x1, starting transfers between devices, on_device(): gathered = lax.all_to_all(spread, 'ctx', 0, 0, tiled=True)  9.81 us
    all_to_all x1, starting transfers between devices, on_device(): lax.all_to_all(jnp.full((ways, 8, 128), local_sq, F32), 'tp', 0, 0, tiled...  9.62 us
    pallas_call x2, Pallas kernels, run_filter(): pl.pallas_call(filter_kernel, out_shape=(wide, wide, wide, rim, rim, part...  8.63 us
    all_to_all x1, waiting for transfers between devices, on_device(): gathered = lax.all_to_all(spread, 'ctx', 0, 0, tiled=True)  6.82 us
    ppermute x1, starting transfers between devices, on_device(): part_got = lax.ppermute(part_sent, 'dp', [(0, 1), (1, 0)])  6.55 us
  transfers between devices with their start and end apart: 10, of which 7 were waited for; matrix products, arithmetic and copies ran while one was open for 0% of the time, Pallas kernels for 3%

profile of v1, /device:TPU:1, one launch (start us, length us, event | category | flops | bytes accessed | tf_op | source)
XLA Modules:
  0.0 162.1 jit_solution(3300460002081042963)
XLA Ops:
  0.6 0.0 copy-start
  0.6 1.0 copy-done
  1.7 1.0 copy-done.2
  2.7 1.0 copy-done.3
  3.8 0.8 copy-done.6
  4.6 1.0 copy-done.8
  5.6 2.3 %gates.1 = (bf16[2,128,1024]{2,1,0:T(8,128)(2,1)S(1)}, bf16[2,128,1024]{2,1,0:T(8,128)(2,1)S(1)}, bf16[2,128,1024]{2,1,0:T(8,128)(2,1)S(1)}) custom-call(s32[1]{0:T(128)} %bitcast.core_ref, bf16[128,2048]{1,0:T(8,128)(2,1)S(1)} %bitcast.57, bf16[128,2048]{1,0:T(8,128)(2,1)S(1)} %bitcast.50, bf16[128,2048]{1,0:T(8,128)(2,1)S(1)} %bitcast.46, ...), custom_call_target="tpu_custom_call" | custom-call | tf_op jit(solution)/shard_map/gates/pallas_call | solution.py:176
  8.0 0.0 copy-start.13
  8.0 4.8 %collective-permute-start.4 = (bf16[128,1024]{1,0:T(8,128)(2,1)S(1)}, bf16[128,1024]{1,0:T(8,128)(2,1)S(1)}, u32[]{:S(2)}, u32[]{:S(2)}) collective-permute-start(bf16[128,1024]{1,0:T(8,128)(2,1)S(1)} %get-tuple-element.41), channel_id=1, source_target_pairs={{0,8},{8,16},{16,24},{24,32},{32,40},{40,48},{48,56},{56,64},{64,7... | collective-permute-start | bytes 786440 | tf_op jit(solution)/shard_map/ppermute | solution.py:155
  12.9 0.0 copy-start.1
  12.9 0.0 copy-start.9
  12.9 0.0 copy-start.10
  12.9 0.0 copy-start.11
  12.9 0.0 copy-start.12
  13.0 0.0 copy-start.7
  13.0 1.4 collective-permute-start.5
  14.4 0.0 copy-start.4
  14.4 0.0 copy-start.5
  14.4 4.7 %collective-permute-start = (bf16[8,2048]{1,0:T(8,128)(2,1)S(1)}, bf16[8,2048]{1,0:T(8,128)(2,1)S(1)}, u32[]{:S(2)}, u32[]{:S(2)}) collective-permute-start(bf16[8,2048]{1,0:T(8,128)(2,1)S(1)} %slice_bitcast_fusion.5), channel_id=1, source_target_pairs={{0,8},{8,16},{16,24},{24,32},{32,40},{40,48},{48,56},{56,64},{64,7... | collective-permute-start | bytes 98312 | tf_op jit(solution)/shard_map/ppermute | solution.py:155
  19.2 1.0 collective-permute-done.rim_ref
  20.2 0.0 copy-done.1
  20.2 0.0 copy-done.7
  20.2 0.4 head.1
  20.7 4.0 %collective-permute-start.2 = (bf16[2,16,1024]{2,1,0:T(8,128)(2,1)S(1)}, bf16[2,16,1024]{2,1,0:T(8,128)(2,1)S(1)}, u32[]{:S(2)}, u32[]{:S(2)}) collective-permute-start(bf16[2,16,1024]{2,1,0:T(8,128)(2,1)S(1)} %get-tuple-element.23.gated_head_ref), channel_id=1, source_target_pairs={{0,8},{8,16},{16,24},{24,32},{32,40},{40,48},{48,56},{56,64},{64,7... | collective-permute-start | bytes 196616 | tf_op jit(solution)/shard_map/ppermute | solution.py:155
  24.7 1.3 collective-permute-done.2.prev_head_ref
  26.0 0.0 collective-permute-done.4
  26.0 0.0 collective-permute-done.5
  26.0 0.0 copy-done.13
  26.0 0.0 copy-done.9
  26.0 0.0 copy-done.10
  26.0 0.0 copy-done.11
  26.0 0.0 copy-done.12
  26.1 4.3 %filters_0.1 = (bf16[128,2048]{1,0:T(8,128)(2,1)}, bf16[128,2048]{1,0:T(8,128)(2,1)}, bf16[128,2048]{1,0:T(8,128)(2,1)}, bf16[16,2048]{1,0:T(8,128)(2,1)S(1)}, b...) custom-call(s32[1]{0:T(128)} %bitcast.core_ref, bf16[2,128,1024]{2,1,0:T(8,128)(2,1)S(1)} %get-tuple-element.22.gated_ref, ...), custom_call_target="tpu_custom_call" | custom-call | tf_op jit(solution)/shard_map/filters_0/pallas_call | solution.py:236
  30.4 6.5 %collective-permute-start.7 = (bf16[8,144,128]{2,1,0:T(8,128)(2,1)S(1)}, bf16[8,144,128]{2,1,0:T(8,128)(2,1)S(1)}, u32[]{:S(2)}, u32[]{:S(2)}) collective-permute-start(bf16[8,144,128]{2,1,0:T(8,128)(2,1)S(1)} %get-tuple-element.38), channel_id=1, source_target_pairs={{0,1},{1,0},{2,3},{3,2},{4,5},{5,4},{6,7},{7,6},{8,9},{9,8},{10,11... | collective-permute-start | bytes 884744 | tf_op jit(solution)/shard_map/ppermute | solution.py:258
  36.9 4.0 %collective-permute-start.1 = (bf16[128,1024]{1,0:T(8,128)(2,1)S(1)}, bf16[128,1024]{1,0:T(8,128)(2,1)S(1)}, u32[]{:S(2)}, u32[]{:S(2)}) collective-permute-start(bf16[128,1024]{1,0:T(8,128)(2,1)S(1)} %get-tuple-element.42), channel_id=1, source_target_pairs={{0,8},{8,16},{16,24},{24,32},{32,40},{40,48},{48,56},{56,64},{64,7... | collective-permute-start | bytes 786440 | tf_op jit(solution)/shard_map/ppermute | solution.py:155
  41.0 1.3 collective-permute-start.3
  42.3 4.4 %collective-permute-done.1 = bf16[128,1024]{1,0:T(8,128)(2,1)S(1)} collective-permute-done((bf16[128,1024]{1,0:T(8,128)(2,1)S(1)}, bf16[128,1024]{1,0:T(8,128)(2,1)S(1)}, u32[]{:S(2)}, u32[]{:S(2)}) %collective-permute-start.1) | collective-permute-done | bytes 262176 | tf_op jit(solution)/shard_map/ppermute | solution.py:155
  46.6 4.8 %collective-permute-done.3 = bf16[128,1024]{1,0:T(8,128)(2,1)S(1)} collective-permute-done((bf16[128,1024]{1,0:T(8,128)(2,1)S(1)}, bf16[128,1024]{1,0:T(8,128)(2,1)S(1)}, u32[]{:S(2)}, u32[]{:S(2)}) %collective-permute-start.3) | collective-permute-done | bytes 262176 | tf_op jit(solution)/shard_map/ppermute | solution.py:155
  51.5 4.3 %filters_1.1 = (bf16[128,2048]{1,0:T(8,128)(2,1)}, bf16[128,2048]{1,0:T(8,128)(2,1)}, bf16[128,2048]{1,0:T(8,128)(2,1)}, bf16[16,2048]{1,0:T(8,128)(2,1)S(1)}, b...) custom-call(s32[1]{0:T(128)} %bitcast.core_ref, ...), custom_call_target="tpu_custom_call", output_to_operand_aliasing={{0}: (20, {}), {1}: (21, {}), {2}: (22, {}), {3}: (23, {}),... | custom-call | tf_op jit(solution)/shard_map/filters_1/pallas_call | solution.py:236
  55.8 0.0 collective-permute-done.7
  55.8 0.1 add_convert_fusion
  56.0 54.7 %all_to_all.15 = bf16[64,17,128]{2,1,0:T(8,128)(2,1)S(1)} all-to-all(bf16[64,17,128]{2,1,0:T(8,128)(2,1)S(1)} %pad_maximum_fusion), channel_id=1, replica_groups=mesh['ctx'=64,'tp'=4,'dp'=2] {'ctx'}, dimensions={0} | all-to-all | bytes 557056 | tf_op jit(solution)/shard_map/all_to_all | solution.py:269
  110.6 0.1 convert_reduce_fusion
  110.7 0.6 multiply_reduce_fusion
  112.6 0.1 pad.1.clone
  112.7 0.1 pad.2.clone
  112.8 0.1 maximum_bitcast_fusion
  112.9 0.8 reshape.67
  113.7 9.8 %all-to-all-start.1 = ((bf16[64,19,128]{2,1,0:T(8,128)(2,1)}), bf16[64,19,128]{2,1,0:T(8,128)(2,1)S(1)}, u32[]{:S(2)}, u32[]{:S(2)}) async-start(bf16[64,19,128]{2,1,0:T(8,128)(2,1)} %reshape.67), calls=%async_computation.1 | async-start | bytes 786432 | tf_op jit(solution)/shard_map/all_to_all | solution.py:277
  123.5 1.3 collective-permute-start.6
  124.8 6.1 %collective-permute-done.6.rim_ref = bf16[16,2048]{1,0:T(8,128)(2,1)S(1)} collective-permute-done((bf16[16,2048]{1,0:T(8,128)(2,1)S(1)}, bf16[16,2048]{1,0:T(8,128)(2,1)S(1)}, u32[]{:S(2)}, u32[]{:S(2)}) %collective-permute-start.6) | collective-permute-done | bytes 65568 | tf_op jit(solution)/shard_map/ppermute | solution.py:155
  130.9 0.9 tail.1
  131.7 6.8 %all-to-all-done.1 = bf16[64,19,128]{2,1,0:T(8,128)(2,1)S(1)} async-done(((bf16[64,19,128]{2,1,0:T(8,128)(2,1)}), bf16[64,19,128]{2,1,0:T(8,128)(2,1)S(1)}, u32[]{:S(2)}, u32[]{:S(2)}) %all-to-all-start.1) | async-done | bytes 311328 | tf_op jit(solution)/shard_map/all_to_all | solution.py:277
  138.6 0.1 copy.34
  138.6 4.3 %all-gather = bf16[128,19,128]{2,0,1:T(8,128)(2,1)S(1)} all-gather(bf16[64,19,128]{2,0,1:T(8,128)(2,1)S(1)} %copy.34), channel_id=2, replica_groups=mesh['ctx'=64,'tp'=4,'dp'=2] {'dp'}, dimensions={0}, use_global_device_ids=true | all-gather | bytes 933888 | tf_op jit(solution)/shard_map/all_gather | solution.py:278
  143.0 0.6 convert_reduce_fusion.1
  143.6 1.3 broadcast_in_dim.60
  144.9 9.6 %all-to-all-start.2 = ((f32[4,8,128]{2,1,0:T(8,128)}), f32[4,8,128]{2,1,0:T(8,128)S(1)}, u32[]{:S(2)}, u32[]{:S(2)}) async-start(f32[4,8,128]{2,1,0:T(8,128)} %broadcast_in_dim.60), calls=%async_computation.2 | async-start | bytes 32768 | tf_op jit(solution)/shard_map/all_to_all | solution.py:282
  154.5 4.5 %all-to-all-done.2 = f32[4,8,128]{2,1,0:T(8,128)S(1)} async-done(((f32[4,8,128]{2,1,0:T(8,128)}), f32[4,8,128]{2,1,0:T(8,128)S(1)}, u32[]{:S(2)}, u32[]{:S(2)}) %all-to-all-start.2) | async-done | bytes 16416 | tf_op jit(solution)/shard_map/all_to_all | solution.py:282
  158.9 0.6 slice_reduce_fusion
  160.2 0.2 fusion
  160.4 0.6 multiply_convert_fusion.1
  161.0 0.1 copy.36
  161.1 1.0 convert_element_type.71
  (14 shorter events, 0.2 us)
Async XLA Ops:
  0.6 1.0 copy-start
  1.7 1.0 copy-start.2
  2.7 1.0 copy-start.3
  3.8 0.8 copy-start.6
  4.6 1.0 copy-start.8
  8.0 18.0 %copy-start.13 = (bf16[256,256]{1,0:T(8,128)(2,1)S(1)}, bf16[256,256]{1,0:T(8,128)(2,1)}, u32[]{:S(2)}) copy-start(bf16[256,256]{1,0:T(8,128)(2,1)} %constant.20.clone.hi_ref) | copy-start | bytes 393220
  8.0 18.0 %collective-permute-start.4 = (bf16[128,1024]{1,0:T(8,128)(2,1)S(1)}, bf16[128,1024]{1,0:T(8,128)(2,1)S(1)}, u32[]{:S(2)}, u32[]{:S(2)}) collective-permute-start(bf16[128,1024]{1,0:T(8,128)(2,1)S(1)} %get-tuple-element.41), channel_id=1, source_target_pairs={{0,8},{8,16},{16,24},{24,32},{32,40},{40,48},{48,56},{56,64},{64,7... | collective-permute-start | bytes 786440 | tf_op jit(solution)/shard_map/ppermute | solution.py:155
  12.9 7.3 %copy-start.1 = (bf16[1,128,2048]{2,1,0:T(8,128)(2,1)S(1)}, bf16[1,128,2048]{2,1,0:T(8,128)(2,1)}, u32[]{:S(2)}) copy-start(bf16[1,128,2048]{2,1,0:T(8,128)(2,1)} %param.13) | copy-start | bytes 1572868
  12.9 13.1 %copy-start.9 = (bf16[256,256]{1,0:T(8,128)(2,1)S(1)}, bf16[256,256]{1,0:T(8,128)(2,1)}, u32[]{:S(2)}) copy-start(bf16[256,256]{1,0:T(8,128)(2,1)} %constant.24.clone.inv_ref) | copy-start | bytes 393220
  12.9 13.1 %copy-start.10 = (bf16[256,256]{1,0:T(8,128)(2,1)S(1)}, bf16[256,256]{1,0:T(8,128)(2,1)}, u32[]{:S(2)}) copy-start(bf16[256,256]{1,0:T(8,128)(2,1)} %constant.23.clone.far_ref) | copy-start | bytes 393220
  12.9 13.1 %copy-start.11 = (bf16[256,256]{1,0:T(8,128)(2,1)S(1)}, bf16[256,256]{1,0:T(8,128)(2,1)}, u32[]{:S(2)}) copy-start(bf16[256,256]{1,0:T(8,128)(2,1)} %constant.22.clone.near_ref) | copy-start | bytes 393220
  12.9 13.1 %copy-start.12 = (bf16[256,256]{1,0:T(8,128)(2,1)S(1)}, bf16[256,256]{1,0:T(8,128)(2,1)}, u32[]{:S(2)}) copy-start(bf16[256,256]{1,0:T(8,128)(2,1)} %constant.21.clone.lo_ref) | copy-start | bytes 393220
  13.0 7.2 %copy-start.7 = (f32[7,2048]{1,0:T(8,128)S(1)}, f32[7,2048]{1,0:T(8,128)}, u32[]{:S(2)}) copy-start(f32[7,2048]{1,0:T(8,128)} %taps_ref.5) | copy-start | bytes 172036
  13.0 13.0 %collective-permute-start.5 = (bf16[128,1024]{1,0:T(8,128)(2,1)S(1)}, bf16[128,1024]{1,0:T(8,128)(2,1)S(1)}, u32[]{:S(2)}, u32[]{:S(2)}) collective-permute-start(bf16[128,1024]{1,0:T(8,128)(2,1)S(1)} %get-tuple-element.39), channel_id=1, source_target_pairs={{8,0},{16,8},{24,16},{32,24},{40,32},{48,40},{56,48},{64,56},{72,6... | collective-permute-start | bytes 786440 | tf_op jit(solution)/shard_map/ppermute | solution.py:155
  14.4 11.6 %copy-start.4 = (bf16[1,128,2048]{2,1,0:T(8,128)(2,1)S(1)}, bf16[1,128,2048]{2,1,0:T(8,128)(2,1)}, u32[]{:S(2)}) copy-start(bf16[1,128,2048]{2,1,0:T(8,128)(2,1)} %param.14) | copy-start | bytes 1572868
  14.4 11.6 %copy-start.5 = (bf16[128,2048]{1,0:T(8,128)(2,1)S(1)}, bf16[128,2048]{1,0:T(8,128)(2,1)}, u32[]{:S(2)}) copy-start(bf16[128,2048]{1,0:T(8,128)(2,1)} %long_ref.3) | copy-start | bytes 1572868
  14.4 5.8 %collective-permute-start = (bf16[8,2048]{1,0:T(8,128)(2,1)S(1)}, bf16[8,2048]{1,0:T(8,128)(2,1)S(1)}, u32[]{:S(2)}, u32[]{:S(2)}) collective-permute-start(bf16[8,2048]{1,0:T(8,128)(2,1)S(1)} %slice_bitcast_fusion.5), channel_id=1, source_target_pairs={{0,8},{8,16},{16,24},{24,32},{32,40},{40,48},{48,56},{56,64},{64,7... | collective-permute-start | bytes 98312 | tf_op jit(solution)/shard_map/ppermute | solution.py:155
  20.7 5.3 %collective-permute-start.2 = (bf16[2,16,1024]{2,1,0:T(8,128)(2,1)S(1)}, bf16[2,16,1024]{2,1,0:T(8,128)(2,1)S(1)}, u32[]{:S(2)}, u32[]{:S(2)}) collective-permute-start(bf16[2,16,1024]{2,1,0:T(8,128)(2,1)S(1)} %get-tuple-element.23.gated_head_ref), channel_id=1, source_target_pairs={{0,8},{8,16},{16,24},{24,32},{32,40},{40,48},{48,56},{56,64},{64,7... | collective-permute-start | bytes 196616 | tf_op jit(solution)/shard_map/ppermute | solution.py:155
  30.4 25.4 %collective-permute-start.7 = (bf16[8,144,128]{2,1,0:T(8,128)(2,1)S(1)}, bf16[8,144,128]{2,1,0:T(8,128)(2,1)S(1)}, u32[]{:S(2)}, u32[]{:S(2)}) collective-permute-start(bf16[8,144,128]{2,1,0:T(8,128)(2,1)S(1)} %get-tuple-element.38), channel_id=1, source_target_pairs={{0,1},{1,0},{2,3},{3,2},{4,5},{5,4},{6,7},{7,6},{8,9},{9,8},{10,11... | collective-permute-start | bytes 884744 | tf_op jit(solution)/shard_map/ppermute | solution.py:258
  36.9 9.7 %collective-permute-start.1 = (bf16[128,1024]{1,0:T(8,128)(2,1)S(1)}, bf16[128,1024]{1,0:T(8,128)(2,1)S(1)}, u32[]{:S(2)}, u32[]{:S(2)}) collective-permute-start(bf16[128,1024]{1,0:T(8,128)(2,1)S(1)} %get-tuple-element.42), channel_id=1, source_target_pairs={{0,8},{8,16},{16,24},{24,32},{32,40},{40,48},{48,56},{56,64},{64,7... | collective-permute-start | bytes 786440 | tf_op jit(solution)/shard_map/ppermute | solution.py:155
  41.0 10.5 %collective-permute-start.3 = (bf16[128,1024]{1,0:T(8,128)(2,1)S(1)}, bf16[128,1024]{1,0:T(8,128)(2,1)S(1)}, u32[]{:S(2)}, u32[]{:S(2)}) collective-permute-start(bf16[128,1024]{1,0:T(8,128)(2,1)S(1)} %get-tuple-element.40), channel_id=1, source_target_pairs={{8,0},{16,8},{24,16},{32,24},{40,32},{48,40},{56,48},{64,56},{72,6... | collective-permute-start | bytes 786440 | tf_op jit(solution)/shard_map/ppermute | solution.py:155
  113.7 24.9 %all-to-all-start.1 = ((bf16[64,19,128]{2,1,0:T(8,128)(2,1)}), bf16[64,19,128]{2,1,0:T(8,128)(2,1)S(1)}, u32[]{:S(2)}, u32[]{:S(2)}) async-start(bf16[64,19,128]{2,1,0:T(8,128)(2,1)} %reshape.67), calls=%async_computation.1 | async-start | bytes 786432 | tf_op jit(solution)/shard_map/all_to_all | solution.py:277
  123.5 7.4 %collective-permute-start.6 = (bf16[16,2048]{1,0:T(8,128)(2,1)S(1)}, bf16[16,2048]{1,0:T(8,128)(2,1)S(1)}, u32[]{:S(2)}, u32[]{:S(2)}) collective-permute-start(bf16[16,2048]{1,0:T(8,128)(2,1)S(1)} %get-tuple-element.35), channel_id=1, source_target_pairs={{8,0},{16,8},{24,16},{32,24},{40,32},{48,40},{56,48},{64,56},{72,6... | collective-permute-start | bytes 196616 | tf_op jit(solution)/shard_map/ppermute | solution.py:155
  144.9 14.1 %all-to-all-start.2 = ((f32[4,8,128]{2,1,0:T(8,128)}), f32[4,8,128]{2,1,0:T(8,128)S(1)}, u32[]{:S(2)}, u32[]{:S(2)}) async-start(f32[4,8,128]{2,1,0:T(8,128)} %broadcast_in_dim.60), calls=%async_computation.2 | async-start | bytes 32768 | tf_op jit(solution)/shard_map/all_to_all | solution.py:282

commit v2 on v1

v2 whole, which is shorter than its diff:
```python
import functools
import math

import jax
import jax.numpy as jnp
import numpy as np
from jax import lax
from jax.experimental import pallas as pl
from jax.experimental.pallas import tpu as pltpu
from jax.sharding import PartitionSpec as P

BF = jnp.bfloat16
F32 = jnp.float32
ROWS = 128
PIECES = 64
WIDTH = 512
VMEM = 60 * 1024 * 1024


def split_table(table):
    high = table.astype(np.float32).astype(jnp.bfloat16)
    low = (table - high.astype(np.float64)).astype(np.float32).astype(jnp.bfloat16)
    return high, low


def tables():
    freq = np.arange(128)[:, None]
    place = np.arange(256)[None, :]
    angle = (freq * place % 256) * (2.0 * np.pi / 256)
    fwd = np.concatenate([np.cos(angle), -np.sin(angle)], axis=0)
    fwd[128] = 1.0 - 2.0 * (np.arange(256) % 2)
    weight = np.full((256,), 2.0 / 256)
    weight[0] = weight[128] = 1.0 / 256
    inv = (fwd * weight[:, None]).T
    fwd_hi, fwd_lo = split_table(fwd)
    inv_hi, inv_lo = split_table(inv)
    near = np.concatenate([fwd_hi[:, :128], fwd_lo[:, :128]], axis=1)
    away = np.concatenate([fwd_hi[:, 128:], fwd_lo[:, 128:]], axis=1)
    inv_both = np.concatenate([inv_hi[:ROWS], inv_lo[:ROWS]], axis=0)
    return fwd_hi, fwd_lo, near, away, inv_both


def half_of(slot, core):
    return jnp.where(core == 0, 1 - slot, slot)


def gate_kernel(query_ref, key_ref, value_ref, grad_ref, taps_ref, up_ref, down_ref, mixed_ref, wide_ref):
    short_len = taps_ref.shape[0]
    width = wide_ref.shape[1]
    down_ref[...] = (grad_ref[...].astype(F32) * query_ref[...].astype(F32)).astype(BF)
    wide_ref[0:8, :] = jnp.zeros((8, width), F32)
    wide_ref[8:, :] = value_ref[...].astype(F32)
    total = taps_ref[0:1, :] * wide_ref[8 : 8 + ROWS, :]
    for lag in range(1, short_len):
        total = total + taps_ref[lag : lag + 1, :] * wide_ref[8 - lag : 8 - lag + ROWS, :]
    mixed = total.astype(BF)
    mixed_ref[...] = mixed
    gated = key_ref[...].astype(F32) * mixed.astype(F32)
    row = lax.broadcasted_iota(jnp.int32, (8, width), 0)
    wide_ref[0:16, :] = gated[0:16]
    top = jnp.where(row < 2, wide_ref[6:14, :], wide_ref[ROWS : ROWS + 8, :])
    up_ref[0:16, :] = jnp.concatenate([top, gated[8:16]], axis=0).astype(BF)
    up_ref[16:ROWS, :] = gated[16:].astype(BF)


def own_head(wide_ref, tail, key_ref, value_ref, taps_ref):
    value = value_ref[0:16, :].astype(F32)[0:8]
    key = key_ref[0:16, :].astype(F32)[0:8]
    wide_ref[0:8, :] = tail
    wide_ref[8:16, :] = value
    total = taps_ref[0:1, :] * value
    for lag in range(1, taps_ref.shape[0]):
        total = total + taps_ref[lag : lag + 1, :] * wide_ref[8 - lag : 16 - lag, :]
    mixed = total.astype(BF).astype(F32)
    return mixed, (key * mixed).astype(BF).astype(F32)


def with_heads(own_head_rows, up_ref, got_head_rows, got_ref):
    parts = []
    for head, ref in ((own_head_rows, up_ref), (got_head_rows, got_ref)):
        parts.append(jnp.concatenate([head, ref[0:16, :].astype(F32)[8:16]], axis=0).astype(BF))
        parts.append(ref[16:ROWS, :])
    return jnp.concatenate(parts, axis=0)


def dot(left, right):
    return jnp.dot(left, right, preferred_element_type=F32)


def product(first, second, conjugate):
    first_re, first_im = first[:128], first[128:]
    second_re, second_im = second[:128], second[128:]
    edge = lax.broadcasted_iota(jnp.int32, first_re.shape, 0) == 0
    cross = first_im * second_im
    inner = jnp.where(edge, 0.0, cross)
    if conjugate:
        real = first_re * second_re + inner
        imag = first_im * second_re - first_re * second_im
    else:
        real = first_re * second_re - inner
        imag = first_re * second_im + first_im * second_re
    return jnp.concatenate([real, jnp.where(edge, cross, imag)], axis=0)


def inverse(inv_ref, spec):
    high = spec.astype(BF)
    low = (spec - high.astype(F32)).astype(BF)
    both = dot(inv_ref[...], high)
    return both[:ROWS] + both[ROWS:] + dot(inv_ref[0:ROWS, :], low)


def twice(rows):
    return jnp.concatenate([rows, rows], axis=0)


def sums_kernel(
    core_ref, up_ref, got_ref, down_ref, back_ref, mixed_ref, key_ref, value_ref, short_ref, long_ref,
    hi_ref, lo_ref, near_ref, away_ref, inv_ref, *rest,
):
    key_out, mixed_out, gated_top_out, mixed_top_out, part_ref, wide_ref = rest[-6:]
    short_len = short_ref.shape[0]
    width = wide_ref.shape[1]
    row = lax.broadcasted_iota(jnp.int32, (8, width), 0)
    got_top = got_ref[0:16, :].astype(F32)[0:8]
    mixed_top, gated_top = own_head(wide_ref, got_top, key_ref, value_ref, short_ref)
    gated_top_out[...] = gated_top.astype(BF)
    wide_ref[8:16, :] = got_top
    before = jnp.where(row < 6, 0.0, wide_ref[2:10, :])
    gated = with_heads(gated_top, up_ref, before, got_ref)
    mid = down_ref[...]
    ahead = back_ref[...]
    gated_spec = dot(hi_ref[...], gated) + dot(lo_ref[...], gated)
    mid_spec = dot(near_ref[...], twice(mid))
    both_spec = mid_spec + dot(away_ref[...], twice(ahead))
    taps_spec = dot(near_ref[...], twice(long_ref[...]))
    long_sum = inverse(inv_ref, product(mid_spec, gated_spec, True))
    gated_grad = inverse(inv_ref, product(both_spec, taps_spec, True))
    next_top = back_ref[0:16, :].astype(F32)[0:8]
    lines = [jnp.zeros((3, width), F32)]
    for gap in range(5, 0, -1):
        line = gated_top[gap : gap + 1] * next_top[0:1]
        for r in range(gap + 1, 6):
            line = line + gated_top[r : r + 1] * next_top[r - gap : r - gap + 1]
        lines.append(line)
    long_end = long_sum[ROWS - 8 :] + jnp.concatenate(lines, axis=0)
    long_sum = jnp.concatenate([long_sum[: ROWS - 8], long_end], axis=0)
    mixed = jnp.concatenate([mixed_top, mixed_ref[0:16, :].astype(F32)[8:16], mixed_ref[16:, :].astype(F32)], axis=0)
    key_out[...] = (gated_grad * mixed).astype(BF)
    mixed_grad = (gated_grad * key_ref[...].astype(F32)).astype(BF)
    mixed_out[...] = mixed_grad
    mixed_grad = mixed_grad.astype(F32)
    mixed_top_out[...] = mixed_grad[0:8].astype(BF)
    wide_ref[0:8, :] = got_top
    wide_ref[8:, :] = value_ref[...].astype(F32)
    sums = []
    for lag in range(short_len):
        sums.append(jnp.sum(mixed_grad * wide_ref[8 - lag : 8 - lag + ROWS, :], axis=0, keepdims=True))
    short_sum = jnp.concatenate(sums + [jnp.zeros((16 - short_len, width), F32)], axis=0)
    for block in range(width // 128):
        lanes = slice(block * 128, block * 128 + 128)
        part_ref[block, 0:ROWS, :] = long_sum[:, lanes].astype(part_ref.dtype)
        part_ref[block, ROWS : ROWS + 16, :] = short_sum[:, lanes].astype(part_ref.dtype)


def rest_kernel(
    up_ref, got_ref, gated_top_ref, before_ref, grad_ref, mixed_ref, rim_ref, short_ref, long_ref,
    hi_ref, lo_ref, near_ref, inv_ref, query_out, value_out, wide_ref,
):
    gated = with_heads(gated_top_ref[...].astype(F32), up_ref, before_ref[...].astype(F32), got_ref)
    gated_spec = dot(hi_ref[...], gated) + dot(lo_ref[...], gated)
    taps_spec = dot(near_ref[...], twice(long_ref[...]))
    long_out = inverse(inv_ref, product(gated_spec, taps_spec, False))
    query_out[...] = (grad_ref[...].astype(F32) * long_out).astype(BF)
    wide_ref[0:ROWS, :] = mixed_ref[...].astype(F32)
    wide_ref[ROWS:, :] = rim_ref[...].astype(F32)
    total = short_ref[0:1, :] * wide_ref[0:ROWS, :]
    for lag in range(1, short_ref.shape[0]):
        total = total + short_ref[lag : lag + 1, :] * wide_ref[lag : lag + ROWS, :]
    value_out[...] = total.astype(BF)


def piece_kernel(arrived_ref, spread_ref):
    total = arrived_ref[0].astype(F32)
    for device in range(1, arrived_ref.shape[0]):
        total = total + arrived_ref[device].astype(F32)
    square = jnp.sum(jnp.sum(total * total, axis=2, keepdims=True), axis=1, keepdims=True)
    square = jnp.broadcast_to(square, (total.shape[0], 1, total.shape[2]))
    high = square.astype(BF).astype(F32)
    message = jnp.concatenate([total, high, square - high], axis=1).astype(BF)
    for device in range(spread_ref.shape[0]):
        spread_ref[device] = message


def norm_kernel(pieces_ref, norm_ref):
    depth = pieces_ref.shape[1]
    total = pieces_ref[0].astype(F32)
    for piece in range(1, pieces_ref.shape[0]):
        total = total + pieces_ref[piece].astype(F32)
    square = total[depth - 2 : depth - 1] + total[depth - 1 : depth]
    norm_ref[...] = jnp.broadcast_to(square[None], norm_ref.shape)


def scale_kernel(limit, core_ref, mine_ref, other_ref, norms_ref, long_ref, short_ref):
    norm_sq = norms_ref[0]
    for device in range(1, norms_ref.shape[0]):
        norm_sq = norm_sq + norms_ref[device]
    factor = (limit / jnp.sqrt(norm_sq + 1e-06))[0:1]
    short_len = short_ref.shape[0]
    blocks = long_ref.shape[1] // 128
    groups = mine_ref.shape[0] // blocks
    rows = ROWS // groups

    def write(pieces_ref):
        for block in range(blocks):
            lanes = slice(block * 128, block * 128 + 128)
            lines = []
            for group in range(groups):
                piece = pieces_ref[block * groups + group].astype(F32) * factor
                long_ref[group * rows : group * rows + rows, lanes] = piece[:rows].astype(BF)
                lines.append(piece[rows : rows + 1])
            short_ref[:, lanes] = jnp.concatenate(lines, axis=0)[:short_len].astype(BF)

    @pl.when(pl.program_id(0) == 0)
    def _():
        write(mine_ref)

    @pl.when(pl.program_id(0) == 1)
    def _():
        write(other_ref)


def params():
    return pltpu.CompilerParams(vmem_limit_bytes=VMEM)


def shifted(value, by):
    devices = lax.axis_size("ctx")
    return lax.ppermute(value, "ctx", [(i, i + by) for i in range(devices) if 0 <= i + by < devices])


def on_device(gate_query, gate_key, input_value, out_grad, short_taps, long_taps):
    query_rows, key_rows, value_rows, grad_rows = gate_query[0], gate_key[0], input_value[0], out_grad[0]
    chan_width = query_rows.shape[1]
    half_width = chan_width // 2
    short_len, long_len = short_taps.shape[0], long_taps.shape[0]
    core = lax.axis_index("dp").astype(jnp.int32).reshape(1)
    devices = lax.axis_size("ctx")
    per_half = half_width // WIDTH
    struct = jax.ShapeDtypeStruct
    count = chan_width // WIDTH

    def chan(rows):
        return pl.BlockSpec((rows, WIDTH), lambda i: (0, i))

    wide = struct((ROWS, chan_width), BF)
    top = struct((8, chan_width), BF)
    up, down, mixed = pl.pallas_call(
        gate_kernel,
        out_shape=(wide, wide, wide),
        grid=(count,),
        in_specs=[chan(ROWS), chan(ROWS), chan(ROWS), chan(ROWS), chan(short_len)],
        out_specs=[chan(ROWS), chan(ROWS), chan(ROWS)],
        scratch_shapes=[pltpu.VMEM((ROWS + 8, WIDTH), F32)],
        compiler_params=params(),
        name="gates",
    )(query_rows, key_rows, value_rows, grad_rows, short_taps)
    got = shifted(up, 1)
    back = shifted(down, -1)

    fwd_hi, fwd_lo, near, away, inv_both = (jnp.asarray(t) for t in tables())

    def run_sums(slot, kept):
        def half(rows):
            return pl.BlockSpec((rows, WIDTH), lambda i, core: (0, half_of(slot, core[0]) * per_half + i))

        table = pl.BlockSpec((256, 256), lambda i, core: (0, 0))
        part = struct((half_width // 128, ROWS + 16, 128), BF if slot == 0 else F32)
        in_specs = [half(ROWS)] * 7 + [half(short_len), half(long_len)] + [table] * 5
        first = 1 + len(in_specs)
        return pl.pallas_call(
            sums_kernel,
            out_shape=(wide, wide, top, top, part),
            grid_spec=pltpu.PrefetchScalarGridSpec(
                num_scalar_prefetch=1,
                grid=(per_half,),
                in_specs=in_specs + [pl.BlockSpec(memory_space=pl.ANY)] * len(kept),
                out_specs=[
                    half(ROWS), half(ROWS), half(8), half(8),
                    pl.BlockSpec((WIDTH // 128, ROWS + 16, 128), lambda i, core: (i, 0, 0)),
                ],
                scratch_shapes=[pltpu.VMEM((ROWS + 8, WIDTH), F32)],
            ),
            input_output_aliases={first + k: k for k in range(len(kept))},
            compiler_params=params(),
            cost_estimate=pl.CostEstimate(flops=2_000_000_000, bytes_accessed=4_000_000, transcendentals=0),
            name=f"sums_{slot}",
        )(
            core, up, got, down, back, mixed, key_rows, value_rows, short_taps, long_taps,
            fwd_hi, fwd_lo, near, away, inv_both, *kept,
        )

    *kept, part_sent = run_sums(0, ())
    part_got = lax.ppermute(part_sent, "dp", [(0, 1), (1, 0)])
    key_grad, mixed_grad, gated_top, mixed_top, part_own = run_sums(1, tuple(kept))

    blocks = half_width // 128
    groups = PIECES // blocks
    total = part_own + part_got.astype(F32)
    long_part = total[:, :ROWS].reshape(blocks, groups, ROWS // groups, 128)
    short_part = total[:, ROWS : ROWS + groups].reshape(blocks, groups, 1, 128)
    pieces = jnp.concatenate([long_part, short_part], axis=2).astype(BF)
    depth = pieces.shape[2]
    owned = PIECES // devices
    arrived = lax.all_to_all(pieces.reshape(PIECES, depth, 128), "ctx", 0, 0, tiled=True)
    spread = pl.pallas_call(
        piece_kernel,
        out_shape=struct((devices, owned, depth + 2, 128), BF),
        compiler_params=params(),
        name="piece",
    )(arrived.reshape(devices, owned, depth, 128))
    spread, gated_top, mixed_top = lax.optimization_barrier((spread, gated_top, mixed_top))
    gathered = lax.all_to_all(spread.reshape(PIECES, depth + 2, 128), "ctx", 0, 0, tiled=True)
    before = shifted(gated_top, 1)
    rim = shifted(mixed_top, -1)
    table = pl.BlockSpec((256, 256), lambda i: (0, 0))
    query_grad, value_grad = pl.pallas_call(
        rest_kernel,
        out_shape=(wide, wide),
        grid=(count,),
        in_specs=[
            chan(ROWS), chan(ROWS), chan(8), chan(8), chan(ROWS), chan(ROWS), chan(8),
            chan(short_len), chan(long_len), table, table, table, table,
        ],
        out_specs=[chan(ROWS), chan(ROWS)],
        scratch_shapes=[pltpu.VMEM((ROWS + 8, WIDTH), F32)],
        compiler_params=params(),
        cost_estimate=pl.CostEstimate(flops=4_000_000_000, bytes_accessed=5_000_000, transcendentals=0),
        name="rest",
    )(
        up, got, gated_top, before, grad_rows, mixed_grad, rim, short_taps, long_taps,
        fwd_hi, fwd_lo, near, inv_both,
    )

    ways = lax.axis_size("tp")
    norms = pl.pallas_call(
        norm_kernel,
        out_shape=struct((2 * ways, 1, 128), F32),
        compiler_params=params(),
        name="norm",
    )(gathered)
    norms = lax.all_to_all(norms, ("tp", "dp"), 0, 0, tiled=True)
    other = lax.ppermute(gathered, "dp", [(0, 1), (1, 0)])
    limit = math.sqrt((long_len + short_len) * chan_width * ways)
    whole = pl.BlockSpec((PIECES, depth + 2, 128), lambda i, core: (0, 0, 0))

    def result(rows):
        return pl.BlockSpec((rows, half_width), lambda i, core: (0, jnp.where(i == 0, core[0], 1 - core[0])))

    long_grad, short_grad = pl.pallas_call(
        functools.partial(scale_kernel, limit),
        out_shape=(struct((long_len, chan_width), BF), struct((short_len, chan_width), BF)),
        grid_spec=pltpu.PrefetchScalarGridSpec(
            num_scalar_prefetch=1,
            grid=(2,),
            in_specs=[whole, whole, pl.BlockSpec((2 * ways, 1, 128), lambda i, core: (0, 0, 0))],
            out_specs=[result(long_len), result(short_len)],
        ),
        compiler_params=params(),
        name="scale",
    )(core, gathered, other, norms)
    return (query_grad[None], key_grad[None], value_grad[None], long_grad, short_grad)


def solution(mesh):
    split = P("dp", "ctx", "tp")
    taps = P(None, "tp")
    return jax.shard_map(
        on_device,
        mesh=mesh,
        in_specs=(split, split, split, split, taps, taps),
        out_specs=(split, split, split, taps, taps),
        check_vma=False,
    )
```

time: 163 us -> 140 us (0.86)
  blocking collectives: 59 us -> 41.5 us
  Pallas kernels: 12.2 us -> 26.3 us
  waiting for transfers between devices: 28.9 us -> 16.1 us
  local copies, waits for them, and re-layouts: 8.54 us -> 3.52 us
  between operations: 2.95 us -> 0.82 us
  other arithmetic: 2.91 us -> 1.17 us
    pallas_call x5 -> x7, Pallas kernels: 12.2 us -> 26.3 us  [the longest x2 9.9 us: run_sums(): pl.pallas_call(sums_kernel, out_shape=(wide, wide, top, top, part), grid_...]
    all_to_all x1, blocking collectives: 54.7 us -> 41.5 us  [on_device(): lax.all_to_all(pieces.reshape(PIECES, depth, 128), 'ctx', 0, 0, tiled=True)]
    ppermute x7 -> x4, waiting for transfers between devices: 17.6 us -> 6.39 us  [shifted(): lax.ppermute(value, 'ctx', [(i, i + by) for i in range(devices) if 0 <= i...]
    ppermute x7 -> x4, starting transfers between devices: 21.6 us -> 12 us  [shifted(): lax.ppermute(value, 'ctx', [(i, i + by) for i in range(devices) if 0 <= i...]
    all_to_all x2, starting transfers between devices: 19.4 us -> 26.5 us  [the longest x1 17.3 us: on_device(): norms = lax.all_to_all(norms, ('tp', 'dp'), 0, 0, tiled=True)]
    all_gather x1 -> x0, blocking collectives: 4.35 us -> none  [on_device(): gathered = lax.all_gather(gathered, 'dp')]
    reduce_sum x4 -> x0, other arithmetic: 1.93 us -> none  [the longest x1 0.63 us: on_device(): local_sq = jnp.sum(gathered[:, :, :, depth:, 0].astype(F32))]
    ppermute x1, starting transfers between devices: 6.55 us -> 8.46 us  [on_device(): part_got = lax.ppermute(part_sent, 'dp', [(0, 1), (1, 0)])]
  transfers between devices with their start and end apart: 10 -> 8, of which waited for: 7 -> 3; matrix products, arithmetic and copies ran while one was open for 0% -> 0% of each run, Pallas kernels for 3% -> 9%
where the time goes in v2:
time: 140 us; the launch traced here: 138 us
  starting transfers between devices  48.9 us (35%)
  blocking collectives  41.5 us (30%)
  Pallas kernels  26.3 us (19%)
  waiting for transfers between devices  16.1 us (12%)
  local copies, waits for them, and re-layouts  3.52 us (3%)
    all_to_all x1, blocking collectives, on_device(): lax.all_to_all(pieces.reshape(PIECES, depth, 128), 'ctx', 0, 0, tiled=True)  41.5 us
    all_to_all x1, starting transfers between devices, on_device(): norms = lax.all_to_all(norms, ('tp', 'dp'), 0, 0, tiled=True)  17.3 us
    ppermute x4, starting transfers between devices, shifted(): lax.ppermute(value, 'ctx', [(i, i + by) for i in range(devices) if 0 <= i...  12 us
    pallas_call x2, Pallas kernels, run_sums(): pl.pallas_call(sums_kernel, out_shape=(wide, wide, top, top, part), grid_...  9.9 us
    all_to_all x1, waiting for transfers between devices, on_device(): lax.all_to_all(spread.reshape(PIECES, depth + 2, 128), 'ctx', 0, 0, tiled...  9.75 us
    all_to_all x1, starting transfers between devices, on_device(): lax.all_to_all(spread.reshape(PIECES, depth + 2, 128), 'ctx', 0, 0, tiled...  9.12 us
    ppermute x1, starting transfers between devices, on_device(): part_got = lax.ppermute(part_sent, 'dp', [(0, 1), (1, 0)])  8.46 us
    ppermute x4, waiting for transfers between devices, shifted(): lax.ppermute(value, 'ctx', [(i, i + by) for i in range(devices) if 0 <= i...  6.39 us
  transfers between devices with their start and end apart: 8, of which 3 were waited for; matrix products, arithmetic and copies ran while one was open for 0% of the time, Pallas kernels for 9%

profile of v2, /device:TPU:1, one launch (start us, length us, event | category | flops | bytes accessed | tf_op | source)
XLA Modules:
  0.0 138.4 jit_solution(4160439827329703999)
XLA Ops:
  0.6 4.4 %gates.1 = (bf16[128,2048]{1,0:T(8,128)(2,1)}, bf16[128,2048]{1,0:T(8,128)(2,1)}, bf16[128,2048]{1,0:T(8,128)(2,1)}) custom-call(bf16[128,2048]{1,0:T(8,128)(2,1)} %bitcast.16, bf16[128,2048]{1,0:T(8,128)(2,1)} %bitcast.17, bf16[128,2048]{1,0:T(8,128)(2,1)} %bitcast.20, bf16[128,2048]{1,0:T(8,128)(2,1)} %bitcast.23, f32[7,2048]{1,0:T(8,128)} %short_ref.5), custom_call_target="tpu_custom_call" | custom-call | tf_op jit(solution)/shard_map/gates/pallas_call | solution.py:257
  5.0 1.3 collective-permute-start.1
  6.3 5.5 %collective-permute-start = (bf16[128,2048]{1,0:T(8,128)(2,1)}, bf16[128,2048]{1,0:T(8,128)(2,1)S(1)}, u32[]{:S(2)}, u32[]{:S(2)}) collective-permute-start(bf16[128,2048]{1,0:T(8,128)(2,1)} %get-tuple-element.25.up_ref), channel_id=1, source_target_pairs={{0,8},{8,16},{16,24},{24,32},{32,40},{40,48},{48,56},{56,64},{64,7... | collective-permute-start | bytes 1572872 | tf_op jit(solution)/shard_map/ppermute | solution.py:238
  11.8 4.8 %collective-permute-done.1.back_ref = bf16[128,2048]{1,0:T(8,128)(2,1)S(1)} collective-permute-done((bf16[128,2048]{1,0:T(8,128)(2,1)}, bf16[128,2048]{1,0:T(8,128)(2,1)S(1)}, u32[]{:S(2)}, u32[]{:S(2)}) %collective-permute-start.1) | collective-permute-done | bytes 524320 | tf_op jit(solution)/shard_map/ppermute | solution.py:238
  16.6 0.0 copy-start.4
  16.6 1.6 %collective-permute-done.got_ref = bf16[128,2048]{1,0:T(8,128)(2,1)S(1)} collective-permute-done((bf16[128,2048]{1,0:T(8,128)(2,1)}, bf16[128,2048]{1,0:T(8,128)(2,1)S(1)}, u32[]{:S(2)}, u32[]{:S(2)}) %collective-permute-start) | collective-permute-done | bytes 524320 | tf_op jit(solution)/shard_map/ppermute | solution.py:238
  18.2 0.0 copy-start.3
  18.2 0.0 copy-done.4
  18.2 0.8 copy-done.3
  19.0 4.9 %sums_0.1 = (bf16[128,2048]{1,0:T(8,128)(2,1)}, bf16[128,2048]{1,0:T(8,128)(2,1)}, bf16[8,2048]{1,0:T(8,128)(2,1)}, bf16[8,2048]{1,0:T(8,128)(2,1)}, bf16[8,144,128]{2,1,0:T(8,128)(2,1)}) custom-call(s32[1]{0:T(128)} %bitcast.4.core_ref, bf16[128,2048]{1,0:T(8,128)(2,1)} %get-tuple-element.25.up_ref, bf16[128,2048]{1,0:T(8,128)(2,1)} %copy-done.3, ...), custom_call_target="tpu_custom_call" | custom-call | flops 2000000000 | bytes 4000000 | tf_op jit(solution)/shard_map/sums_0/pallas_call | solution.py:280
  23.9 8.5 %collective-permute-start.2 = (bf16[8,144,128]{2,1,0:T(8,128)(2,1)}, bf16[8,144,128]{2,1,0:T(8,128)(2,1)S(1)}, u32[]{:S(2)}, u32[]{:S(2)}) collective-permute-start(bf16[8,144,128]{2,1,0:T(8,128)(2,1)} %get-tuple-element.33), channel_id=1, source_target_pairs={{0,1},{1,0},{2,3},{3,2},{4,5},{5,4},{6,7},{7,6},{8,9},{9,8},{10,11... | collective-permute-start | bytes 884744 | tf_op jit(solution)/shard_map/ppermute | solution.py:303
  32.4 5.0 %sums_1.1 = (bf16[128,2048]{1,0:T(8,128)(2,1)}, bf16[128,2048]{1,0:T(8,128)(2,1)}, bf16[8,2048]{1,0:T(8,128)(2,1)}, bf16[8,2048]{1,0:T(8,128)(2,1)}, f32[8,144,128]{2,1,0:T(8,128)}) custom-call(s32[1]{0:T(128)} %bitcast.4.core_ref, ...), custom_call_target="tpu_custom_call", output_to_operand_aliasing={{0}: (15, {}), {1}: (16, {}), {2}: (17, {}), {3}: (18, {})} | custom-call | flops 2000000000 | bytes 4000000 | tf_op jit(solution)/shard_map/sums_1/pallas_call | solution.py:280
  37.4 0.0 collective-permute-done.2
  37.4 1.1 add_convert_fusion
  38.7 41.5 %all_to_all.15 = bf16[64,17,128]{2,1,0:T(8,128)(2,1)} all-to-all(bf16[64,17,128]{2,1,0:T(8,128)(2,1)S(1)} %pad_maximum_fusion), channel_id=1, replica_groups=mesh['ctx'=64,'tp'=4,'dp'=2] {'ctx'}, dimensions={0} | all-to-all | bytes 557056 | tf_op jit(solution)/shard_map/all_to_all | solution.py:314
  80.2 1.9 %piece.1 = bf16[64,1,19,128]{3,2,1,0:T(8,128)(2,1)} custom-call(bf16[64,1,17,128]{3,2,1,0:T(8,128)(2,1)} %bitcast.14), custom_call_target="tpu_custom_call" | custom-call | tf_op jit(solution)/shard_map/piece/pallas_call | solution.py:315
  82.1 0.0 copy-start.8
  82.1 0.0 copy-start.7
  82.1 9.1 %all-to-all-start.1 = ((bf16[64,19,128]{2,1,0:T(8,128)(2,1)}), bf16[64,19,128]{2,1,0:T(8,128)(2,1)S(1)}, u32[]{:S(2)}, u32[]{:S(2)}) async-start(bf16[64,19,128]{2,1,0:T(8,128)(2,1)} %bitcast.13), calls=%async_computation.1 | async-start | bytes 786432 | tf_op jit(solution)/shard_map/all_to_all | solution.py:322
  91.3 0.0 copy-done.8
  91.3 1.3 collective-permute-start.4
  92.6 0.0 copy-done.7
  92.6 4.0 %collective-permute-start.3 = (bf16[8,2048]{1,0:T(8,128)(2,1)S(1)}, bf16[8,2048]{1,0:T(8,128)(2,1)S(1)}, u32[]{:S(2)}, u32[]{:S(2)}) collective-permute-start(bf16[8,2048]{1,0:T(8,128)(2,1)S(1)} %copy-done.7), channel_id=1, source_target_pairs={{0,8},{8,16},{16,24},{24,32},{32,40},{40,48},{48,56},{56,64},{64,7... | collective-permute-start | bytes 98312 | tf_op jit(solution)/shard_map/ppermute | solution.py:238
  96.6 9.7 %all-to-all-done.1.pieces_ref.mine_ref = bf16[64,19,128]{2,1,0:T(8,128)(2,1)S(1)} async-done(((bf16[64,19,128]{2,1,0:T(8,128)(2,1)}), bf16[64,19,128]{2,1,0:T(8,128)(2,1)S(1)}, u32[]{:S(2)}, u32[]{:S(2)}) %all-to-all-start.1) | async-done | bytes 311328 | tf_op jit(solution)/shard_map/all_to_all | solution.py:322
  106.3 0.0 copy-start
  106.3 0.7 copy-done
  107.1 1.7 %norm.1 = f32[8,1,128]{2,1,0:T(1,128)} custom-call(bf16[64,19,128]{2,1,0:T(8,128)(2,1)} %copy-done), custom_call_target="tpu_custom_call" | custom-call | tf_op jit(solution)/shard_map/norm/pallas_call | solution.py:345
  108.7 17.3 %all-to-all-start.2 = ((f32[8,1,128]{2,1,0:T(1,128)}), f32[8,1,128]{2,1,0:T(1,128)S(1)}, u32[]{:S(2)}, u32[]{:S(2)}) async-start(f32[8,1,128]{2,1,0:T(1,128)} %norm.1), calls=%async_computation.2 | async-start | bytes 8192 | tf_op jit(solution)/shard_map/all_to_all | solution.py:351
  126.1 1.9 %collective-permute-start.5 = (bf16[64,19,128]{2,1,0:T(8,128)(2,1)}, bf16[64,19,128]{2,1,0:T(8,128)(2,1)S(1)}, u32[]{:S(2)}, u32[]{:S(2)}) collective-permute-start(bf16[64,19,128]{2,1,0:T(8,128)(2,1)} %copy-done), channel_id=1, source_target_pairs={{0,1},{1,0},{2,3},{3,2},{4,5},{5,4},{6,7},{7,6},{8,9},{9,8},{10,11... | collective-permute-start | bytes 933896 | tf_op jit(solution)/shard_map/ppermute | solution.py:352
  128.0 0.0 collective-permute-done.4.rim_ref
  128.0 0.0 copy-start.5
  128.0 0.0 collective-permute-done.3.before_ref
  128.0 0.0 copy-start.6
  128.0 0.6 copy-done.5
  128.6 0.0 copy-done.6
  128.6 6.3 %rest.1 = (bf16[128,2048]{1,0:T(8,128)(2,1)}, bf16[128,2048]{1,0:T(8,128)(2,1)}) custom-call(bf16[128,2048]{1,0:T(8,128)(2,1)} %get-tuple-element.25.up_ref, bf16[128,2048]{1,0:T(8,128)(2,1)} %copy-done.3, bf16[8,2048]{1,0:T(8,128)(2,1)} %get-tuple-element.36.gated_top_ref, bf16[8,2048]{1,0:T(8,128)(2,1)} %copy-done.6, bf16[128,2048]{1,0:T(8,128)(2,1)} %bitcast.24, ...), custom_call_target="tpu_custom_call" | custom-call | flops 4000000000 | bytes 5000000 | tf_op jit(solution)/shard_map/rest/pallas_call | solution.py:326
  135.0 0.0 all-to-all-done.2.norms_ref
  135.0 0.0 copy-start.2
  135.0 0.0 collective-permute-done.5.other_ref
  135.0 0.6 copy-done.2
  135.6 0.0 copy-start.1
  135.6 0.7 copy-done.1
  136.3 2.1 %scale.1 = (bf16[128,2048]{1,0:T(8,128)(2,1)}, bf16[7,2048]{1,0:T(8,128)(2,1)}) custom-call(s32[1]{0:T(128)} %bitcast.4.core_ref, bf16[64,19,128]{2,1,0:T(8,128)(2,1)} %copy-done, bf16[64,19,128]{2,1,0:T(8,128)(2,1)} %copy-done.1, f32[8,1,128]{2,1,0:T(1,128)} %copy-done.2), custom_call_target="tpu_custom_call" | custom-call | tf_op jit(solution)/shard_map/scale/pallas_call | solution.py:359
  (4 shorter events, 0.1 us)
Async XLA Ops:
  5.0 11.6 %collective-permute-start.1 = (bf16[128,2048]{1,0:T(8,128)(2,1)}, bf16[128,2048]{1,0:T(8,128)(2,1)S(1)}, u32[]{:S(2)}, u32[]{:S(2)}) collective-permute-start(bf16[128,2048]{1,0:T(8,128)(2,1)} %get-tuple-element.26.down_ref), channel_id=1, source_target_pairs={{8,0},{16,8},{24,16},{32,24},{40,32},{48,40},{56,48},{64,56},{72,6... | collective-permute-start | bytes 1572872 | tf_op jit(solution)/shard_map/ppermute | solution.py:238
  6.3 11.9 %collective-permute-start = (bf16[128,2048]{1,0:T(8,128)(2,1)}, bf16[128,2048]{1,0:T(8,128)(2,1)S(1)}, u32[]{:S(2)}, u32[]{:S(2)}) collective-permute-start(bf16[128,2048]{1,0:T(8,128)(2,1)} %get-tuple-element.25.up_ref), channel_id=1, source_target_pairs={{0,8},{8,16},{16,24},{24,32},{32,40},{40,48},{48,56},{56,64},{64,7... | collective-permute-start | bytes 1572872 | tf_op jit(solution)/shard_map/ppermute | solution.py:238
  16.6 1.6 %copy-start.4 = (bf16[128,2048]{1,0:T(8,128)(2,1)}, bf16[128,2048]{1,0:T(8,128)(2,1)S(1)}, u32[]{:S(2)}) copy-start(bf16[128,2048]{1,0:T(8,128)(2,1)S(1)} %collective-permute-done.1.back_ref) | copy-start | bytes 1572868
  18.2 0.8 copy-start.3
  23.9 13.5 %collective-permute-start.2 = (bf16[8,144,128]{2,1,0:T(8,128)(2,1)}, bf16[8,144,128]{2,1,0:T(8,128)(2,1)S(1)}, u32[]{:S(2)}, u32[]{:S(2)}) collective-permute-start(bf16[8,144,128]{2,1,0:T(8,128)(2,1)} %get-tuple-element.33), channel_id=1, source_target_pairs={{0,1},{1,0},{2,3},{3,2},{4,5},{5,4},{6,7},{7,6},{8,9},{9,8},{10,11... | collective-permute-start | bytes 884744 | tf_op jit(solution)/shard_map/ppermute | solution.py:303
  82.1 9.1 %copy-start.8 = (bf16[8,2048]{1,0:T(8,128)(2,1)S(1)}, bf16[8,2048]{1,0:T(8,128)(2,1)}, u32[]{:S(2)}) copy-start(bf16[8,2048]{1,0:T(8,128)(2,1)} %get-tuple-element.38) | copy-start | bytes 98308
  82.1 10.4 %copy-start.7 = (bf16[8,2048]{1,0:T(8,128)(2,1)S(1)}, bf16[8,2048]{1,0:T(8,128)(2,1)}, u32[]{:S(2)}) copy-start(bf16[8,2048]{1,0:T(8,128)(2,1)} %get-tuple-element.36.gated_top_ref) | copy-start | bytes 98308
  82.1 24.2 %all-to-all-start.1 = ((bf16[64,19,128]{2,1,0:T(8,128)(2,1)}), bf16[64,19,128]{2,1,0:T(8,128)(2,1)S(1)}, u32[]{:S(2)}, u32[]{:S(2)}) async-start(bf16[64,19,128]{2,1,0:T(8,128)(2,1)} %bitcast.13), calls=%async_computation.1 | async-start | bytes 786432 | tf_op jit(solution)/shard_map/all_to_all | solution.py:322
  91.3 36.7 %collective-permute-start.4 = (bf16[8,2048]{1,0:T(8,128)(2,1)S(1)}, bf16[8,2048]{1,0:T(8,128)(2,1)S(1)}, u32[]{:S(2)}, u32[]{:S(2)}) collective-permute-start(bf16[8,2048]{1,0:T(8,128)(2,1)S(1)} %copy-done.8), channel_id=1, source_target_pairs={{8,0},{16,8},{24,16},{32,24},{40,32},{48,40},{56,48},{64,56},{72,6... | collective-permute-start | bytes 98312 | tf_op jit(solution)/shard_map/ppermute | solution.py:238
  92.6 35.4 %collective-permute-start.3 = (bf16[8,2048]{1,0:T(8,128)(2,1)S(1)}, bf16[8,2048]{1,0:T(8,128)(2,1)S(1)}, u32[]{:S(2)}, u32[]{:S(2)}) collective-permute-start(bf16[8,2048]{1,0:T(8,128)(2,1)S(1)} %copy-done.7), channel_id=1, source_target_pairs={{0,8},{8,16},{16,24},{24,32},{32,40},{40,48},{48,56},{56,64},{64,7... | collective-permute-start | bytes 98312 | tf_op jit(solution)/shard_map/ppermute | solution.py:238
  106.3 0.7 copy-start
  108.7 26.2 %all-to-all-start.2 = ((f32[8,1,128]{2,1,0:T(1,128)}), f32[8,1,128]{2,1,0:T(1,128)S(1)}, u32[]{:S(2)}, u32[]{:S(2)}) async-start(f32[8,1,128]{2,1,0:T(1,128)} %norm.1), calls=%async_computation.2 | async-start | bytes 8192 | tf_op jit(solution)/shard_map/all_to_all | solution.py:351
  126.1 8.9 %collective-permute-start.5 = (bf16[64,19,128]{2,1,0:T(8,128)(2,1)}, bf16[64,19,128]{2,1,0:T(8,128)(2,1)S(1)}, u32[]{:S(2)}, u32[]{:S(2)}) collective-permute-start(bf16[64,19,128]{2,1,0:T(8,128)(2,1)} %copy-done), channel_id=1, source_target_pairs={{0,1},{1,0},{2,3},{3,2},{4,5},{5,4},{6,7},{7,6},{8,9},{9,8},{10,11... | collective-permute-start | bytes 933896 | tf_op jit(solution)/shard_map/ppermute | solution.py:352
  128.0 0.6 copy-start.5
  128.0 0.6 copy-start.6
  135.0 0.6 copy-start.2
  135.6 0.7 copy-start.1

commit v3 on v2

--- a/solution.py
+++ b/solution.py
@@ -12,9 +12,9 @@
 BF = jnp.bfloat16
 F32 = jnp.float32
 ROWS = 128
-PIECES = 64
 WIDTH = 512
 VMEM = 60 * 1024 * 1024
+SMALL = 16 * 1024 * 1024
 
 
 def split_table(table):
@@ -179,24 +179,33 @@
     value_out[...] = total.astype(BF)
 
 
+def line_kernel(arrived_ref, spread_ref):
+    total = arrived_ref[0].astype(F32)
+    for device in range(1, arrived_ref.shape[0]):
+        total = total + arrived_ref[device].astype(F32)
+    message = total.astype(BF)
+    for device in range(spread_ref.shape[0]):
+        spread_ref[device] = message
+
+
 def piece_kernel(arrived_ref, spread_ref):
     total = arrived_ref[0].astype(F32)
     for device in range(1, arrived_ref.shape[0]):
         total = total + arrived_ref[device].astype(F32)
-    square = jnp.sum(jnp.sum(total * total, axis=2, keepdims=True), axis=1, keepdims=True)
-    square = jnp.broadcast_to(square, (total.shape[0], 1, total.shape[2]))
+    square = jnp.sum(jnp.sum(total * total, axis=1, keepdims=True), axis=0, keepdims=True)
     high = square.astype(BF).astype(F32)
-    message = jnp.concatenate([total, high, square - high], axis=1).astype(BF)
+    row = lax.broadcasted_iota(jnp.int32, (8, 128), 0)
+    norm_rows = jnp.where(row == 0, high, jnp.where(row == 1, square - high, 0.0))
+    message = jnp.concatenate([total[: ROWS + 8], norm_rows], axis=0).astype(BF)
     for device in range(spread_ref.shape[0]):
         spread_ref[device] = message
 
 
 def norm_kernel(pieces_ref, norm_ref):
-    depth = pieces_ref.shape[1]
-    total = pieces_ref[0].astype(F32)
+    total = pieces_ref[0, ROWS:, :].astype(F32)
     for piece in range(1, pieces_ref.shape[0]):
-        total = total + pieces_ref[piece].astype(F32)
-    square = total[depth - 2 : depth - 1] + total[depth - 1 : depth]
+        total = total + pieces_ref[piece, ROWS:, :].astype(F32)
+    square = total[8:9] + total[9:10]
     norm_ref[...] = jnp.broadcast_to(square[None], norm_ref.shape)
 
 
@@ -204,21 +213,15 @@
     norm_sq = norms_ref[0]
     for device in range(1, norms_ref.shape[0]):
         norm_sq = norm_sq + norms_ref[device]
-    factor = (limit / jnp.sqrt(norm_sq + 1e-06))[0:1]
+    factor = limit / jnp.sqrt(norm_sq + 1e-06)
     short_len = short_ref.shape[0]
-    blocks = long_ref.shape[1] // 128
-    groups = mine_ref.shape[0] // blocks
-    rows = ROWS // groups
 
     def write(pieces_ref):
-        for block in range(blocks):
+        for block in range(pieces_ref.shape[0]):
             lanes = slice(block * 128, block * 128 + 128)
-            lines = []
-            for group in range(groups):
-                piece = pieces_ref[block * groups + group].astype(F32) * factor
-                long_ref[group * rows : group * rows + rows, lanes] = piece[:rows].astype(BF)
-                lines.append(piece[rows : rows + 1])
-            short_ref[:, lanes] = jnp.concatenate(lines, axis=0)[:short_len].astype(BF)
+            piece = pieces_ref[block].astype(F32) * factor
+            long_ref[:, lanes] = piece[:ROWS].astype(BF)
+            short_ref[:, lanes] = piece[ROWS : ROWS + short_len].astype(BF)
 
     @pl.when(pl.program_id(0) == 0)
     def _():
@@ -229,8 +232,8 @@
         write(other_ref)
 
 
-def params():
-    return pltpu.CompilerParams(vmem_limit_bytes=VMEM)
+def params(limit=VMEM):
+    return pltpu.CompilerParams(vmem_limit_bytes=limit)
 
 
 def shifted(value, by):
@@ -304,24 +307,24 @@
     key_grad, mixed_grad, gated_top, mixed_top, part_own = run_sums(1, tuple(kept))
 
     blocks = half_width // 128
-    groups = PIECES // blocks
-    total = part_own + part_got.astype(F32)
-    long_part = total[:, :ROWS].reshape(blocks, groups, ROWS // groups, 128)
-    short_part = total[:, ROWS : ROWS + groups].reshape(blocks, groups, 1, 128)
-    pieces = jnp.concatenate([long_part, short_part], axis=2).astype(BF)
-    depth = pieces.shape[2]
-    owned = PIECES // devices
-    arrived = lax.all_to_all(pieces.reshape(PIECES, depth, 128), "ctx", 0, 0, tiled=True)
-    spread = pl.pallas_call(
-        piece_kernel,
-        out_shape=struct((devices, owned, depth + 2, 128), BF),
-        compiler_params=params(),
-        name="piece",
-    )(arrived.reshape(devices, owned, depth, 128))
-    spread, gated_top, mixed_top = lax.optimization_barrier((spread, gated_top, mixed_top))
-    gathered = lax.all_to_all(spread.reshape(PIECES, depth + 2, 128), "ctx", 0, 0, tiled=True)
+    lines = devices // blocks
+    along = [[line * blocks + i for i in range(blocks)] for line in range(lines)]
+    across = [[line * blocks + i for line in range(lines)] for i in range(blocks)]
+    depth = ROWS + 16
+
+    def swap(value, groups):
+        return lax.all_to_all(value, "ctx", 0, 0, tiled=True, axis_index_groups=groups)
+
+    def small_call(kernel, name, count):
+        return pl.pallas_call(kernel, out_shape=struct((count, depth, 128), BF), compiler_params=params(SMALL), name=name)
+
+    total = (part_own + part_got.astype(F32)).astype(BF)
     before = shifted(gated_top, 1)
     rim = shifted(mixed_top, -1)
+    scattered = small_call(line_kernel, "line", lines)(swap(total, along))
+    scattered, before, rim = lax.optimization_barrier((scattered, before, rim))
+    spread = small_call(piece_kernel, "piece", blocks)(swap(scattered, across))
+    gathered = swap(spread, along)
     table = pl.BlockSpec((256, 256), lambda i: (0, 0))
     query_grad, value_grad = pl.pallas_call(
         rest_kernel,
@@ -341,17 +344,18 @@
         fwd_hi, fwd_lo, near, inv_both,
     )
 
+    gathered, query_grad, value_grad = lax.optimization_barrier((gathered, query_grad, value_grad))
     ways = lax.axis_size("tp")
     norms = pl.pallas_call(
         norm_kernel,
         out_shape=struct((2 * ways, 1, 128), F32),
-        compiler_params=params(),
+        compiler_params=params(SMALL),
         name="norm",
     )(gathered)
     norms = lax.all_to_all(norms, ("tp", "dp"), 0, 0, tiled=True)
     other = lax.ppermute(gathered, "dp", [(0, 1), (1, 0)])
     limit = math.sqrt((long_len + short_len) * chan_width * ways)
-    whole = pl.BlockSpec((PIECES, depth + 2, 128), lambda i, core: (0, 0, 0))
+    whole = pl.BlockSpec((blocks, depth, 128), lambda i, core: (0, 0, 0))
 
     def result(rows):
         return pl.BlockSpec((rows, half_width), lambda i, core: (0, jnp.where(i == 0, core[0], 1 - core[0])))
@@ -365,7 +369,7 @@
             in_specs=[whole, whole, pl.BlockSpec((2 * ways, 1, 128), lambda i, core: (0, 0, 0))],
             out_specs=[result(long_len), result(short_len)],
         ),
-        compiler_params=params(),
+        compiler_params=params(SMALL),
         name="scale",
     )(core, gathered, other, norms)
     return (query_grad[None], key_grad[None], value_grad[None], long_grad, short_grad)

time: 140 us -> 134 us (0.957)
  starting transfers between devices: 48.9 us -> 41.2 us
  blocking collectives: 41.5 us -> 49.1 us
  Pallas kernels: 26.3 us -> 22.5 us
  local copies, waits for them, and re-layouts: 3.52 us -> 0.83 us
    all_to_all x2, starting transfers between devices: 26.5 us -> 14.5 us  [swap(): lax.all_to_all(value, 'ctx', 0, 0, tiled=True, axis_index_groups=groups)]
    all_to_all x1 -> x2, blocking collectives: 41.5 us -> 49.1 us  [the longest x1 29.3 us: swap(): lax.all_to_all(value, 'ctx', 0, 0, tiled=True, axis_index_groups=groups)]
    ppermute x1, starting transfers between devices: 1.91 us -> 6.14 us  [on_device(): other = lax.ppermute(gathered, 'dp', [(0, 1), (1, 0)])]
    unnamed x18 -> x12, local copies, waits for them, and re-layouts: 3.47 us -> 0.83 us
    convert_element_type x0 -> x1, other arithmetic: none -> 1.84 us  [on_device(): total = (part_own + part_got.astype(F32)).astype(BF)]
    pallas_call x1, Pallas kernels: 1.66 us -> 0.01 us  [on_device(): pl.pallas_call(norm_kernel, out_shape=struct((2 * ways, 1, 128), F32), co...]
  transfers between devices with their start and end apart: 8 -> 8, of which waited for: 3 -> 4; matrix products, arithmetic and copies ran while one was open for 0% -> 0% of each run, Pallas kernels for 9% -> 9%
where the time goes in v3:
time: 134 us
  blocking collectives  49.1 us (37%)
  starting transfers between devices  41.2 us (31%)
  Pallas kernels  22.5 us (17%)
  waiting for transfers between devices  17.4 us (13%)
  other arithmetic  1.84 us (1%)
    all_to_all x1, blocking collectives, swap(): lax.all_to_all(value, 'ctx', 0, 0, tiled=True, axis_index_groups=groups)  29.3 us
    all_to_all x1, blocking collectives, on_device(): norms = lax.all_to_all(norms, ('tp', 'dp'), 0, 0, tiled=True)  19.8 us
    all_to_all x2, starting transfers between devices, swap(): lax.all_to_all(value, 'ctx', 0, 0, tiled=True, axis_index_groups=groups)  14.5 us
    ppermute x4, starting transfers between devices, shifted(): lax.ppermute(value, 'ctx', [(i, i + by) for i in range(devices) if 0 <= i...  12 us
    all_to_all x2, waiting for transfers between devices, swap(): lax.all_to_all(value, 'ctx', 0, 0, tiled=True, axis_index_groups=groups)  11 us
    pallas_call x2, Pallas kernels, run_sums(): pl.pallas_call(sums_kernel, out_shape=(wide, wide, top, top, part), grid_...  9.91 us
    ppermute x1, starting transfers between devices, on_device(): part_got = lax.ppermute(part_sent, 'dp', [(0, 1), (1, 0)])  8.45 us
    ppermute x4, waiting for transfers between devices, shifted(): lax.ppermute(value, 'ctx', [(i, i + by) for i in range(devices) if 0 <= i...  6.39 us
  transfers between devices with their start and end apart: 8, of which 4 were waited for; matrix products, arithmetic and copies ran while one was open for 0% of the time, Pallas kernels for 9%

profile of v3, /device:TPU:1, one launch (start us, length us, event | category | flops | bytes accessed | tf_op | source)
XLA Modules:
  0.0 133.6 jit_solution(18204163077150304708)
XLA Ops:
  0.6 4.4 %gates.1 = (bf16[128,2048]{1,0:T(8,128)(2,1)}, bf16[128,2048]{1,0:T(8,128)(2,1)}, bf16[128,2048]{1,0:T(8,128)(2,1)}) custom-call(bf16[128,2048]{1,0:T(8,128)(2,1)} %bitcast.8, bf16[128,2048]{1,0:T(8,128)(2,1)} %bitcast.9, bf16[128,2048]{1,0:T(8,128)(2,1)} %bitcast.12, bf16[128,2048]{1,0:T(8,128)(2,1)} %bitcast.15, f32[7,2048]{1,0:T(8,128)} %short_ref.5), custom_call_target="tpu_custom_call" | custom-call | tf_op jit(solution)/shard_map/gates/pallas_call | solution.py:260
  5.0 1.3 collective-permute-start.1
  6.3 5.5 %collective-permute-start = (bf16[128,2048]{1,0:T(8,128)(2,1)}, bf16[128,2048]{1,0:T(8,128)(2,1)S(1)}, u32[]{:S(2)}, u32[]{:S(2)}) collective-permute-start(bf16[128,2048]{1,0:T(8,128)(2,1)} %get-tuple-element.28.up_ref), channel_id=1, source_target_pairs={{0,8},{8,16},{16,24},{24,32},{32,40},{40,48},{48,56},{56,64},{64,7... | collective-permute-start | bytes 1572872 | tf_op jit(solution)/shard_map/ppermute | solution.py:241
  11.8 4.8 %collective-permute-done.1.back_ref = bf16[128,2048]{1,0:T(8,128)(2,1)S(1)} collective-permute-done((bf16[128,2048]{1,0:T(8,128)(2,1)}, bf16[128,2048]{1,0:T(8,128)(2,1)S(1)}, u32[]{:S(2)}, u32[]{:S(2)}) %collective-permute-start.1) | collective-permute-done | bytes 524320 | tf_op jit(solution)/shard_map/ppermute | solution.py:241
  16.6 0.0 copy-start.1
  16.6 1.6 %collective-permute-done.got_ref = bf16[128,2048]{1,0:T(8,128)(2,1)S(1)} collective-permute-done((bf16[128,2048]{1,0:T(8,128)(2,1)}, bf16[128,2048]{1,0:T(8,128)(2,1)S(1)}, u32[]{:S(2)}, u32[]{:S(2)}) %collective-permute-start) | collective-permute-done | bytes 524320 | tf_op jit(solution)/shard_map/ppermute | solution.py:241
  18.2 0.0 copy-start
  18.2 0.0 copy-done.1
  18.2 0.8 copy-done
  19.0 4.9 %sums_0.1 = (bf16[128,2048]{1,0:T(8,128)(2,1)}, bf16[128,2048]{1,0:T(8,128)(2,1)}, bf16[8,2048]{1,0:T(8,128)(2,1)}, bf16[8,2048]{1,0:T(8,128)(2,1)}, bf16[8,144,128]{2,1,0:T(8,128)(2,1)}) custom-call(s32[1]{0:T(128)} %bitcast.core_ref, bf16[128,2048]{1,0:T(8,128)(2,1)} %get-tuple-element.28.up_ref, bf16[128,2048]{1,0:T(8,128)(2,1)} %copy-done, ...), custom_call_target="tpu_custom_call" | custom-call | flops 2000000000 | bytes 4000000 | tf_op jit(solution)/shard_map/sums_0/pallas_call | solution.py:283
  23.9 8.5 %collective-permute-start.2 = (bf16[8,144,128]{2,1,0:T(8,128)(2,1)}, bf16[8,144,128]{2,1,0:T(8,128)(2,1)S(1)}, u32[]{:S(2)}, u32[]{:S(2)}) collective-permute-start(bf16[8,144,128]{2,1,0:T(8,128)(2,1)} %get-tuple-element.36), channel_id=1, source_target_pairs={{0,1},{1,0},{2,3},{3,2},{4,5},{5,4},{6,7},{7,6},{8,9},{9,8},{10,11... | collective-permute-start | bytes 884744 | tf_op jit(solution)/shard_map/ppermute | solution.py:306
  32.4 5.0 %sums_1.1 = (bf16[128,2048]{1,0:T(8,128)(2,1)}, bf16[128,2048]{1,0:T(8,128)(2,1)}, bf16[8,2048]{1,0:T(8,128)(2,1)}, bf16[8,2048]{1,0:T(8,128)(2,1)}, f32[8,144,128]{2,1,0:T(8,128)}) custom-call(s32[1]{0:T(128)} %bitcast.core_ref, ...), custom_call_target="tpu_custom_call", output_to_operand_aliasing={{0}: (15, {}), {1}: (16, {}), {2}: (17, {}), {3}: (18, {})} | custom-call | flops 2000000000 | bytes 4000000 | tf_op jit(solution)/shard_map/sums_1/pallas_call | solution.py:283
  37.4 0.0 collective-permute-done.2
  37.4 1.8 %add_convert_fusion = bf16[8,144,128]{2,1,0:T(8,128)(2,1)} fusion(f32[8,144,128]{2,1,0:T(8,128)} %get-tuple-element.35, bf16[8,144,128]{2,1,0:T(8,128)(2,1)S(1)} %collective-permute-done.2), kind=kLoop, calls=%fused_computation | loop fusion | flops 442368 | bytes 1179648 | tf_op jit(solution)/shard_map/convert_element_type | solution.py:321
  39.3 0.0 copy-start.5
  39.3 0.0 copy-start.4
  39.3 11.1 %all-to-all-start = ((bf16[8,144,128]{2,1,0:T(8,128)(2,1)}), bf16[8,144,128]{2,1,0:T(8,128)(2,1)S(1)}, u32[]{:S(2)}, u32[]{:S(2)}) async-start(bf16[8,144,128]{2,1,0:T(8,128)(2,1)} %add_convert_fusion), calls=%async_computation | async-start | bytes 589824 | tf_op jit(solution)/shard_map/all_to_all | solution.py:316
  50.4 0.0 copy-done.5
  50.4 1.3 collective-permute-start.4
  51.7 0.0 copy-done.4
  51.7 4.0 %collective-permute-start.3 = (bf16[8,2048]{1,0:T(8,128)(2,1)S(1)}, bf16[8,2048]{1,0:T(8,128)(2,1)S(1)}, u32[]{:S(2)}, u32[]{:S(2)}) collective-permute-start(bf16[8,2048]{1,0:T(8,128)(2,1)S(1)} %copy-done.4), channel_id=1, source_target_pairs={{0,8},{8,16},{16,24},{24,32},{32,40},{40,48},{48,56},{56,64},{64,7... | collective-permute-start | bytes 98312 | tf_op jit(solution)/shard_map/ppermute | solution.py:241
  55.7 7.7 %all-to-all-done.arrived_ref = bf16[8,144,128]{2,1,0:T(8,128)(2,1)S(1)} async-done(((bf16[8,144,128]{2,1,0:T(8,128)(2,1)}), bf16[8,144,128]{2,1,0:T(8,128)(2,1)S(1)}, u32[]{:S(2)}, u32[]{:S(2)}) %all-to-all-start) | async-done | bytes 294944 | tf_op jit(solution)/shard_map/all_to_all | solution.py:316
  63.4 0.0 collective-permute-done.4.rim_ref
  63.4 0.0 copy-start.2
  63.5 0.0 collective-permute-done.3.before_ref
  63.5 0.0 copy-start.3
  63.5 29.3 %all_to_all.20.arrived_ref = bf16[8,144,128]{2,1,0:T(8,128)(2,1)S(1)} all-to-all(bf16[8,144,128]{2,1,0:T(8,128)(2,1)S(1)} %line.1), channel_id=1, replica_groups={{0,64,128,192,256,320,384,448},{8,72,136,200,264,328,392,456},{16,80,14..., dimensions={0} | all-to-all | bytes 589824 | tf_op jit(solution)/shard_map/all_to_all | solution.py:316
  92.8 0.0 copy-done.2
  92.8 0.0 copy-done.3
  92.8 0.9 piece.1
  93.6 3.4 %all-to-all-start.2 = ((bf16[8,144,128]{2,1,0:T(8,128)(2,1)}), bf16[8,144,128]{2,1,0:T(8,128)(2,1)S(1)}, u32[]{:S(2)}, u32[]{:S(2)}) async-start(bf16[8,144,128]{2,1,0:T(8,128)(2,1)} %piece.1), calls=%async_computation.2 | async-start | bytes 589824 | tf_op jit(solution)/shard_map/all_to_all | solution.py:316
  97.1 6.3 %rest.1 = (bf16[128,2048]{1,0:T(8,128)(2,1)}, bf16[128,2048]{1,0:T(8,128)(2,1)}) custom-call(bf16[128,2048]{1,0:T(8,128)(2,1)} %get-tuple-element.28.up_ref, bf16[128,2048]{1,0:T(8,128)(2,1)} %copy-done, bf16[8,2048]{1,0:T(8,128)(2,1)} %get-tuple-element.37.gated_top_ref, bf16[8,2048]{1,0:T(8,128)(2,1)} %copy-done.3, bf16[128,2048]{1,0:T(8,128)(2,1)} %bitcast.16, ...), custom_call_target="tpu_custom_call" | custom-call | flops 4000000000 | bytes 5000000 | tf_op jit(solution)/shard_map/rest/pallas_call | solution.py:329
  103.4 3.3 %all-to-all-done.2.pieces_ref.mine_ref = bf16[8,144,128]{2,1,0:T(8,128)(2,1)S(1)} async-done(((bf16[8,144,128]{2,1,0:T(8,128)(2,1)}), bf16[8,144,128]{2,1,0:T(8,128)(2,1)S(1)}, u32[]{:S(2)}, u32[]{:S(2)}) %all-to-all-start.2) | async-done | bytes 294944 | tf_op jit(solution)/shard_map/all_to_all | solution.py:316
  106.7 6.1 %collective-permute-start.5 = (bf16[8,144,128]{2,1,0:T(8,128)(2,1)S(1)}, bf16[8,144,128]{2,1,0:T(8,128)(2,1)S(1)}, u32[]{:S(2)}, u32[]{:S(2)}) collective-permute-start(bf16[8,144,128]{2,1,0:T(8,128)(2,1)S(1)} %all-to-all-done.2.pieces_ref.mine_ref), channel_id=1, source_target_pairs={{0,1},{1,0},{2,3},{3,2},{4,5},{5,4},{6,7},{7,6},{8,9},{9,8},{10,11... | collective-permute-start | bytes 884744 | tf_op jit(solution)/shard_map/ppermute | solution.py:356
  112.9 19.8 %all_to_all.21.norms_ref = f32[8,1,128]{2,1,0:T(1,128)S(1)} all-to-all(f32[8,1,128]{2,1,0:T(1,128)S(1)} %norm.1), channel_id=1, replica_groups=mesh['ctx'=64,'tp'=4,'dp'=2] {'tp','dp'}, dimensions={0} | all-to-all | bytes 8192 | tf_op jit(solution)/shard_map/all_to_all | solution.py:355
  132.7 0.0 collective-permute-done.5.other_ref
  132.7 0.9 scale.1
  (2 shorter events, 0.1 us)
Async XLA Ops:
  5.0 11.6 %collective-permute-start.1 = (bf16[128,2048]{1,0:T(8,128)(2,1)}, bf16[128,2048]{1,0:T(8,128)(2,1)S(1)}, u32[]{:S(2)}, u32[]{:S(2)}) collective-permute-start(bf16[128,2048]{1,0:T(8,128)(2,1)} %get-tuple-element.29.down_ref), channel_id=1, source_target_pairs={{8,0},{16,8},{24,16},{32,24},{40,32},{48,40},{56,48},{64,56},{72,6... | collective-permute-start | bytes 1572872 | tf_op jit(solution)/shard_map/ppermute | solution.py:241
  6.3 11.9 %collective-permute-start = (bf16[128,2048]{1,0:T(8,128)(2,1)}, bf16[128,2048]{1,0:T(8,128)(2,1)S(1)}, u32[]{:S(2)}, u32[]{:S(2)}) collective-permute-start(bf16[128,2048]{1,0:T(8,128)(2,1)} %get-tuple-element.28.up_ref), channel_id=1, source_target_pairs={{0,8},{8,16},{16,24},{24,32},{32,40},{40,48},{48,56},{56,64},{64,7... | collective-permute-start | bytes 1572872 | tf_op jit(solution)/shard_map/ppermute | solution.py:241
  16.6 1.6 %copy-start.1 = (bf16[128,2048]{1,0:T(8,128)(2,1)}, bf16[128,2048]{1,0:T(8,128)(2,1)S(1)}, u32[]{:S(2)}) copy-start(bf16[128,2048]{1,0:T(8,128)(2,1)S(1)} %collective-permute-done.1.back_ref) | copy-start | bytes 1572868
  18.2 0.8 copy-start
  23.9 13.5 %collective-permute-start.2 = (bf16[8,144,128]{2,1,0:T(8,128)(2,1)}, bf16[8,144,128]{2,1,0:T(8,128)(2,1)S(1)}, u32[]{:S(2)}, u32[]{:S(2)}) collective-permute-start(bf16[8,144,128]{2,1,0:T(8,128)(2,1)} %get-tuple-element.36), channel_id=1, source_target_pairs={{0,1},{1,0},{2,3},{3,2},{4,5},{5,4},{6,7},{7,6},{8,9},{9,8},{10,11... | collective-permute-start | bytes 884744 | tf_op jit(solution)/shard_map/ppermute | solution.py:306
  39.3 11.1 %copy-start.5 = (bf16[8,2048]{1,0:T(8,128)(2,1)S(1)}, bf16[8,2048]{1,0:T(8,128)(2,1)}, u32[]{:S(2)}) copy-start(bf16[8,2048]{1,0:T(8,128)(2,1)} %get-tuple-element.38) | copy-start | bytes 98308
  39.3 12.4 %copy-start.4 = (bf16[8,2048]{1,0:T(8,128)(2,1)S(1)}, bf16[8,2048]{1,0:T(8,128)(2,1)}, u32[]{:S(2)}) copy-start(bf16[8,2048]{1,0:T(8,128)(2,1)} %get-tuple-element.37.gated_top_ref) | copy-start | bytes 98308
  39.3 24.1 %all-to-all-start = ((bf16[8,144,128]{2,1,0:T(8,128)(2,1)}), bf16[8,144,128]{2,1,0:T(8,128)(2,1)S(1)}, u32[]{:S(2)}, u32[]{:S(2)}) async-start(bf16[8,144,128]{2,1,0:T(8,128)(2,1)} %add_convert_fusion), calls=%async_computation | async-start | bytes 589824 | tf_op jit(solution)/shard_map/all_to_all | solution.py:316
  50.4 13.1 %collective-permute-start.4 = (bf16[8,2048]{1,0:T(8,128)(2,1)S(1)}, bf16[8,2048]{1,0:T(8,128)(2,1)S(1)}, u32[]{:S(2)}, u32[]{:S(2)}) collective-permute-start(bf16[8,2048]{1,0:T(8,128)(2,1)S(1)} %copy-done.5), channel_id=1, source_target_pairs={{8,0},{16,8},{24,16},{32,24},{40,32},{48,40},{56,48},{64,56},{72,6... | collective-permute-start | bytes 98312 | tf_op jit(solution)/shard_map/ppermute | solution.py:241
  51.7 11.8 %collective-permute-start.3 = (bf16[8,2048]{1,0:T(8,128)(2,1)S(1)}, bf16[8,2048]{1,0:T(8,128)(2,1)S(1)}, u32[]{:S(2)}, u32[]{:S(2)}) collective-permute-start(bf16[8,2048]{1,0:T(8,128)(2,1)S(1)} %copy-done.4), channel_id=1, source_target_pairs={{0,8},{8,16},{16,24},{24,32},{32,40},{40,48},{48,56},{56,64},{64,7... | collective-permute-start | bytes 98312 | tf_op jit(solution)/shard_map/ppermute | solution.py:241
  63.4 29.3 %copy-start.2 = (bf16[8,2048]{1,0:T(8,128)(2,1)}, bf16[8,2048]{1,0:T(8,128)(2,1)S(1)}, u32[]{:S(2)}) copy-start(bf16[8,2048]{1,0:T(8,128)(2,1)S(1)} %collective-permute-done.4.rim_ref) | copy-start | bytes 98308
  63.5 29.3 %copy-start.3 = (bf16[8,2048]{1,0:T(8,128)(2,1)}, bf16[8,2048]{1,0:T(8,128)(2,1)S(1)}, u32[]{:S(2)}) copy-start(bf16[8,2048]{1,0:T(8,128)(2,1)S(1)} %collective-permute-done.3.before_ref) | copy-start | bytes 98308
  93.6 13.1 %all-to-all-start.2 = ((bf16[8,144,128]{2,1,0:T(8,128)(2,1)}), bf16[8,144,128]{2,1,0:T(8,128)(2,1)S(1)}, u32[]{:S(2)}, u32[]{:S(2)}) async-start(bf16[8,144,128]{2,1,0:T(8,128)(2,1)} %piece.1), calls=%async_computation.2 | async-start | bytes 589824 | tf_op jit(solution)/shard_map/all_to_all | solution.py:316
  106.7 26.0 %collective-permute-start.5 = (bf16[8,144,128]{2,1,0:T(8,128)(2,1)S(1)}, bf16[8,144,128]{2,1,0:T(8,128)(2,1)S(1)}, u32[]{:S(2)}, u32[]{:S(2)}) collective-permute-start(bf16[8,144,128]{2,1,0:T(8,128)(2,1)S(1)} %all-to-all-done.2.pieces_ref.mine_ref), channel_id=1, source_target_pairs={{0,1},{1,0},{2,3},{3,2},{4,5},{5,4},{6,7},{7,6},{8,9},{9,8},{10,11... | collective-permute-start | bytes 884744 | tf_op jit(solution)/shard_map/ppermute | solution.py:356

commit v4 on v3

--- a/solution.py
+++ b/solution.py
@@ -44,7 +44,7 @@
     return jnp.where(core == 0, 1 - slot, slot)
 
 
-def gate_kernel(query_ref, key_ref, value_ref, grad_ref, taps_ref, up_ref, down_ref, mixed_ref, wide_ref):
+def gate_kernel(core_ref, query_ref, key_ref, value_ref, grad_ref, taps_ref, up_ref, down_ref, mixed_ref, wide_ref):
     short_len = taps_ref.shape[0]
     width = wide_ref.shape[1]
     down_ref[...] = (grad_ref[...].astype(F32) * query_ref[...].astype(F32)).astype(BF)
@@ -163,9 +163,10 @@
 
 
 def rest_kernel(
-    up_ref, got_ref, gated_top_ref, before_ref, grad_ref, mixed_ref, rim_ref, short_ref, long_ref,
-    hi_ref, lo_ref, near_ref, inv_ref, query_out, value_out, wide_ref,
+    core_ref, up_ref, got_ref, gated_top_ref, before_ref, grad_ref, mixed_ref, rim_ref, short_ref, long_ref,
+    hi_ref, lo_ref, near_ref, inv_ref, *rest,
 ):
+    query_out, value_out, wide_ref = rest[-3:]
     gated = with_heads(gated_top_ref[...].astype(F32), up_ref, before_ref[...].astype(F32), got_ref)
     gated_spec = dot(hi_ref[...], gated) + dot(lo_ref[...], gated)
     taps_spec = dot(near_ref[...], twice(long_ref[...]))
@@ -250,56 +251,82 @@
     devices = lax.axis_size("ctx")
     per_half = half_width // WIDTH
     struct = jax.ShapeDtypeStruct
-    count = chan_width // WIDTH
-
-    def chan(rows):
-        return pl.BlockSpec((rows, WIDTH), lambda i: (0, i))
-
-    wide = struct((ROWS, chan_width), BF)
-    top = struct((8, chan_width), BF)
-    up, down, mixed = pl.pallas_call(
-        gate_kernel,
-        out_shape=(wide, wide, wide),
-        grid=(count,),
-        in_specs=[chan(ROWS), chan(ROWS), chan(ROWS), chan(ROWS), chan(short_len)],
-        out_specs=[chan(ROWS), chan(ROWS), chan(ROWS)],
-        scratch_shapes=[pltpu.VMEM((ROWS + 8, WIDTH), F32)],
-        compiler_params=params(),
-        name="gates",
-    )(query_rows, key_rows, value_rows, grad_rows, short_taps)
-    got = shifted(up, 1)
-    back = shifted(down, -1)
-
-    fwd_hi, fwd_lo, near, away, inv_both = (jnp.asarray(t) for t in tables())
-
-    def run_sums(slot, kept):
-        def half(rows):
-            return pl.BlockSpec((rows, WIDTH), lambda i, core: (0, half_of(slot, core[0]) * per_half + i))
-
-        table = pl.BlockSpec((256, 256), lambda i, core: (0, 0))
-        part = struct((half_width // 128, ROWS + 16, 128), BF if slot == 0 else F32)
-        in_specs = [half(ROWS)] * 7 + [half(short_len), half(long_len)] + [table] * 5
-        first = 1 + len(in_specs)
+    def half(slot):
+        return lambda rows: pl.BlockSpec((rows, WIDTH), lambda i, core: (0, half_of(slot, core[0]) * per_half + i))
+
+    def held(rows):
+        return pl.BlockSpec((rows, WIDTH), lambda i, core: (0, i))
+
+    def call(kernel, name, slot, operands, specs, kept, out_shape, out_specs, cost):
+        first = 1 + len(specs)
         return pl.pallas_call(
-            sums_kernel,
-            out_shape=(wide, wide, top, top, part),
+            kernel,
+            out_shape=out_shape,
             grid_spec=pltpu.PrefetchScalarGridSpec(
                 num_scalar_prefetch=1,
                 grid=(per_half,),
-                in_specs=in_specs + [pl.BlockSpec(memory_space=pl.ANY)] * len(kept),
-                out_specs=[
-                    half(ROWS), half(ROWS), half(8), half(8),
-                    pl.BlockSpec((WIDTH // 128, ROWS + 16, 128), lambda i, core: (i, 0, 0)),
-                ],
+                in_specs=specs + [pl.BlockSpec(memory_space=pl.ANY)] * len(kept),
+                out_specs=out_specs,
                 scratch_shapes=[pltpu.VMEM((ROWS + 8, WIDTH), F32)],
             ),
             input_output_aliases={first + k: k for k in range(len(kept))},
             compiler_params=params(),
-            cost_estimate=pl.CostEstimate(flops=2_000_000_000, bytes_accessed=4_000_000, transcendentals=0),
-            name=f"sums_{slot}",
-        )(
-            core, up, got, down, back, mixed, key_rows, value_rows, short_taps, long_taps,
-            fwd_hi, fwd_lo, near, away, inv_both, *kept,
+            cost_estimate=cost,
+            name=f"{name}_{slot}",
+        )(core, *operands, *kept)
+
+    little = pl.CostEstimate(flops=1000, bytes_accessed=1000, transcendentals=0)
+    wide = struct((ROWS, chan_width), BF)
+    top = struct((8, chan_width), BF)
+    own = struct((ROWS, half_width), BF)
+    ups, downs, mixeds, gots, backs = [], [], [], [], []
+    for slot in range(2):
+        part = half(slot)
+        up, down, mixed = call(
+            gate_kernel, "gates", slot, (query_rows, key_rows, value_rows, grad_rows, short_taps),
+            [part(ROWS), part(ROWS), part(ROWS), part(ROWS), part(short_len)], (),
+            (own, own, own), [held(ROWS)] * 3, little,
+        )
+        ups.append(up)
+        downs.append(down)
+        mixeds.append(mixed)
+        gots.append(shifted(up, 1))
+        backs.append(shifted(down, -1))
+
+    ups[0], ups[1], downs[1] = lax.optimization_barrier((ups[0], ups[1], downs[1]))
+
+    fwd_hi, fwd_lo, near, away, inv_both = (jnp.asarray(t) for t in tables())
+    table = pl.BlockSpec((256, 256), lambda i, core: (0, 0))
+
+    def run_sums(slot, kept):
+        part = half(slot)
+        return call(
+            sums_kernel, "sums", slot,
+            (
+                ups[slot], gots[slot], downs[slot], backs[slot], mixeds[slot], key_rows, value_rows, short_taps, long_taps,
+                fwd_hi, fwd_lo, near, away, inv_both,
+            ),
+            [held(ROWS)] * 5 + [part(ROWS), part(ROWS), part(short_len), part(long_len)] + [table] * 5,
+            kept,
+            (wide, wide, top, top, struct((half_width // 128, ROWS + 16, 128), BF if slot == 0 else F32)),
+            [part(ROWS), part(ROWS), part(8), part(8), pl.BlockSpec((WIDTH // 128, ROWS + 16, 128), lambda i, core: (i, 0, 0))],
+            pl.CostEstimate(flops=6_000_000_000, bytes_accessed=8_000_000, transcendentals=0),
+        )
+
+    def run_rest(slot, kept, before, rim):
+        part = half(slot)
+        return call(
+            rest_kernel, "rest", slot,
+            (
+                ups[slot], gots[slot], gated_top, before, grad_rows, mixed_grad, rim, short_taps, long_taps,
+                fwd_hi, fwd_lo, near, inv_both,
+            ),
+            [held(ROWS), held(ROWS), part(8), part(8), part(ROWS), part(ROWS), part(8), part(short_len), part(long_len)]
+            + [table] * 4,
+            kept,
+            (wide, wide),
+            [part(ROWS), part(ROWS)],
+            pl.CostEstimate(flops=4_000_000_000, bytes_accessed=5_000_000, transcendentals=0),
         )
 
     *kept, part_sent = run_sums(0, ())
@@ -319,32 +346,15 @@
         return pl.pallas_call(kernel, out_shape=struct((count, depth, 128), BF), compiler_params=params(SMALL), name=name)
 
     total = (part_own + part_got.astype(F32)).astype(BF)
+    scattered = swap(total, along)
+    scattered, gated_top, mixed_top = lax.optimization_barrier((scattered, gated_top, mixed_top))
     before = shifted(gated_top, 1)
     rim = shifted(mixed_top, -1)
-    scattered = small_call(line_kernel, "line", lines)(swap(total, along))
-    scattered, before, rim = lax.optimization_barrier((scattered, before, rim))
-    spread = small_call(piece_kernel, "piece", blocks)(swap(scattered, across))
-    gathered = swap(spread, along)
-    table = pl.BlockSpec((256, 256), lambda i: (0, 0))
-    query_grad, value_grad = pl.pallas_call(
-        rest_kernel,
-        out_shape=(wide, wide),
-        grid=(count,),
-        in_specs=[
-            chan(ROWS), chan(ROWS), chan(8), chan(8), chan(ROWS), chan(ROWS), chan(8),
-            chan(short_len), chan(long_len), table, table, table, table,
-        ],
-        out_specs=[chan(ROWS), chan(ROWS)],
-        scratch_shapes=[pltpu.VMEM((ROWS + 8, WIDTH), F32)],
-        compiler_params=params(),
-        cost_estimate=pl.CostEstimate(flops=4_000_000_000, bytes_accessed=5_000_000, transcendentals=0),
-        name="rest",
-    )(
-        up, got, gated_top, before, grad_rows, mixed_grad, rim, short_taps, long_taps,
-        fwd_hi, fwd_lo, near, inv_both,
-    )
-
-    gathered, query_grad, value_grad = lax.optimization_barrier((gathered, query_grad, value_grad))
+    crossed = swap(small_call(line_kernel, "line", lines)(scattered), across)
+    crossed, before, rim = lax.optimization_barrier((crossed, before, rim))
+    gathered = swap(small_call(piece_kernel, "piece", blocks)(crossed), along)
+    grads = run_rest(1, run_rest(0, (), before, rim), before, rim)
+    gathered, query_grad, value_grad = lax.optimization_barrier((gathered, *grads))
     ways = lax.axis_size("tp")
     norms = pl.pallas_call(
         norm_kernel,

time: 134 us -> 129 us (0.963)
  the two profiles are of different devices: /device:TPU:1 before, /device:TPU:32 now
where the time goes in v4:
time: 129 us; the launch traced here: 128 us
  starting transfers between devices  49.2 us (38%)
  blocking collectives  32.5 us (25%)
  Pallas kernels  26.5 us (21%)
  waiting for transfers between devices  16.2 us (13%)
  local copies, waits for them, and re-layouts  1.56 us (1%)
    ppermute x6, starting transfers between devices, shifted(): lax.ppermute(value, 'ctx', [(i, i + by) for i in range(devices) if 0 <= i...  34.6 us
    pallas_call x6, Pallas kernels, call(): pl.pallas_call(kernel, out_shape=out_shape, grid_spec=pltpu.PrefetchScala...  23.9 us
    all_to_all x1, blocking collectives, on_device(): norms = lax.all_to_all(norms, ('tp', 'dp'), 0, 0, tiled=True)  16.6 us
    all_to_all x1, blocking collectives, swap(): lax.all_to_all(value, 'ctx', 0, 0, tiled=True, axis_index_groups=groups)  15.9 us
    ppermute x6, waiting for transfers between devices, shifted(): lax.ppermute(value, 'ctx', [(i, i + by) for i in range(devices) if 0 <= i...  13.9 us
    all_to_all x2, starting transfers between devices, swap(): lax.all_to_all(value, 'ctx', 0, 0, tiled=True, axis_index_groups=groups)  10.8 us
  transfers between devices with their start and end apart: 10, of which 2 were waited for; matrix products, arithmetic and copies ran while one was open for 0% of the time, Pallas kernels for 17%

profile of v4, /device:TPU:32, one launch (start us, length us, event | category | flops | bytes accessed | tf_op | source)
XLA Modules:
  0.0 127.8 jit_solution(11008137329469574420)
XLA Ops:
  0.6 2.8 %gates_0.1 = (bf16[128,1024]{1,0:T(8,128)(2,1)}, bf16[128,1024]{1,0:T(8,128)(2,1)}, bf16[128,1024]{1,0:T(8,128)(2,1)}) custom-call(s32[1]{0:T(128)} %bitcast.core_ref, bf16[128,2048]{1,0:T(8,128)(2,1)} %bitcast.8, bf16[128,2048]{1,0:T(8,128)(2,1)} %bitcast.10, bf16[128,2048]{1,0:T(8,128)(2,1)} %bitcast.14, bf16[128,2048]{1,0:T(8,128)(2,1)} %bitcast.18, ...), custom_call_target="tpu_custom_call" | custom-call | flops 1000 | bytes 1000 | tf_op jit(solution)/shard_map/gates_0/pallas_call | solution.py:262
  3.4 4.3 %collective-permute-start.2 = (bf16[128,1024]{1,0:T(8,128)(2,1)}, bf16[128,1024]{1,0:T(8,128)(2,1)S(1)}, u32[]{:S(2)}, u32[]{:S(2)}) collective-permute-start(bf16[128,1024]{1,0:T(8,128)(2,1)} %get-tuple-element.45.up_ref), channel_id=1, source_target_pairs={{0,8},{8,16},{16,24},{24,32},{32,40},{40,48},{48,56},{56,64},{64,7... | collective-permute-start | bytes 786440 | tf_op jit(solution)/shard_map/ppermute | solution.py:242
  7.7 10.3 %collective-permute-start.3 = (bf16[128,1024]{1,0:T(8,128)(2,1)}, bf16[128,1024]{1,0:T(8,128)(2,1)S(1)}, u32[]{:S(2)}, u32[]{:S(2)}) collective-permute-start(bf16[128,1024]{1,0:T(8,128)(2,1)} %get-tuple-element.46.down_ref), channel_id=1, source_target_pairs={{8,0},{16,8},{24,16},{32,24},{40,32},{48,40},{56,48},{64,56},{72,6... | collective-permute-start | bytes 786440 | tf_op jit(solution)/shard_map/ppermute | solution.py:242
  18.0 2.8 %gates_1.1 = (bf16[128,1024]{1,0:T(8,128)(2,1)}, bf16[128,1024]{1,0:T(8,128)(2,1)}, bf16[128,1024]{1,0:T(8,128)(2,1)}) custom-call(s32[1]{0:T(128)} %bitcast.core_ref, bf16[128,2048]{1,0:T(8,128)(2,1)} %bitcast.9, bf16[128,2048]{1,0:T(8,128)(2,1)} %bitcast.11, bf16[128,2048]{1,0:T(8,128)(2,1)} %bitcast.15, bf16[128,2048]{1,0:T(8,128)(2,1)} %bitcast.19, ...), custom_call_target="tpu_custom_call" | custom-call | flops 1000 | bytes 1000 | tf_op jit(solution)/shard_map/gates_1/pallas_call | solution.py:262
  20.8 1.9 %collective-permute-start = (bf16[128,1024]{1,0:T(8,128)(2,1)}, bf16[128,1024]{1,0:T(8,128)(2,1)S(1)}, u32[]{:S(2)}, u32[]{:S(2)}) collective-permute-start(bf16[128,1024]{1,0:T(8,128)(2,1)} %get-tuple-element.42.up_ref), channel_id=1, source_target_pairs={{0,8},{8,16},{16,24},{24,32},{32,40},{40,48},{48,56},{56,64},{64,7... | collective-permute-start | bytes 786440 | tf_op jit(solution)/shard_map/ppermute | solution.py:242
  22.7 12.0 %collective-permute-start.1 = (bf16[128,1024]{1,0:T(8,128)(2,1)}, bf16[128,1024]{1,0:T(8,128)(2,1)S(1)}, u32[]{:S(2)}, u32[]{:S(2)}) collective-permute-start(bf16[128,1024]{1,0:T(8,128)(2,1)} %get-tuple-element.43.down_ref), channel_id=1, source_target_pairs={{8,0},{16,8},{24,16},{32,24},{40,32},{48,40},{56,48},{64,56},{72,6... | collective-permute-start | bytes 786440 | tf_op jit(solution)/shard_map/ppermute | solution.py:242
  34.7 0.0 collective-permute-done.2.got_ref
  34.8 0.0 copy-start
  34.8 0.0 collective-permute-done.3.back_ref
  34.8 0.0 copy-start.3
  34.8 0.7 copy-done
  35.5 0.1 copy-done.3
  35.5 4.9 %sums_0.1 = (bf16[128,2048]{1,0:T(8,128)(2,1)}, bf16[128,2048]{1,0:T(8,128)(2,1)}, bf16[8,2048]{1,0:T(8,128)(2,1)}, bf16[8,2048]{1,0:T(8,128)(2,1)}, bf16[8,144,128]{2,1,0:T(8,128)(2,1)}) custom-call(s32[1]{0:T(128)} %bitcast.core_ref, bf16[128,1024]{1,0:T(8,128)(2,1)} %get-tuple-element.45.up_ref, bf16[128,1024]{1,0:T(8,128)(2,1)} %copy-done, ...), custom_call_target="tpu_custom_call" | custom-call | flops 6000000000 | bytes 8000000 | tf_op jit(solution)/shard_map/sums_0/pallas_call | solution.py:262
  40.5 1.9 %collective-permute-start.4 = (bf16[8,144,128]{2,1,0:T(8,128)(2,1)}, bf16[8,144,128]{2,1,0:T(8,128)(2,1)S(1)}, u32[]{:S(2)}, u32[]{:S(2)}) collective-permute-start(bf16[8,144,128]{2,1,0:T(8,128)(2,1)} %get-tuple-element.53), channel_id=1, source_target_pairs={{0,1},{1,0},{2,3},{3,2},{4,5},{5,4},{6,7},{7,6},{8,9},{9,8},{10,11... | collective-permute-start | bytes 884744 | tf_op jit(solution)/shard_map/ppermute | solution.py:333
  42.4 0.0 collective-permute-done.got_ref
  42.4 0.0 copy-start.1
  42.4 0.0 collective-permute-done.1.back_ref
  42.4 0.0 copy-start.2
  42.4 0.7 copy-done.1
  43.1 0.1 copy-done.2
  43.2 5.0 %sums_1.1 = (bf16[128,2048]{1,0:T(8,128)(2,1)}, bf16[128,2048]{1,0:T(8,128)(2,1)}, bf16[8,2048]{1,0:T(8,128)(2,1)}, bf16[8,2048]{1,0:T(8,128)(2,1)}, f32[8,144,128]{2,1,0:T(8,128)}) custom-call(s32[1]{0:T(128)} %bitcast.core_ref, ...), custom_call_target="tpu_custom_call", output_to_operand_aliasing={{0}: (15, {}), {1}: (16, {}), {2}: (17, {}), {3}: (18, {})} | custom-call | flops 6000000000 | bytes 8000000 | tf_op jit(solution)/shard_map/sums_1/pallas_call | solution.py:262
  48.2 0.0 collective-permute-done.4
  48.2 1.1 add_convert_fusion
  49.3 15.9 %all_to_all.20.arrived_ref = bf16[8,144,128]{2,1,0:T(8,128)(2,1)S(1)} all-to-all(bf16[8,144,128]{2,1,0:T(8,128)(2,1)S(1)} %add_convert_fusion), channel_id=1, replica_groups={{0,8,16,24,32,40,48,56},{64,72,80,88,96,104,112,120},{128,136,144,152,1..., dimensions={0} | all-to-all | bytes 589824 | tf_op jit(solution)/shard_map/all_to_all | solution.py:343
  65.2 0.8 line.1
  66.0 0.0 copy-start.7
  66.0 0.0 copy-start.6
  66.0 7.3 %all-to-all-start.1 = ((bf16[8,144,128]{2,1,0:T(8,128)(2,1)}), bf16[8,144,128]{2,1,0:T(8,128)(2,1)S(1)}, u32[]{:S(2)}, u32[]{:S(2)}) async-start(bf16[8,144,128]{2,1,0:T(8,128)(2,1)} %line.1), calls=%async_computation.1 | async-start | bytes 589824 | tf_op jit(solution)/shard_map/all_to_all | solution.py:343
  73.3 0.0 copy-done.7
  73.3 4.1 %collective-permute-start.6 = (bf16[8,2048]{1,0:T(8,128)(2,1)S(1)}, bf16[8,2048]{1,0:T(8,128)(2,1)S(1)}, u32[]{:S(2)}, u32[]{:S(2)}) collective-permute-start(bf16[8,2048]{1,0:T(8,128)(2,1)S(1)} %copy-done.7), channel_id=1, source_target_pairs={{8,0},{16,8},{24,16},{32,24},{40,32},{48,40},{56,48},{64,56},{72,6... | collective-permute-start | bytes 98312 | tf_op jit(solution)/shard_map/ppermute | solution.py:242
  77.5 0.0 copy-done.6
  77.5 1.9 %collective-permute-start.5 = (bf16[8,2048]{1,0:T(8,128)(2,1)S(1)}, bf16[8,2048]{1,0:T(8,128)(2,1)S(1)}, u32[]{:S(2)}, u32[]{:S(2)}) collective-permute-start(bf16[8,2048]{1,0:T(8,128)(2,1)S(1)} %copy-done.6), channel_id=1, source_target_pairs={{0,8},{8,16},{16,24},{24,32},{32,40},{40,48},{48,56},{56,64},{64,7... | collective-permute-start | bytes 98312 | tf_op jit(solution)/shard_map/ppermute | solution.py:242
  79.4 0.0 collective-permute-done.6.rim_ref
  79.4 0.0 copy-start.4
  79.4 13.9 %collective-permute-done.5.before_ref = bf16[8,2048]{1,0:T(8,128)(2,1)S(1)} collective-permute-done((bf16[8,2048]{1,0:T(8,128)(2,1)S(1)}, bf16[8,2048]{1,0:T(8,128)(2,1)S(1)}, u32[]{:S(2)}, u32[]{:S(2)}) %collective-permute-start.5) | collective-permute-done | bytes 32800 | tf_op jit(solution)/shard_map/ppermute | solution.py:242
  93.3 0.0 copy-start.5
  93.3 0.0 all-to-all-done.1.arrived_ref
  93.3 0.8 piece.1
  94.2 0.0 copy-done.4
  94.2 0.0 copy-done.5
  94.2 3.4 %all-to-all-start.2 = ((bf16[8,144,128]{2,1,0:T(8,128)(2,1)}), bf16[8,144,128]{2,1,0:T(8,128)(2,1)S(1)}, u32[]{:S(2)}, u32[]{:S(2)}) async-start(bf16[8,144,128]{2,1,0:T(8,128)(2,1)} %piece.1), calls=%async_computation.2 | async-start | bytes 589824 | tf_op jit(solution)/shard_map/all_to_all | solution.py:343
  97.6 4.2 %rest_0.1 = (bf16[128,2048]{1,0:T(8,128)(2,1)}, bf16[128,2048]{1,0:T(8,128)(2,1)}) custom-call(s32[1]{0:T(128)} %bitcast.core_ref, bf16[128,1024]{1,0:T(8,128)(2,1)} %get-tuple-element.45.up_ref, bf16[128,1024]{1,0:T(8,128)(2,1)} %copy-done, bf16[8,2048]{1,0:T(8,128)(2,1)} %get-tuple-element.57.gated_top_ref, bf16[8,2048]{1,0:T(8,128)(2,1)} %copy-done.5, ...), custom_call_target="tpu_custom_call" | custom-call | flops 4000000000 | bytes 5000000 | tf_op jit(solution)/shard_map/rest_0/pallas_call | solution.py:262
  101.9 4.2 %rest_1.1 = (bf16[128,2048]{1,0:T(8,128)(2,1)}, bf16[128,2048]{1,0:T(8,128)(2,1)}) custom-call(s32[1]{0:T(128)} %bitcast.core_ref, bf16[128,1024]{1,0:T(8,128)(2,1)} %get-tuple-element.42.up_ref, bf16[128,1024]{1,0:T(8,128)(2,1)} %copy-done.1, bf16[8,2048]{1,0:T(8,128)(2,1)} %get-tuple-element.57.gated_top_ref, ...), custom_call_target="tpu_custom_call", output_to_operand_aliasing={{0}: (14, {}), {1}: (15, {})} | custom-call | flops 4000000000 | bytes 5000000 | tf_op jit(solution)/shard_map/rest_1/pallas_call | solution.py:262
  106.1 2.2 %all-to-all-done.2.pieces_ref.mine_ref = bf16[8,144,128]{2,1,0:T(8,128)(2,1)S(1)} async-done(((bf16[8,144,128]{2,1,0:T(8,128)(2,1)}), bf16[8,144,128]{2,1,0:T(8,128)(2,1)S(1)}, u32[]{:S(2)}, u32[]{:S(2)}) %all-to-all-start.2) | async-done | bytes 294944 | tf_op jit(solution)/shard_map/all_to_all | solution.py:343
  108.4 1.9 %collective-permute-start.7 = (bf16[8,144,128]{2,1,0:T(8,128)(2,1)S(1)}, bf16[8,144,128]{2,1,0:T(8,128)(2,1)S(1)}, u32[]{:S(2)}, u32[]{:S(2)}) collective-permute-start(bf16[8,144,128]{2,1,0:T(8,128)(2,1)S(1)} %all-to-all-done.2.pieces_ref.mine_ref), channel_id=1, source_target_pairs={{0,1},{1,0},{2,3},{3,2},{4,5},{5,4},{6,7},{7,6},{8,9},{9,8},{10,11... | collective-permute-start | bytes 884744 | tf_op jit(solution)/shard_map/ppermute | solution.py:366
  110.3 16.6 %all_to_all.21.norms_ref = f32[8,1,128]{2,1,0:T(1,128)S(1)} all-to-all(f32[8,1,128]{2,1,0:T(1,128)S(1)} %norm.1), channel_id=1, replica_groups=mesh['ctx'=64,'tp'=4,'dp'=2] {'tp','dp'}, dimensions={0} | all-to-all | bytes 8192 | tf_op jit(solution)/shard_map/all_to_all | solution.py:365
  126.9 0.0 collective-permute-done.7.other_ref
  126.9 0.9 scale.1
  (1 shorter events, 0.0 us)
Async XLA Ops:
  3.4 31.4 %collective-permute-start.2 = (bf16[128,1024]{1,0:T(8,128)(2,1)}, bf16[128,1024]{1,0:T(8,128)(2,1)S(1)}, u32[]{:S(2)}, u32[]{:S(2)}) collective-permute-start(bf16[128,1024]{1,0:T(8,128)(2,1)} %get-tuple-element.45.up_ref), channel_id=1, source_target_pairs={{0,8},{8,16},{16,24},{24,32},{32,40},{40,48},{48,56},{56,64},{64,7... | collective-permute-start | bytes 786440 | tf_op jit(solution)/shard_map/ppermute | solution.py:242
  7.7 27.1 %collective-permute-start.3 = (bf16[128,1024]{1,0:T(8,128)(2,1)}, bf16[128,1024]{1,0:T(8,128)(2,1)S(1)}, u32[]{:S(2)}, u32[]{:S(2)}) collective-permute-start(bf16[128,1024]{1,0:T(8,128)(2,1)} %get-tuple-element.46.down_ref), channel_id=1, source_target_pairs={{8,0},{16,8},{24,16},{32,24},{40,32},{48,40},{56,48},{64,56},{72,6... | collective-permute-start | bytes 786440 | tf_op jit(solution)/shard_map/ppermute | solution.py:242
  20.8 21.6 %collective-permute-start = (bf16[128,1024]{1,0:T(8,128)(2,1)}, bf16[128,1024]{1,0:T(8,128)(2,1)S(1)}, u32[]{:S(2)}, u32[]{:S(2)}) collective-permute-start(bf16[128,1024]{1,0:T(8,128)(2,1)} %get-tuple-element.42.up_ref), channel_id=1, source_target_pairs={{0,8},{8,16},{16,24},{24,32},{32,40},{40,48},{48,56},{56,64},{64,7... | collective-permute-start | bytes 786440 | tf_op jit(solution)/shard_map/ppermute | solution.py:242
  22.7 19.7 %collective-permute-start.1 = (bf16[128,1024]{1,0:T(8,128)(2,1)}, bf16[128,1024]{1,0:T(8,128)(2,1)S(1)}, u32[]{:S(2)}, u32[]{:S(2)}) collective-permute-start(bf16[128,1024]{1,0:T(8,128)(2,1)} %get-tuple-element.43.down_ref), channel_id=1, source_target_pairs={{8,0},{16,8},{24,16},{32,24},{40,32},{48,40},{56,48},{64,56},{72,6... | collective-permute-start | bytes 786440 | tf_op jit(solution)/shard_map/ppermute | solution.py:242
  34.8 0.7 copy-start
  34.8 0.8 copy-start.3
  40.5 7.7 %collective-permute-start.4 = (bf16[8,144,128]{2,1,0:T(8,128)(2,1)}, bf16[8,144,128]{2,1,0:T(8,128)(2,1)S(1)}, u32[]{:S(2)}, u32[]{:S(2)}) collective-permute-start(bf16[8,144,128]{2,1,0:T(8,128)(2,1)} %get-tuple-element.53), channel_id=1, source_target_pairs={{0,1},{1,0},{2,3},{3,2},{4,5},{5,4},{6,7},{7,6},{8,9},{9,8},{10,11... | collective-permute-start | bytes 884744 | tf_op jit(solution)/shard_map/ppermute | solution.py:333
  42.4 0.7 copy-start.1
  42.4 0.8 copy-start.2
  66.0 7.3 %copy-start.7 = (bf16[8,2048]{1,0:T(8,128)(2,1)S(1)}, bf16[8,2048]{1,0:T(8,128)(2,1)}, u32[]{:S(2)}) copy-start(bf16[8,2048]{1,0:T(8,128)(2,1)} %get-tuple-element.58) | copy-start | bytes 98308
  66.0 11.5 %copy-start.6 = (bf16[8,2048]{1,0:T(8,128)(2,1)S(1)}, bf16[8,2048]{1,0:T(8,128)(2,1)}, u32[]{:S(2)}) copy-start(bf16[8,2048]{1,0:T(8,128)(2,1)} %get-tuple-element.57.gated_top_ref) | copy-start | bytes 98308
  66.0 27.3 %all-to-all-start.1 = ((bf16[8,144,128]{2,1,0:T(8,128)(2,1)}), bf16[8,144,128]{2,1,0:T(8,128)(2,1)S(1)}, u32[]{:S(2)}, u32[]{:S(2)}) async-start(bf16[8,144,128]{2,1,0:T(8,128)(2,1)} %line.1), calls=%async_computation.1 | async-start | bytes 589824 | tf_op jit(solution)/shard_map/all_to_all | solution.py:343
  73.3 6.1 %collective-permute-start.6 = (bf16[8,2048]{1,0:T(8,128)(2,1)S(1)}, bf16[8,2048]{1,0:T(8,128)(2,1)S(1)}, u32[]{:S(2)}, u32[]{:S(2)}) collective-permute-start(bf16[8,2048]{1,0:T(8,128)(2,1)S(1)} %copy-done.7), channel_id=1, source_target_pairs={{8,0},{16,8},{24,16},{32,24},{40,32},{48,40},{56,48},{64,56},{72,6... | collective-permute-start | bytes 98312 | tf_op jit(solution)/shard_map/ppermute | solution.py:242
  77.5 15.9 %collective-permute-start.5 = (bf16[8,2048]{1,0:T(8,128)(2,1)S(1)}, bf16[8,2048]{1,0:T(8,128)(2,1)S(1)}, u32[]{:S(2)}, u32[]{:S(2)}) collective-permute-start(bf16[8,2048]{1,0:T(8,128)(2,1)S(1)} %copy-done.6), channel_id=1, source_target_pairs={{0,8},{8,16},{16,24},{24,32},{32,40},{40,48},{48,56},{56,64},{64,7... | collective-permute-start | bytes 98312 | tf_op jit(solution)/shard_map/ppermute | solution.py:242
  79.4 14.8 %copy-start.4 = (bf16[8,2048]{1,0:T(8,128)(2,1)}, bf16[8,2048]{1,0:T(8,128)(2,1)S(1)}, u32[]{:S(2)}) copy-start(bf16[8,2048]{1,0:T(8,128)(2,1)S(1)} %collective-permute-done.6.rim_ref) | copy-start | bytes 98308
  93.3 0.9 copy-start.5
  94.2 14.2 %all-to-all-start.2 = ((bf16[8,144,128]{2,1,0:T(8,128)(2,1)}), bf16[8,144,128]{2,1,0:T(8,128)(2,1)S(1)}, u32[]{:S(2)}, u32[]{:S(2)}) async-start(bf16[8,144,128]{2,1,0:T(8,128)(2,1)} %piece.1), calls=%async_computation.2 | async-start | bytes 589824 | tf_op jit(solution)/shard_map/all_to_all | solution.py:343
  108.4 18.5 %collective-permute-start.7 = (bf16[8,144,128]{2,1,0:T(8,128)(2,1)S(1)}, bf16[8,144,128]{2,1,0:T(8,128)(2,1)S(1)}, u32[]{:S(2)}, u32[]{:S(2)}) collective-permute-start(bf16[8,144,128]{2,1,0:T(8,128)(2,1)S(1)} %all-to-all-done.2.pieces_ref.mine_ref), channel_id=1, source_target_pairs={{0,1},{1,0},{2,3},{3,2},{4,5},{5,4},{6,7},{7,6},{8,9},{9,8},{10,11... | collective-permute-start | bytes 884744 | tf_op jit(solution)/shard_map/ppermute | solution.py:366

commit v5 on v4

--- a/solution.py
+++ b/solution.py
@@ -44,10 +44,10 @@
     return jnp.where(core == 0, 1 - slot, slot)
 
 
-def gate_kernel(core_ref, query_ref, key_ref, value_ref, grad_ref, taps_ref, up_ref, down_ref, mixed_ref, wide_ref):
+def gate_kernel(place_ref, query_ref, key_ref, value_ref, grad_ref, taps_ref, first_ref, second_ref, mixed_ref, wide_ref):
     short_len = taps_ref.shape[0]
     width = wide_ref.shape[1]
-    down_ref[...] = (grad_ref[...].astype(F32) * query_ref[...].astype(F32)).astype(BF)
+    mid = (grad_ref[...].astype(F32) * query_ref[...].astype(F32)).astype(BF)
     wide_ref[0:8, :] = jnp.zeros((8, width), F32)
     wide_ref[8:, :] = value_ref[...].astype(F32)
     total = taps_ref[0:1, :] * wide_ref[8 : 8 + ROWS, :]
@@ -59,8 +59,21 @@
     row = lax.broadcasted_iota(jnp.int32, (8, width), 0)
     wide_ref[0:16, :] = gated[0:16]
     top = jnp.where(row < 2, wide_ref[6:14, :], wide_ref[ROWS : ROWS + 8, :])
-    up_ref[0:16, :] = jnp.concatenate([top, gated[8:16]], axis=0).astype(BF)
-    up_ref[16:ROWS, :] = gated[16:].astype(BF)
+    begin = jnp.concatenate([top, gated[8:16]], axis=0).astype(BF)
+    gated = gated[16:].astype(BF)
+
+    def write(up_ref, down_ref):
+        up_ref[0:16, :] = begin
+        up_ref[16:ROWS, :] = gated
+        down_ref[...] = mid
+
+    @pl.when(place_ref[1] == 1)
+    def _():
+        write(first_ref, second_ref)
+
+    @pl.when(place_ref[1] == 0)
+    def _():
+        write(second_ref, first_ref)
 
 
 def own_head(wide_ref, tail, key_ref, value_ref, taps_ref):
@@ -75,11 +88,17 @@
     return mixed, (key * mixed).astype(BF).astype(F32)
 
 
-def with_heads(own_head_rows, up_ref, got_head_rows, got_ref):
+def by_direction(place_ref, first_ref, second_ref):
+    odd = place_ref[1] == 1
+    first, second = first_ref[...], second_ref[...]
+    return jnp.where(odd, first, second), jnp.where(odd, second, first)
+
+
+def with_heads(own_head_rows, up, got_head_rows, got):
     parts = []
-    for head, ref in ((own_head_rows, up_ref), (got_head_rows, got_ref)):
-        parts.append(jnp.concatenate([head, ref[0:16, :].astype(F32)[8:16]], axis=0).astype(BF))
-        parts.append(ref[16:ROWS, :])
+    for head, rows in ((own_head_rows, up), (got_head_rows, got)):
+        parts.append(jnp.concatenate([head, rows[0:16].astype(F32)[8:16]], axis=0).astype(BF))
+        parts.append(rows[16:])
     return jnp.concatenate(parts, axis=0)
 
 
@@ -114,28 +133,28 @@
 
 
 def sums_kernel(
-    core_ref, up_ref, got_ref, down_ref, back_ref, mixed_ref, key_ref, value_ref, short_ref, long_ref,
+    place_ref, sent_a_ref, sent_b_ref, got_a_ref, got_b_ref, mixed_ref, key_ref, value_ref, short_ref, long_ref,
     hi_ref, lo_ref, near_ref, away_ref, inv_ref, *rest,
 ):
     key_out, mixed_out, gated_top_out, mixed_top_out, part_ref, wide_ref = rest[-6:]
     short_len = short_ref.shape[0]
     width = wide_ref.shape[1]
     row = lax.broadcasted_iota(jnp.int32, (8, width), 0)
-    got_top = got_ref[0:16, :].astype(F32)[0:8]
+    up, mid = by_direction(place_ref, sent_a_ref, sent_b_ref)
+    ahead, got = by_direction(place_ref, got_a_ref, got_b_ref)
+    got_top = got[0:16].astype(F32)[0:8]
     mixed_top, gated_top = own_head(wide_ref, got_top, key_ref, value_ref, short_ref)
     gated_top_out[...] = gated_top.astype(BF)
     wide_ref[8:16, :] = got_top
     before = jnp.where(row < 6, 0.0, wide_ref[2:10, :])
-    gated = with_heads(gated_top, up_ref, before, got_ref)
-    mid = down_ref[...]
-    ahead = back_ref[...]
+    gated = with_heads(gated_top, up, before, got)
     gated_spec = dot(hi_ref[...], gated) + dot(lo_ref[...], gated)
     mid_spec = dot(near_ref[...], twice(mid))
     both_spec = mid_spec + dot(away_ref[...], twice(ahead))
     taps_spec = dot(near_ref[...], twice(long_ref[...]))
     long_sum = inverse(inv_ref, product(mid_spec, gated_spec, True))
     gated_grad = inverse(inv_ref, product(both_spec, taps_spec, True))
-    next_top = back_ref[0:16, :].astype(F32)[0:8]
+    next_top = ahead[0:16].astype(F32)[0:8]
     lines = [jnp.zeros((3, width), F32)]
     for gap in range(5, 0, -1):
         line = gated_top[gap : gap + 1] * next_top[0:1]
@@ -163,11 +182,13 @@
 
 
 def rest_kernel(
-    core_ref, up_ref, got_ref, gated_top_ref, before_ref, grad_ref, mixed_ref, rim_ref, short_ref, long_ref,
+    place_ref, sent_a_ref, sent_b_ref, got_a_ref, got_b_ref, gated_top_ref, before_ref, grad_ref, mixed_ref, rim_ref, short_ref, long_ref,
     hi_ref, lo_ref, near_ref, inv_ref, *rest,
 ):
     query_out, value_out, wide_ref = rest[-3:]
-    gated = with_heads(gated_top_ref[...].astype(F32), up_ref, before_ref[...].astype(F32), got_ref)
+    up, _ = by_direction(place_ref, sent_a_ref, sent_b_ref)
+    _, got = by_direction(place_ref, got_a_ref, got_b_ref)
+    gated = with_heads(gated_top_ref[...].astype(F32), up, before_ref[...].astype(F32), got)
     gated_spec = dot(hi_ref[...], gated) + dot(lo_ref[...], gated)
     taps_spec = dot(near_ref[...], twice(long_ref[...]))
     long_out = inverse(inv_ref, product(gated_spec, taps_spec, False))
@@ -210,7 +231,7 @@
     norm_ref[...] = jnp.broadcast_to(square[None], norm_ref.shape)
 
 
-def scale_kernel(limit, core_ref, mine_ref, other_ref, norms_ref, long_ref, short_ref):
+def scale_kernel(limit, place_ref, mine_ref, other_ref, norms_ref, long_ref, short_ref):
     norm_sq = norms_ref[0]
     for device in range(1, norms_ref.shape[0]):
         norm_sq = norm_sq + norms_ref[device]
@@ -237,6 +258,12 @@
     return pltpu.CompilerParams(vmem_limit_bytes=limit)
 
 
+def swapped(value, phase):
+    devices = lax.axis_size("ctx")
+    starts = range(1 - phase, devices - 1, 2)
+    return lax.ppermute(value, "ctx", [(i, i + 1) for i in starts] + [(i + 1, i) for i in starts])
+
+
 def shifted(value, by):
     devices = lax.axis_size("ctx")
     return lax.ppermute(value, "ctx", [(i, i + by) for i in range(devices) if 0 <= i + by < devices])
@@ -247,7 +274,7 @@
     chan_width = query_rows.shape[1]
     half_width = chan_width // 2
     short_len, long_len = short_taps.shape[0], long_taps.shape[0]
-    core = lax.axis_index("dp").astype(jnp.int32).reshape(1)
+    core = jnp.stack([lax.axis_index("dp"), lax.axis_index("ctx") % 2]).astype(jnp.int32)
     devices = lax.axis_size("ctx")
     per_half = half_width // WIDTH
     struct = jax.ShapeDtypeStruct
@@ -279,21 +306,18 @@
     wide = struct((ROWS, chan_width), BF)
     top = struct((8, chan_width), BF)
     own = struct((ROWS, half_width), BF)
-    ups, downs, mixeds, gots, backs = [], [], [], [], []
+    sent, mixeds, got = [], [], []
     for slot in range(2):
         part = half(slot)
-        up, down, mixed = call(
+        first, second, mixed = call(
             gate_kernel, "gates", slot, (query_rows, key_rows, value_rows, grad_rows, short_taps),
             [part(ROWS), part(ROWS), part(ROWS), part(ROWS), part(short_len)], (),
             (own, own, own), [held(ROWS)] * 3, little,
         )
-        ups.append(up)
-        downs.append(down)
+        sent.append((first, second))
         mixeds.append(mixed)
-        gots.append(shifted(up, 1))
-        backs.append(shifted(down, -1))
-
-    ups[0], ups[1], downs[1] = lax.optimization_barrier((ups[0], ups[1], downs[1]))
+        got.append((swapped(first, 0), swapped(second, 1)))
+    sent = lax.optimization_barrier(sent)
 
     fwd_hi, fwd_lo, near, away, inv_both = (jnp.asarray(t) for t in tables())
     table = pl.BlockSpec((256, 256), lambda i, core: (0, 0))
@@ -303,7 +327,7 @@
         return call(
             sums_kernel, "sums", slot,
             (
-                ups[slot], gots[slot], downs[slot], backs[slot], mixeds[slot], key_rows, value_rows, short_taps, long_taps,
+                *sent[slot], *got[slot], mixeds[slot], key_rows, value_rows, short_taps, long_taps,
                 fwd_hi, fwd_lo, near, away, inv_both,
             ),
             [held(ROWS)] * 5 + [part(ROWS), part(ROWS), part(short_len), part(long_len)] + [table] * 5,
@@ -318,10 +342,10 @@
         return call(
             rest_kernel, "rest", slot,
             (
-                ups[slot], gots[slot], gated_top, before, grad_rows, mixed_grad, rim, short_taps, long_taps,
+                *sent[slot], *got[slot], gated_top, before, grad_rows, mixed_grad, rim, short_taps, long_taps,
                 fwd_hi, fwd_lo, near, inv_both,
             ),
-            [held(ROWS), held(ROWS), part(8), part(8), part(ROWS), part(ROWS), part(8), part(short_len), part(long_len)]
+            [held(ROWS)] * 4 + [part(8), part(8), part(ROWS), part(ROWS), part(8), part(short_len), part(long_len)]
             + [table] * 4,
             kept,
             (wide, wide),
@@ -351,7 +375,6 @@
     before = shifted(gated_top, 1)
     rim = shifted(mixed_top, -1)
     crossed = swap(small_call(line_kernel, "line", lines)(scattered), across)
-    crossed, before, rim = lax.optimization_barrier((crossed, before, rim))
     gathered = swap(small_call(piece_kernel, "piece", blocks)(crossed), along)
     grads = run_rest(1, run_rest(0, (), before, rim), before, rim)
     gathered, query_grad, value_grad = lax.optimization_barrier((gathered, *grads))

time: 129 us -> 121 us (0.938)
  the two profiles are of different devices: /device:TPU:32 before, /device:TPU:1 now
where the time goes in v5:
time: 121 us; the launch traced here: 119 us
  starting transfers between devices  45.2 us (37%)
  blocking collectives  32.9 us (27%)
  Pallas kernels  31.2 us (26%)
  waiting for transfers between devices  4.83 us (4%)
  local copies, waits for them, and re-layouts  2.16 us (2%)
  other arithmetic  1.79 us (1%)
    pallas_call x6, Pallas kernels, call(): pl.pallas_call(kernel, out_shape=out_shape, grid_spec=pltpu.PrefetchScala...  28.1 us
    ppermute x4, starting transfers between devices, swapped(): lax.ppermute(value, 'ctx', [(i, i + 1) for i in starts] + [(i + 1, i) for...  18 us
    all_to_all x1, blocking collectives, swap(): lax.all_to_all(value, 'ctx', 0, 0, tiled=True, axis_index_groups=groups)  17.4 us
    all_to_all x1, blocking collectives, on_device(): norms = lax.all_to_all(norms, ('tp', 'dp'), 0, 0, tiled=True)  15.5 us
    all_to_all x2, starting transfers between devices, swap(): lax.all_to_all(value, 'ctx', 0, 0, tiled=True, axis_index_groups=groups)  13.3 us
    ppermute x2, starting transfers between devices, shifted(): lax.ppermute(value, 'ctx', [(i, i + by) for i in range(devices) if 0 <= i...  5.28 us
    ppermute x1, starting transfers between devices, on_device(): other = lax.ppermute(gathered, 'dp', [(0, 1), (1, 0)])  4.9 us
    all_to_all x2, waiting for transfers between devices, swap(): lax.all_to_all(value, 'ctx', 0, 0, tiled=True, axis_index_groups=groups)  4.81 us
  transfers between devices with their start and end apart: 10, of which 1 were waited for; matrix products, arithmetic and copies ran while one was open for 0% of the time, Pallas kernels for 21%

profile of v5, /device:TPU:1, one launch (start us, length us, event | category | flops | bytes accessed | tf_op | source)
XLA Modules:
  0.0 119.0 jit_solution(13466940159060266463)
XLA Ops:
  0.6 0.7 pad_add_fusion.place_ref
  1.3 3.5 %gates_0.1 = (bf16[128,1024]{1,0:T(8,128)(2,1)}, bf16[128,1024]{1,0:T(8,128)(2,1)}, bf16[128,1024]{1,0:T(8,128)(2,1)}) custom-call(s32[2]{0:T(128)} %pad_add_fusion.place_ref, bf16[128,2048]{1,0:T(8,128)(2,1)} %bitcast.9, bf16[128,2048]{1,0:T(8,128)(2,1)} %bitcast.11, bf16[128,2048]{1,0:T(8,128)(2,1)} %bitcast.15, bf16[128,2048]{1,0:T(8,128)(2,1)} %bitcast.19, ...), custom_call_target="tpu_custom_call" | custom-call | flops 1000 | bytes 1000 | tf_op jit(solution)/shard_map/gates_0/pallas_call | solution.py:289
  4.9 0.7 collective-permute-start.2
  5.5 8.2 %collective-permute-start.3 = (bf16[128,1024]{1,0:T(8,128)(2,1)}, bf16[128,1024]{1,0:T(8,128)(2,1)S(1)}, u32[]{:S(2)}, u32[]{:S(2)}) collective-permute-start(bf16[128,1024]{1,0:T(8,128)(2,1)} %get-tuple-element.45.sent_b_ref), channel_id=1, source_target_pairs={{0,8},{16,24},{32,40},{48,56},{64,72},{80,88},{96,104},{112,120},{... | collective-permute-start | bytes 786440 | tf_op jit(solution)/shard_map/ppermute | solution.py:264
  13.7 3.5 %gates_1.1 = (bf16[128,1024]{1,0:T(8,128)(2,1)}, bf16[128,1024]{1,0:T(8,128)(2,1)}, bf16[128,1024]{1,0:T(8,128)(2,1)}) custom-call(s32[2]{0:T(128)} %pad_add_fusion.place_ref, bf16[128,2048]{1,0:T(8,128)(2,1)} %bitcast.10, bf16[128,2048]{1,0:T(8,128)(2,1)} %bitcast.12, bf16[128,2048]{1,0:T(8,128)(2,1)} %bitcast.16, bf16[128,2048]{1,0:T(8,128)(2,1)} %bitcast.20, ...), custom_call_target="tpu_custom_call" | custom-call | flops 1000 | bytes 1000 | tf_op jit(solution)/shard_map/gates_1/pallas_call | solution.py:289
  17.2 0.7 collective-permute-start
  17.9 8.5 %collective-permute-start.1 = (bf16[128,1024]{1,0:T(8,128)(2,1)}, bf16[128,1024]{1,0:T(8,128)(2,1)S(1)}, u32[]{:S(2)}, u32[]{:S(2)}) collective-permute-start(bf16[128,1024]{1,0:T(8,128)(2,1)} %get-tuple-element.42.sent_b_ref), channel_id=1, source_target_pairs={{0,8},{16,24},{32,40},{48,56},{64,72},{80,88},{96,104},{112,120},{... | collective-permute-start | bytes 786440 | tf_op jit(solution)/shard_map/ppermute | solution.py:264
  26.4 0.0 collective-permute-done.2.got_a_ref
  26.4 0.0 copy-start.1
  26.4 0.0 collective-permute-done.3.got_b_ref
  26.4 0.0 copy-start.3
  26.5 0.7 copy-done.1
  27.1 0.1 copy-done.3
  27.2 5.6 %sums_0.1 = (bf16[128,2048]{1,0:T(8,128)(2,1)}, bf16[128,2048]{1,0:T(8,128)(2,1)}, bf16[8,2048]{1,0:T(8,128)(2,1)}, bf16[8,2048]{1,0:T(8,128)(2,1)}, bf16[8,144,128]{2,1,0:T(8,128)(2,1)}) custom-call(s32[2]{0:T(128)} %pad_add_fusion.place_ref, bf16[128,1024]{1,0:T(8,128)(2,1)} %get-tuple-element.44.sent_a_ref, ...), custom_call_target="tpu_custom_call" | custom-call | flops 6000000000 | bytes 8000000 | tf_op jit(solution)/shard_map/sums_0/pallas_call | solution.py:289
  32.8 3.7 %collective-permute-start.4 = (bf16[8,144,128]{2,1,0:T(8,128)(2,1)}, bf16[8,144,128]{2,1,0:T(8,128)(2,1)S(1)}, u32[]{:S(2)}, u32[]{:S(2)}) collective-permute-start(bf16[8,144,128]{2,1,0:T(8,128)(2,1)} %get-tuple-element.52), channel_id=1, source_target_pairs={{0,1},{1,0},{2,3},{3,2},{4,5},{5,4},{6,7},{7,6},{8,9},{9,8},{10,11... | collective-permute-start | bytes 884744 | tf_op jit(solution)/shard_map/ppermute | solution.py:357
  36.5 0.0 collective-permute-done.got_a_ref
  36.5 0.0 copy-start.2
  36.6 0.0 collective-permute-done.1.got_b_ref
  36.6 0.0 copy-start.4
  36.6 0.7 copy-done.2
  37.3 0.1 copy-done.4
  37.3 5.6 %sums_1.1 = (bf16[128,2048]{1,0:T(8,128)(2,1)}, bf16[128,2048]{1,0:T(8,128)(2,1)}, bf16[8,2048]{1,0:T(8,128)(2,1)}, bf16[8,2048]{1,0:T(8,128)(2,1)}, f32[8,144,128]{2,1,0:T(8,128)}) custom-call(s32[2]{0:T(128)} %pad_add_fusion.place_ref, ...), custom_call_target="tpu_custom_call", output_to_operand_aliasing={{0}: (15, {}), {1}: (16, {}), {2}: (17, {}), {3}: (18, {})} | custom-call | flops 6000000000 | bytes 8000000 | tf_op jit(solution)/shard_map/sums_1/pallas_call | solution.py:289
  43.0 0.0 collective-permute-done.4
  43.0 1.1 add_convert_fusion
  44.1 17.4 %all_to_all.20.arrived_ref = bf16[8,144,128]{2,1,0:T(8,128)(2,1)S(1)} all-to-all(bf16[8,144,128]{2,1,0:T(8,128)(2,1)S(1)} %add_convert_fusion), channel_id=1, replica_groups={{0,8,16,24,32,40,48,56},{64,72,80,88,96,104,112,120},{128,136,144,152,1..., dimensions={0} | all-to-all | bytes 589824 | tf_op jit(solution)/shard_map/all_to_all | solution.py:367
  61.6 0.8 line.1
  62.3 0.0 copy-start.8
  62.3 0.0 copy-start.7
  62.3 9.9 %all-to-all-start.1 = ((bf16[8,144,128]{2,1,0:T(8,128)(2,1)}), bf16[8,144,128]{2,1,0:T(8,128)(2,1)S(1)}, u32[]{:S(2)}, u32[]{:S(2)}) async-start(bf16[8,144,128]{2,1,0:T(8,128)(2,1)} %line.1), calls=%async_computation.1 | async-start | bytes 589824 | tf_op jit(solution)/shard_map/all_to_all | solution.py:367
  72.2 0.0 copy-done.8
  72.2 1.3 %collective-permute-start.6 = (bf16[8,2048]{1,0:T(8,128)(2,1)S(1)}, bf16[8,2048]{1,0:T(8,128)(2,1)S(1)}, u32[]{:S(2)}, u32[]{:S(2)}) collective-permute-start(bf16[8,2048]{1,0:T(8,128)(2,1)S(1)} %copy-done.8), channel_id=1, source_target_pairs={{8,0},{16,8},{24,16},{32,24},{40,32},{48,40},{56,48},{64,56},{72,6... | collective-permute-start | bytes 98312 | tf_op jit(solution)/shard_map/ppermute | solution.py:269
  73.5 0.0 copy-done.7
  73.6 4.0 %collective-permute-start.5 = (bf16[8,2048]{1,0:T(8,128)(2,1)S(1)}, bf16[8,2048]{1,0:T(8,128)(2,1)S(1)}, u32[]{:S(2)}, u32[]{:S(2)}) collective-permute-start(bf16[8,2048]{1,0:T(8,128)(2,1)S(1)} %copy-done.7), channel_id=1, source_target_pairs={{0,8},{8,16},{16,24},{24,32},{32,40},{40,48},{48,56},{56,64},{64,7... | collective-permute-start | bytes 98312 | tf_op jit(solution)/shard_map/ppermute | solution.py:269
  77.5 4.8 %all-to-all-done.1.arrived_ref = bf16[8,144,128]{2,1,0:T(8,128)(2,1)S(1)} async-done(((bf16[8,144,128]{2,1,0:T(8,128)(2,1)}), bf16[8,144,128]{2,1,0:T(8,128)(2,1)S(1)}, u32[]{:S(2)}, u32[]{:S(2)}) %all-to-all-start.1) | async-done | bytes 294944 | tf_op jit(solution)/shard_map/all_to_all | solution.py:367
  82.4 0.8 piece.1
  83.2 3.4 %all-to-all-start.2 = ((bf16[8,144,128]{2,1,0:T(8,128)(2,1)}), bf16[8,144,128]{2,1,0:T(8,128)(2,1)S(1)}, u32[]{:S(2)}, u32[]{:S(2)}) async-start(bf16[8,144,128]{2,1,0:T(8,128)(2,1)} %piece.1), calls=%async_computation.2 | async-start | bytes 589824 | tf_op jit(solution)/shard_map/all_to_all | solution.py:367
  86.6 0.0 collective-permute-done.6.rim_ref
  86.6 0.0 copy-start.5
  86.6 0.0 collective-permute-done.5.before_ref
  86.7 0.0 copy-start.6
  86.7 0.6 copy-done.5
  87.2 0.0 copy-done.6
  87.3 4.9 %rest_0.1 = (bf16[128,2048]{1,0:T(8,128)(2,1)}, bf16[128,2048]{1,0:T(8,128)(2,1)}) custom-call(s32[2]{0:T(128)} %pad_add_fusion.place_ref, bf16[128,1024]{1,0:T(8,128)(2,1)} %get-tuple-element.44.sent_a_ref, bf16[128,1024]{1,0:T(8,128)(2,1)} %get-tuple-element.45.sent_b_ref, bf16[128,1024]{1,0:T(8,128)(2,1)} %copy-done.1, bf16[128,1024]{1,0:T(8,128)(2,1)} %copy-done.3, ...), custom_call_target="tpu_custom_call" | custom-call | flops 4000000000 | bytes 5000000 | tf_op jit(solution)/shard_map/rest_0/pallas_call | solution.py:289
  92.2 4.9 %rest_1.1 = (bf16[128,2048]{1,0:T(8,128)(2,1)}, bf16[128,2048]{1,0:T(8,128)(2,1)}) custom-call(s32[2]{0:T(128)} %pad_add_fusion.place_ref, bf16[128,1024]{1,0:T(8,128)(2,1)} %get-tuple-element.41.sent_a_ref, bf16[128,1024]{1,0:T(8,128)(2,1)} %get-tuple-element.42.sent_b_ref, ...), custom_call_target="tpu_custom_call", output_to_operand_aliasing={{0}: (16, {}), {1}: (17, {})} | custom-call | flops 4000000000 | bytes 5000000 | tf_op jit(solution)/shard_map/rest_1/pallas_call | solution.py:289
  97.1 0.0 all-to-all-done.2.pieces_ref.mine_ref
  97.1 4.9 %collective-permute-start.7 = (bf16[8,144,128]{2,1,0:T(8,128)(2,1)S(1)}, bf16[8,144,128]{2,1,0:T(8,128)(2,1)S(1)}, u32[]{:S(2)}, u32[]{:S(2)}) collective-permute-start(bf16[8,144,128]{2,1,0:T(8,128)(2,1)S(1)} %all-to-all-done.2.pieces_ref.mine_ref), channel_id=1, source_target_pairs={{0,1},{1,0},{2,3},{3,2},{4,5},{5,4},{6,7},{7,6},{8,9},{9,8},{10,11... | collective-permute-start | bytes 884744 | tf_op jit(solution)/shard_map/ppermute | solution.py:389
  102.0 0.0 copy-start
  102.0 15.5 %all_to_all.21.norms_ref = f32[8,1,128]{2,1,0:T(1,128)S(1)} all-to-all(f32[8,1,128]{2,1,0:T(1,128)S(1)} %norm.1), channel_id=1, replica_groups=mesh['ctx'=64,'tp'=4,'dp'=2] {'tp','dp'}, dimensions={0} | all-to-all | bytes 8192 | tf_op jit(solution)/shard_map/all_to_all | solution.py:388
  117.5 0.0 collective-permute-done.7.other_ref
  117.5 0.0 copy-done
  117.5 1.5 %scale.1 = (bf16[128,2048]{1,0:T(8,128)(2,1)}, bf16[7,2048]{1,0:T(8,128)(2,1)}) custom-call(s32[2]{0:T(128)S(1)} %copy-done, bf16[8,144,128]{2,1,0:T(8,128)(2,1)S(1)} %all-to-all-done.2.pieces_ref.mine_ref, bf16[8,144,128]{2,1,0:T(8,128)(2,1)S(1)} %collective-permute-done.7.other_ref, f32[8,1,128]{2,1,0:T(1,128)S(1)} %all_to_all.21.norms_ref), custom_call_target="tpu_custom_call" | custom-call | tf_op jit(solution)/shard_map/scale/pallas_call | solution.py:396
  (1 shorter events, 0.0 us)
Async XLA Ops:
  4.9 21.6 %collective-permute-start.2 = (bf16[128,1024]{1,0:T(8,128)(2,1)}, bf16[128,1024]{1,0:T(8,128)(2,1)S(1)}, u32[]{:S(2)}, u32[]{:S(2)}) collective-permute-start(bf16[128,1024]{1,0:T(8,128)(2,1)} %get-tuple-element.44.sent_a_ref), channel_id=1, source_target_pairs={{8,16},{24,32},{40,48},{56,64},{72,80},{88,96},{104,112},{120,128}... | collective-permute-start | bytes 786440 | tf_op jit(solution)/shard_map/ppermute | solution.py:264
  5.5 20.9 %collective-permute-start.3 = (bf16[128,1024]{1,0:T(8,128)(2,1)}, bf16[128,1024]{1,0:T(8,128)(2,1)S(1)}, u32[]{:S(2)}, u32[]{:S(2)}) collective-permute-start(bf16[128,1024]{1,0:T(8,128)(2,1)} %get-tuple-element.45.sent_b_ref), channel_id=1, source_target_pairs={{0,8},{16,24},{32,40},{48,56},{64,72},{80,88},{96,104},{112,120},{... | collective-permute-start | bytes 786440 | tf_op jit(solution)/shard_map/ppermute | solution.py:264
  17.2 19.3 %collective-permute-start = (bf16[128,1024]{1,0:T(8,128)(2,1)}, bf16[128,1024]{1,0:T(8,128)(2,1)S(1)}, u32[]{:S(2)}, u32[]{:S(2)}) collective-permute-start(bf16[128,1024]{1,0:T(8,128)(2,1)} %get-tuple-element.41.sent_a_ref), channel_id=1, source_target_pairs={{8,16},{24,32},{40,48},{56,64},{72,80},{88,96},{104,112},{120,128}... | collective-permute-start | bytes 786440 | tf_op jit(solution)/shard_map/ppermute | solution.py:264
  17.9 18.7 %collective-permute-start.1 = (bf16[128,1024]{1,0:T(8,128)(2,1)}, bf16[128,1024]{1,0:T(8,128)(2,1)S(1)}, u32[]{:S(2)}, u32[]{:S(2)}) collective-permute-start(bf16[128,1024]{1,0:T(8,128)(2,1)} %get-tuple-element.42.sent_b_ref), channel_id=1, source_target_pairs={{0,8},{16,24},{32,40},{48,56},{64,72},{80,88},{96,104},{112,120},{... | collective-permute-start | bytes 786440 | tf_op jit(solution)/shard_map/ppermute | solution.py:264
  26.4 0.7 copy-start.1
  26.4 0.8 copy-start.3
  32.8 10.2 %collective-permute-start.4 = (bf16[8,144,128]{2,1,0:T(8,128)(2,1)}, bf16[8,144,128]{2,1,0:T(8,128)(2,1)S(1)}, u32[]{:S(2)}, u32[]{:S(2)}) collective-permute-start(bf16[8,144,128]{2,1,0:T(8,128)(2,1)} %get-tuple-element.52), channel_id=1, source_target_pairs={{0,1},{1,0},{2,3},{3,2},{4,5},{5,4},{6,7},{7,6},{8,9},{9,8},{10,11... | collective-permute-start | bytes 884744 | tf_op jit(solution)/shard_map/ppermute | solution.py:357
  36.5 0.7 copy-start.2
  36.6 0.8 copy-start.4
  62.3 9.9 %copy-start.8 = (bf16[8,2048]{1,0:T(8,128)(2,1)S(1)}, bf16[8,2048]{1,0:T(8,128)(2,1)}, u32[]{:S(2)}) copy-start(bf16[8,2048]{1,0:T(8,128)(2,1)} %get-tuple-element.58) | copy-start | bytes 98308
  62.3 11.2 %copy-start.7 = (bf16[8,2048]{1,0:T(8,128)(2,1)S(1)}, bf16[8,2048]{1,0:T(8,128)(2,1)}, u32[]{:S(2)}) copy-start(bf16[8,2048]{1,0:T(8,128)(2,1)} %get-tuple-element.56.gated_top_ref) | copy-start | bytes 98308
  62.3 20.0 %all-to-all-start.1 = ((bf16[8,144,128]{2,1,0:T(8,128)(2,1)}), bf16[8,144,128]{2,1,0:T(8,128)(2,1)S(1)}, u32[]{:S(2)}, u32[]{:S(2)}) async-start(bf16[8,144,128]{2,1,0:T(8,128)(2,1)} %line.1), calls=%async_computation.1 | async-start | bytes 589824 | tf_op jit(solution)/shard_map/all_to_all | solution.py:367
  72.2 14.4 %collective-permute-start.6 = (bf16[8,2048]{1,0:T(8,128)(2,1)S(1)}, bf16[8,2048]{1,0:T(8,128)(2,1)S(1)}, u32[]{:S(2)}, u32[]{:S(2)}) collective-permute-start(bf16[8,2048]{1,0:T(8,128)(2,1)S(1)} %copy-done.8), channel_id=1, source_target_pairs={{8,0},{16,8},{24,16},{32,24},{40,32},{48,40},{56,48},{64,56},{72,6... | collective-permute-start | bytes 98312 | tf_op jit(solution)/shard_map/ppermute | solution.py:269
  73.6 13.1 %collective-permute-start.5 = (bf16[8,2048]{1,0:T(8,128)(2,1)S(1)}, bf16[8,2048]{1,0:T(8,128)(2,1)S(1)}, u32[]{:S(2)}, u32[]{:S(2)}) collective-permute-start(bf16[8,2048]{1,0:T(8,128)(2,1)S(1)} %copy-done.7), channel_id=1, source_target_pairs={{0,8},{8,16},{16,24},{24,32},{32,40},{40,48},{48,56},{56,64},{64,7... | collective-permute-start | bytes 98312 | tf_op jit(solution)/shard_map/ppermute | solution.py:269
  83.2 13.9 %all-to-all-start.2 = ((bf16[8,144,128]{2,1,0:T(8,128)(2,1)}), bf16[8,144,128]{2,1,0:T(8,128)(2,1)S(1)}, u32[]{:S(2)}, u32[]{:S(2)}) async-start(bf16[8,144,128]{2,1,0:T(8,128)(2,1)} %piece.1), calls=%async_computation.2 | async-start | bytes 589824 | tf_op jit(solution)/shard_map/all_to_all | solution.py:367
  86.6 0.6 copy-start.5
  86.7 0.6 copy-start.6
  97.1 20.4 %collective-permute-start.7 = (bf16[8,144,128]{2,1,0:T(8,128)(2,1)S(1)}, bf16[8,144,128]{2,1,0:T(8,128)(2,1)S(1)}, u32[]{:S(2)}, u32[]{:S(2)}) collective-permute-start(bf16[8,144,128]{2,1,0:T(8,128)(2,1)S(1)} %all-to-all-done.2.pieces_ref.mine_ref), channel_id=1, source_target_pairs={{0,1},{1,0},{2,3},{3,2},{4,5},{5,4},{6,7},{7,6},{8,9},{9,8},{10,11... | collective-permute-start | bytes 884744 | tf_op jit(solution)/shard_map/ppermute | solution.py:389
  102.0 15.5 %copy-start = (s32[2]{0:T(128)S(1)}, s32[2]{0:T(128)}, u32[]{:S(2)}) copy-start(s32[2]{0:T(128)} %pad_add_fusion.place_ref) | copy-start | bytes 28

commit v6 on v4

--- a/solution.py
+++ b/solution.py
@@ -44,23 +44,38 @@
     return jnp.where(core == 0, 1 - slot, slot)
 
 
-def gate_kernel(core_ref, query_ref, key_ref, value_ref, grad_ref, taps_ref, up_ref, down_ref, mixed_ref, wide_ref):
+def by_parity(place_ref, body):
+    @pl.when(place_ref[0] >= 2)
+    def _():
+        body(0, 1)
+
+    @pl.when(place_ref[0] < 2)
+    def _():
+        body(1, 0)
+
+
+def gate_kernel(place_ref, query_ref, key_ref, value_ref, grad_ref, taps_ref, first_ref, second_ref, mixed_ref, wide_ref):
     short_len = taps_ref.shape[0]
     width = wide_ref.shape[1]
-    down_ref[...] = (grad_ref[...].astype(F32) * query_ref[...].astype(F32)).astype(BF)
-    wide_ref[0:8, :] = jnp.zeros((8, width), F32)
-    wide_ref[8:, :] = value_ref[...].astype(F32)
-    total = taps_ref[0:1, :] * wide_ref[8 : 8 + ROWS, :]
-    for lag in range(1, short_len):
-        total = total + taps_ref[lag : lag + 1, :] * wide_ref[8 - lag : 8 - lag + ROWS, :]
-    mixed = total.astype(BF)
-    mixed_ref[...] = mixed
-    gated = key_ref[...].astype(F32) * mixed.astype(F32)
-    row = lax.broadcasted_iota(jnp.int32, (8, width), 0)
-    wide_ref[0:16, :] = gated[0:16]
-    top = jnp.where(row < 2, wide_ref[6:14, :], wide_ref[ROWS : ROWS + 8, :])
-    up_ref[0:16, :] = jnp.concatenate([top, gated[8:16]], axis=0).astype(BF)
-    up_ref[16:ROWS, :] = gated[16:].astype(BF)
+
+    def body(up_at, down_at):
+        up_ref, down_ref = (first_ref, second_ref)[up_at], (first_ref, second_ref)[down_at]
+        down_ref[...] = (grad_ref[...].astype(F32) * query_ref[...].astype(F32)).astype(BF)
+        wide_ref[0:8, :] = jnp.zeros((8, width), F32)
+        wide_ref[8:, :] = value_ref[...].astype(F32)
+        total = taps_ref[0:1, :] * wide_ref[8 : 8 + ROWS, :]
+        for lag in range(1, short_len):
+            total = total + taps_ref[lag : lag + 1, :] * wide_ref[8 - lag : 8 - lag + ROWS, :]
+        mixed = total.astype(BF)
+        mixed_ref[...] = mixed
+        gated = key_ref[...].astype(F32) * mixed.astype(F32)
+        row = lax.broadcasted_iota(jnp.int32, (8, width), 0)
+        wide_ref[0:16, :] = gated[0:16]
+        top = jnp.where(row < 2, wide_ref[6:14, :], wide_ref[ROWS : ROWS + 8, :])
+        up_ref[0:16, :] = jnp.concatenate([top, gated[8:16]], axis=0).astype(BF)
+        up_ref[16:ROWS, :] = gated[16:].astype(BF)
+
+    by_parity(place_ref, body)
 
 
 def own_head(wide_ref, tail, key_ref, value_ref, taps_ref):
@@ -73,6 +88,12 @@
         total = total + taps_ref[lag : lag + 1, :] * wide_ref[8 - lag : 16 - lag, :]
     mixed = total.astype(BF).astype(F32)
     return mixed, (key * mixed).astype(BF).astype(F32)
+
+
+def early_rows(wide_ref, got_top):
+    row = lax.broadcasted_iota(jnp.int32, got_top.shape, 0)
+    wide_ref[8:16, :] = got_top
+    return jnp.where(row < 6, 0.0, wide_ref[2:10, :])
 
 
 def with_heads(own_head_rows, up_ref, got_head_rows, got_ref):
@@ -114,24 +135,34 @@
 
 
 def sums_kernel(
-    core_ref, up_ref, got_ref, down_ref, back_ref, mixed_ref, key_ref, value_ref, short_ref, long_ref,
+    place_ref, sent_a_ref, sent_b_ref, got_a_ref, got_b_ref, mixed_ref, key_ref, value_ref, short_ref, long_ref,
     hi_ref, lo_ref, near_ref, away_ref, inv_ref, *rest,
 ):
-    key_out, mixed_out, gated_top_out, mixed_top_out, part_ref, wide_ref = rest[-6:]
+    sent, arrived = (sent_a_ref, sent_b_ref), (got_a_ref, got_b_ref)
+
+    def body(up_at, down_at):
+        sums_body(
+            sent[up_at], arrived[down_at], sent[down_at], arrived[up_at], mixed_ref, key_ref, value_ref, short_ref, long_ref,
+            hi_ref, lo_ref, near_ref, away_ref, inv_ref, *rest[-6:],
+        )
+
+    by_parity(place_ref, body)
+
+
+def sums_body(
+    up_ref, got_ref, down_ref, back_ref, mixed_ref, key_ref, value_ref, short_ref, long_ref,
+    hi_ref, lo_ref, near_ref, away_ref, inv_ref, key_out, mixed_out, gated_top_out, mixed_top_out, part_ref, wide_ref,
+):
     short_len = short_ref.shape[0]
     width = wide_ref.shape[1]
-    row = lax.broadcasted_iota(jnp.int32, (8, width), 0)
     got_top = got_ref[0:16, :].astype(F32)[0:8]
     mixed_top, gated_top = own_head(wide_ref, got_top, key_ref, value_ref, short_ref)
     gated_top_out[...] = gated_top.astype(BF)
-    wide_ref[8:16, :] = got_top
-    before = jnp.where(row < 6, 0.0, wide_ref[2:10, :])
-    gated = with_heads(gated_top, up_ref, before, got_ref)
+    gated = with_heads(gated_top, up_ref, early_rows(wide_ref, got_top), got_ref)
     mid = down_ref[...]
-    ahead = back_ref[...]
     gated_spec = dot(hi_ref[...], gated) + dot(lo_ref[...], gated)
     mid_spec = dot(near_ref[...], twice(mid))
-    both_spec = mid_spec + dot(away_ref[...], twice(ahead))
+    both_spec = mid_spec + dot(away_ref[...], twice(back_ref[...]))
     taps_spec = dot(near_ref[...], twice(long_ref[...]))
     long_sum = inverse(inv_ref, product(mid_spec, gated_spec, True))
     gated_grad = inverse(inv_ref, product(both_spec, taps_spec, True))
@@ -163,20 +194,53 @@
 
 
 def rest_kernel(
-    core_ref, up_ref, got_ref, gated_top_ref, before_ref, grad_ref, mixed_ref, rim_ref, short_ref, long_ref,
+    place_ref, sent_a_ref, sent_b_ref, got_a_ref, got_b_ref, gated_top_ref, grad_ref, mixed_ref, short_ref, long_ref,
     hi_ref, lo_ref, near_ref, inv_ref, *rest,
 ):
-    query_out, value_out, wide_ref = rest[-3:]
-    gated = with_heads(gated_top_ref[...].astype(F32), up_ref, before_ref[...].astype(F32), got_ref)
-    gated_spec = dot(hi_ref[...], gated) + dot(lo_ref[...], gated)
-    taps_spec = dot(near_ref[...], twice(long_ref[...]))
-    long_out = inverse(inv_ref, product(gated_spec, taps_spec, False))
-    query_out[...] = (grad_ref[...].astype(F32) * long_out).astype(BF)
-    wide_ref[0:ROWS, :] = mixed_ref[...].astype(F32)
-    wide_ref[ROWS:, :] = rim_ref[...].astype(F32)
-    total = short_ref[0:1, :] * wide_ref[0:ROWS, :]
+    query_out, value_out, long_top_out, wide_ref = rest[-4:]
+    sent, arrived = (sent_a_ref, sent_b_ref), (got_a_ref, got_b_ref)
+
+    def body(up_at, down_at):
+        up_ref, got_ref = sent[up_at], arrived[down_at]
+        before = early_rows(wide_ref, got_ref[0:16, :].astype(F32)[0:8])
+        gated = with_heads(gated_top_ref[...].astype(F32), up_ref, before, got_ref)
+        gated_spec = dot(hi_ref[...], gated) + dot(lo_ref[...], gated)
+        taps_spec = dot(near_ref[...], twice(long_ref[...]))
+        long_out = inverse(inv_ref, product(gated_spec, taps_spec, False))
+        long_top_out[...] = long_out[0:8]
+        query_out[...] = (grad_ref[...].astype(F32) * long_out).astype(BF)
+        wide_ref[0:ROWS, :] = mixed_ref[...].astype(F32)
+        wide_ref[ROWS:, :] = jnp.zeros((8, wide_ref.shape[1]), F32)
+        total = short_ref[0:1, :] * wide_ref[0:ROWS, :]
+        for lag in range(1, short_ref.shape[0]):
+            total = total + short_ref[lag : lag + 1, :] * wide_ref[lag : lag + ROWS, :]
+        value_out[...] = total.astype(BF)
+
+    by_parity(place_ref, body)
+
+
+def edge_kernel(
+    before_ref, rim_ref, long_top_ref, grad_ref, taps_ref, mixed_ref, short_ref, query_ref, value_ref,
+    query_out, value_out, wide_ref,
+):
+    width = wide_ref.shape[1]
+    before = before_ref[...].astype(F32)
+    ends = taps_ref[...].astype(F32)
+    lines = []
+    for t in range(5):
+        line = ends[15:16] * before[t + 1 : t + 2]
+        for r in range(t + 2, 6):
+            line = line + ends[16 - r + t : 17 - r + t] * before[r : r + 1]
+        lines.append(line)
+    lines.append(jnp.zeros((3, width), F32))
+    long_out = long_top_ref[...] + jnp.concatenate(lines, axis=0)
+    query = grad_ref[...].astype(F32)[0:8] * long_out
+    query_out[...] = jnp.concatenate([query, query_ref[...].astype(F32)[8:16]], axis=0).astype(BF)
+    wide_ref[0:16, :] = mixed_ref[...].astype(F32)
+    wide_ref[16:, :] = rim_ref[...].astype(F32)
+    total = short_ref[0:1, :] * wide_ref[0:16, :]
     for lag in range(1, short_ref.shape[0]):
-        total = total + short_ref[lag : lag + 1, :] * wide_ref[lag : lag + ROWS, :]
+        total = total + short_ref[lag : lag + 1, :] * wide_ref[lag : lag + 16, :]
     value_out[...] = total.astype(BF)
 
 
@@ -210,7 +274,7 @@
     norm_ref[...] = jnp.broadcast_to(square[None], norm_ref.shape)
 
 
-def scale_kernel(limit, core_ref, mine_ref, other_ref, norms_ref, long_ref, short_ref):
+def scale_kernel(limit, place_ref, mine_ref, other_ref, norms_ref, long_ref, short_ref):
     norm_sq = norms_ref[0]
     for device in range(1, norms_ref.shape[0]):
         norm_sq = norm_sq + norms_ref[device]
@@ -237,6 +301,12 @@
     return pltpu.CompilerParams(vmem_limit_bytes=limit)
 
 
+def swapped(value, phase):
+    devices = lax.axis_size("ctx")
+    starts = range(1 - phase, devices - 1, 2)
+    return lax.ppermute(value, "ctx", [(i, i + 1) for i in starts] + [(i + 1, i) for i in starts])
+
+
 def shifted(value, by):
     devices = lax.axis_size("ctx")
     return lax.ppermute(value, "ctx", [(i, i + by) for i in range(devices) if 0 <= i + by < devices])
@@ -247,12 +317,12 @@
     chan_width = query_rows.shape[1]
     half_width = chan_width // 2
     short_len, long_len = short_taps.shape[0], long_taps.shape[0]
-    core = lax.axis_index("dp").astype(jnp.int32).reshape(1)
+    core = (lax.axis_index("dp") + 2 * (lax.axis_index("ctx") % 2)).astype(jnp.int32).reshape(1)
     devices = lax.axis_size("ctx")
     per_half = half_width // WIDTH
     struct = jax.ShapeDtypeStruct
     def half(slot):
-        return lambda rows: pl.BlockSpec((rows, WIDTH), lambda i, core: (0, half_of(slot, core[0]) * per_half + i))
+        return lambda rows: pl.BlockSpec((rows, WIDTH), lambda i, core: (0, half_of(slot, core[0] % 2) * per_half + i))
 
     def held(rows):
         return pl.BlockSpec((rows, WIDTH), lambda i, core: (0, i))
@@ -279,21 +349,18 @@
     wide = struct((ROWS, chan_width), BF)
     top = struct((8, chan_width), BF)
     own = struct((ROWS, half_width), BF)
-    ups, downs, mixeds, gots, backs = [], [], [], [], []
+    sent, mixeds, got = [], [], []
     for slot in range(2):
         part = half(slot)
-        up, down, mixed = call(
+        first, second, mixed = call(
             gate_kernel, "gates", slot, (query_rows, key_rows, value_rows, grad_rows, short_taps),
             [part(ROWS), part(ROWS), part(ROWS), part(ROWS), part(short_len)], (),
             (own, own, own), [held(ROWS)] * 3, little,
         )
-        ups.append(up)
-        downs.append(down)
+        sent.append((first, second))
         mixeds.append(mixed)
-        gots.append(shifted(up, 1))
-        backs.append(shifted(down, -1))
-
-    ups[0], ups[1], downs[1] = lax.optimization_barrier((ups[0], ups[1], downs[1]))
+        got.append((swapped(first, 0), swapped(second, 1)))
+    sent = lax.optimization_barrier(sent)
 
     fwd_hi, fwd_lo, near, away, inv_both = (jnp.asarray(t) for t in tables())
     table = pl.BlockSpec((256, 256), lambda i, core: (0, 0))
@@ -303,7 +370,7 @@
         return call(
             sums_kernel, "sums", slot,
             (
-                ups[slot], gots[slot], downs[slot], backs[slot], mixeds[slot], key_rows, value_rows, short_taps, long_taps,
+                *sent[slot], *got[slot], mixeds[slot], key_rows, value_rows, short_taps, long_taps,
                 fwd_hi, fwd_lo, near, away, inv_both,
             ),
             [held(ROWS)] * 5 + [part(ROWS), part(ROWS), part(short_len), part(long_len)] + [table] * 5,
@@ -313,20 +380,16 @@
             pl.CostEstimate(flops=6_000_000_000, bytes_accessed=8_000_000, transcendentals=0),
         )
 
-    def run_rest(slot, kept, before, rim):
+    def run_rest(slot, kept):
         part = half(slot)
         return call(
             rest_kernel, "rest", slot,
-            (
-                ups[slot], gots[slot], gated_top, before, grad_rows, mixed_grad, rim, short_taps, long_taps,
-                fwd_hi, fwd_lo, near, inv_both,
-            ),
-            [held(ROWS), held(ROWS), part(8), part(8), part(ROWS), part(ROWS), part(8), part(short_len), part(long_len)]
-            + [table] * 4,
+            (*sent[slot], *got[slot], gated_top, grad_rows, mixed_grad, short_taps, long_taps, fwd_hi, fwd_lo, near, inv_both),
+            [held(ROWS)] * 4 + [part(8), part(ROWS), part(ROWS), part(short_len), part(long_len)] + [table] * 4,
             kept,
-            (wide, wide),
-            [part(ROWS), part(ROWS)],
-            pl.CostEstimate(flops=4_000_000_000, bytes_accessed=5_000_000, transcendentals=0),
+            (wide, wide, struct((8, chan_width), F32)),
+            [part(ROWS), part(ROWS), part(8)],
+            pl.CostEstimate(flops=2_000_000_000, bytes_accessed=4_000_000, transcendentals=0),
         )
 
     *kept, part_sent = run_sums(0, ())
@@ -347,14 +410,35 @@
 
     total = (part_own + part_got.astype(F32)).astype(BF)
     scattered = swap(total, along)
-    scattered, gated_top, mixed_top = lax.optimization_barrier((scattered, gated_top, mixed_top))
+    scattered, gated_top, mixed_top, *grads = lax.optimization_barrier((scattered, gated_top, mixed_top, *run_rest(0, ())))
     before = shifted(gated_top, 1)
     rim = shifted(mixed_top, -1)
     crossed = swap(small_call(line_kernel, "line", lines)(scattered), across)
-    crossed, before, rim = lax.optimization_barrier((crossed, before, rim))
+    crossed, *grads = lax.optimization_barrier((crossed, *run_rest(1, tuple(grads))))
+    query_grad, value_grad, long_top = grads
     gathered = swap(small_call(piece_kernel, "piece", blocks)(crossed), along)
-    grads = run_rest(1, run_rest(0, (), before, rim), before, rim)
-    gathered, query_grad, value_grad = lax.optimization_barrier((gathered, *grads))
+
+    def rows_at(rows, index):
+        return pl.BlockSpec((rows, chan_width), lambda i: (index, 0))
+
+    last = ROWS // 16 - 1
+    query_grad, value_grad = pl.pallas_call(
+        edge_kernel,
+        out_shape=(wide, wide),
+        grid=(1,),
+        in_specs=[
+            rows_at(8, 0), rows_at(8, 0), rows_at(8, 0), rows_at(16, 0), rows_at(16, long_len // 16 - 1), rows_at(16, last),
+            rows_at(short_len, 0), rows_at(16, 0), pl.BlockSpec(memory_space=pl.ANY),
+        ],
+        out_specs=[rows_at(16, 0), rows_at(16, last)],
+        scratch_shapes=[pltpu.VMEM((24, chan_width), F32)],
+        input_output_aliases={7: 0, 8: 1},
+        compiler_params=params(),
+        cost_estimate=pl.CostEstimate(flops=1_000_000, bytes_accessed=500_000, transcendentals=0),
+        name="edge",
+    )(before, rim, long_top, grad_rows, long_taps, mixed_grad, short_taps, query_grad, value_grad)
+    gathered, query_grad, value_grad = lax.optimization_barrier((gathered, query_grad, value_grad))
+
     ways = lax.axis_size("tp")
     norms = pl.pallas_call(
         norm_kernel,
@@ -368,7 +452,7 @@
     whole = pl.BlockSpec((blocks, depth, 128), lambda i, core: (0, 0, 0))
 
     def result(rows):
-        return pl.BlockSpec((rows, half_width), lambda i, core: (0, jnp.where(i == 0, core[0], 1 - core[0])))
+        return pl.BlockSpec((rows, half_width), lambda i, core: (0, jnp.where(i == 0, core[0] % 2, 1 - core[0] % 2)))
 
     long_grad, short_grad = pl.pallas_call(
         functools.partial(scale_kernel, limit),

time: 129 us -> 127 us (0.984)
  blocking collectives: 32.5 us -> 16.9 us
  waiting for transfers between devices: 16.2 us -> 26.3 us
  Pallas kernels: 26.5 us -> 28 us
    ppermute x6 -> x2, starting transfers between devices: 34.6 us -> 11.9 us  [shifted(): lax.ppermute(value, 'ctx', [(i, i + by) for i in range(devices) if 0 <= i...]
    ppermute x0 -> x4, starting transfers between devices: none -> 20.4 us  [swapped(): lax.ppermute(value, 'ctx', [(i, i + 1) for i in starts] + [(i + 1, i) for...]
    all_to_all x1 -> x0, blocking collectives: 15.9 us -> none  [swap(): lax.all_to_all(value, 'ctx', 0, 0, tiled=True, axis_index_groups=groups)]
    all_to_all x2 -> x3, waiting for transfers between devices: 2.24 us -> 9.65 us  [swap(): lax.all_to_all(value, 'ctx', 0, 0, tiled=True, axis_index_groups=groups)]
    ppermute x0 -> x4, waiting for transfers between devices: none -> 4.65 us  [swapped(): lax.ppermute(value, 'ctx', [(i, i + 1) for i in starts] + [(i + 1, i) for...]
    all_to_all x2 -> x3, starting transfers between devices: 10.8 us -> 14.2 us  [swap(): lax.all_to_all(value, 'ctx', 0, 0, tiled=True, axis_index_groups=groups)]
    pallas_call x0 -> x1, Pallas kernels: none -> 2 us  [on_device(): pl.pallas_call(edge_kernel, out_shape=(wide, wide), grid=(1,), in_specs=[...]
    ppermute x6 -> x2, waiting for transfers between devices: 13.9 us -> 12 us  [shifted(): lax.ppermute(value, 'ctx', [(i, i + by) for i in range(devices) if 0 <= i...]
  transfers between devices with their start and end apart: 10 -> 11, of which waited for: 2 -> 4; matrix products, arithmetic and copies ran while one was open for 0% -> 0% of each run, Pallas kernels for 17% -> 18%
where the time goes in v6:
time: 127 us; the launch traced here: 126 us
  starting transfers between devices  50.3 us (40%)
  Pallas kernels  28 us (22%)
  waiting for transfers between devices  26.3 us (21%)
  blocking collectives  16.9 us (13%)
  local copies, waits for them, and re-layouts  2.22 us (2%)
  other arithmetic  1.84 us (1%)
    pallas_call x6, Pallas kernels, call(): pl.pallas_call(kernel, out_shape=out_shape, grid_spec=pltpu.PrefetchScala...  23.4 us
    ppermute x4, starting transfers between devices, swapped(): lax.ppermute(value, 'ctx', [(i, i + 1) for i in starts] + [(i + 1, i) for...  20.4 us
    all_to_all x1, blocking collectives, on_device(): norms = lax.all_to_all(norms, ('tp', 'dp'), 0, 0, tiled=True)  16.9 us
    all_to_all x3, starting transfers between devices, swap(): lax.all_to_all(value, 'ctx', 0, 0, tiled=True, axis_index_groups=groups)  14.2 us
    ppermute x2, waiting for transfers between devices, shifted(): lax.ppermute(value, 'ctx', [(i, i + by) for i in range(devices) if 0 <= i...  12 us
    ppermute x2, starting transfers between devices, shifted(): lax.ppermute(value, 'ctx', [(i, i + by) for i in range(devices) if 0 <= i...  11.9 us
    all_to_all x3, waiting for transfers between devices, swap(): lax.all_to_all(value, 'ctx', 0, 0, tiled=True, axis_index_groups=groups)  9.65 us
    ppermute x4, waiting for transfers between devices, swapped(): lax.ppermute(value, 'ctx', [(i, i + 1) for i in starts] + [(i + 1, i) for...  4.65 us
  transfers between devices with their start and end apart: 11, of which 4 were waited for; matrix products, arithmetic and copies ran while one was open for 0% of the time, Pallas kernels for 18%

profile of v6, /device:TPU:32, one launch (start us, length us, event | category | flops | bytes accessed | tf_op | source)
XLA Modules:
  0.0 126.4 jit_solution(10349272269409674840)
XLA Ops:
  0.6 2.9 %gates_0.1 = (bf16[128,1024]{1,0:T(8,128)(2,1)}, bf16[128,1024]{1,0:T(8,128)(2,1)}, bf16[128,1024]{1,0:T(8,128)(2,1)}) custom-call(s32[1]{0:T(128)} %bitcast.place_ref, bf16[128,2048]{1,0:T(8,128)(2,1)} %bitcast.13, bf16[128,2048]{1,0:T(8,128)(2,1)} %bitcast.15, bf16[128,2048]{1,0:T(8,128)(2,1)} %bitcast.19, bf16[128,2048]{1,0:T(8,128)(2,1)} %bitcast.8, ...), custom_call_target="tpu_custom_call" | custom-call | flops 1000 | bytes 1000 | tf_op jit(solution)/shard_map/gates_0/pallas_call | solution.py:332
  3.5 12.7 %collective-permute-start.2 = (bf16[128,1024]{1,0:T(8,128)(2,1)}, bf16[128,1024]{1,0:T(8,128)(2,1)S(1)}, u32[]{:S(2)}, u32[]{:S(2)}) collective-permute-start(bf16[128,1024]{1,0:T(8,128)(2,1)} %get-tuple-element.55.sent_a_ref), channel_id=1, source_target_pairs={{8,16},{24,32},{40,48},{56,64},{72,80},{88,96},{104,112},{120,128}... | collective-permute-start | bytes 786440 | tf_op jit(solution)/shard_map/ppermute | solution.py:307
  16.2 1.9 %collective-permute-start.3 = (bf16[128,1024]{1,0:T(8,128)(2,1)}, bf16[128,1024]{1,0:T(8,128)(2,1)S(1)}, u32[]{:S(2)}, u32[]{:S(2)}) collective-permute-start(bf16[128,1024]{1,0:T(8,128)(2,1)} %get-tuple-element.56.sent_b_ref), channel_id=1, source_target_pairs={{0,8},{16,24},{32,40},{48,56},{64,72},{80,88},{96,104},{112,120},{... | collective-permute-start | bytes 786440 | tf_op jit(solution)/shard_map/ppermute | solution.py:307
  18.1 2.9 %gates_1.1 = (bf16[128,1024]{1,0:T(8,128)(2,1)}, bf16[128,1024]{1,0:T(8,128)(2,1)}, bf16[128,1024]{1,0:T(8,128)(2,1)}) custom-call(s32[1]{0:T(128)} %bitcast.place_ref, bf16[128,2048]{1,0:T(8,128)(2,1)} %bitcast.14, bf16[128,2048]{1,0:T(8,128)(2,1)} %bitcast.16, bf16[128,2048]{1,0:T(8,128)(2,1)} %bitcast.20, bf16[128,2048]{1,0:T(8,128)(2,1)} %bitcast.9, ...), custom_call_target="tpu_custom_call" | custom-call | flops 1000 | bytes 1000 | tf_op jit(solution)/shard_map/gates_1/pallas_call | solution.py:332
  21.0 3.0 %collective-permute-start = (bf16[128,1024]{1,0:T(8,128)(2,1)}, bf16[128,1024]{1,0:T(8,128)(2,1)S(1)}, u32[]{:S(2)}, u32[]{:S(2)}) collective-permute-start(bf16[128,1024]{1,0:T(8,128)(2,1)} %get-tuple-element.52.sent_a_ref), channel_id=1, source_target_pairs={{8,16},{24,32},{40,48},{56,64},{72,80},{88,96},{104,112},{120,128}... | collective-permute-start | bytes 786440 | tf_op jit(solution)/shard_map/ppermute | solution.py:307
  24.0 2.8 %collective-permute-start.1 = (bf16[128,1024]{1,0:T(8,128)(2,1)}, bf16[128,1024]{1,0:T(8,128)(2,1)S(1)}, u32[]{:S(2)}, u32[]{:S(2)}) collective-permute-start(bf16[128,1024]{1,0:T(8,128)(2,1)} %get-tuple-element.53.sent_b_ref), channel_id=1, source_target_pairs={{0,8},{16,24},{32,40},{48,56},{64,72},{80,88},{96,104},{112,120},{... | collective-permute-start | bytes 786440 | tf_op jit(solution)/shard_map/ppermute | solution.py:307
  26.9 0.0 collective-permute-done.2.got_a_ref
  26.9 0.0 copy-start.4
  26.9 0.0 collective-permute-done.3.got_b_ref
  26.9 0.0 copy-start.5
  26.9 0.7 copy-done.4
  27.6 0.1 copy-done.5
  27.7 4.9 %sums_0.1 = (bf16[128,2048]{1,0:T(8,128)(2,1)}, bf16[128,2048]{1,0:T(8,128)(2,1)}, bf16[8,2048]{1,0:T(8,128)(2,1)}, bf16[8,2048]{1,0:T(8,128)(2,1)}, bf16[8,144,128]{2,1,0:T(8,128)(2,1)}) custom-call(s32[1]{0:T(128)} %bitcast.place_ref, bf16[128,1024]{1,0:T(8,128)(2,1)} %get-tuple-element.55.sent_a_ref, bf16[128,1024]{1,0:T(8,128)(2,1)} %get-tuple-element.56.sent_b_ref, ...), custom_call_target="tpu_custom_call" | custom-call | flops 6000000000 | bytes 8000000 | tf_op jit(solution)/shard_map/sums_0/pallas_call | solution.py:332
  32.5 1.9 %collective-permute-start.4 = (bf16[8,144,128]{2,1,0:T(8,128)(2,1)}, bf16[8,144,128]{2,1,0:T(8,128)(2,1)S(1)}, u32[]{:S(2)}, u32[]{:S(2)}) collective-permute-start(bf16[8,144,128]{2,1,0:T(8,128)(2,1)} %get-tuple-element.63), channel_id=1, source_target_pairs={{0,1},{1,0},{2,3},{3,2},{4,5},{5,4},{6,7},{7,6},{8,9},{9,8},{10,11... | collective-permute-start | bytes 884744 | tf_op jit(solution)/shard_map/ppermute | solution.py:396
  34.4 4.6 %collective-permute-done.got_a_ref = bf16[128,1024]{1,0:T(8,128)(2,1)S(1)} collective-permute-done((bf16[128,1024]{1,0:T(8,128)(2,1)}, bf16[128,1024]{1,0:T(8,128)(2,1)S(1)}, u32[]{:S(2)}, u32[]{:S(2)}) %collective-permute-start) | collective-permute-done | bytes 262176 | tf_op jit(solution)/shard_map/ppermute | solution.py:307
  39.1 0.0 copy-start.2
  39.1 0.0 collective-permute-done.1.got_b_ref
  39.1 0.0 copy-start.3
  39.1 0.7 copy-done.2
  39.8 0.1 copy-done.3
  39.9 4.9 %sums_1.1 = (bf16[128,2048]{1,0:T(8,128)(2,1)}, bf16[128,2048]{1,0:T(8,128)(2,1)}, bf16[8,2048]{1,0:T(8,128)(2,1)}, bf16[8,2048]{1,0:T(8,128)(2,1)}, f32[8,144,128]{2,1,0:T(8,128)}) custom-call(s32[1]{0:T(128)} %bitcast.place_ref, ...), custom_call_target="tpu_custom_call", output_to_operand_aliasing={{0}: (15, {}), {1}: (16, {}), {2}: (17, {}), {3}: (18, {})} | custom-call | flops 6000000000 | bytes 8000000 | tf_op jit(solution)/shard_map/sums_1/pallas_call | solution.py:332
  44.8 0.0 collective-permute-done.4
  44.8 1.8 %add_convert_fusion = bf16[8,144,128]{2,1,0:T(8,128)(2,1)} fusion(f32[8,144,128]{2,1,0:T(8,128)} %get-tuple-element.62, bf16[8,144,128]{2,1,0:T(8,128)(2,1)S(1)} %collective-permute-done.4), kind=kLoop, calls=%fused_computation | loop fusion | flops 442368 | bytes 1179648 | tf_op jit(solution)/shard_map/convert_element_type | solution.py:411
  46.7 3.4 %all-to-all-start = ((bf16[8,144,128]{2,1,0:T(8,128)(2,1)}), bf16[8,144,128]{2,1,0:T(8,128)(2,1)S(1)}, u32[]{:S(2)}, u32[]{:S(2)}) async-start(bf16[8,144,128]{2,1,0:T(8,128)(2,1)} %add_convert_fusion), calls=%async_computation | async-start | bytes 589824 | tf_op jit(solution)/shard_map/all_to_all | solution.py:406
  50.1 4.0 %rest_0.1 = (bf16[128,2048]{1,0:T(8,128)(2,1)}, bf16[128,2048]{1,0:T(8,128)(2,1)}, f32[8,2048]{1,0:T(8,128)}) custom-call(s32[1]{0:T(128)} %bitcast.place_ref, bf16[128,1024]{1,0:T(8,128)(2,1)} %get-tuple-element.55.sent_a_ref, bf16[128,1024]{1,0:T(8,128)(2,1)} %get-tuple-element.56.sent_b_ref, bf16[128,1024]{1,0:T(8,128)(2,1)} %copy-done.4, ...), custom_call_target="tpu_custom_call" | custom-call | flops 2000000000 | bytes 4000000 | tf_op jit(solution)/shard_map/rest_0/pallas_call | solution.py:332
  54.1 7.5 %all-to-all-done.arrived_ref = bf16[8,144,128]{2,1,0:T(8,128)(2,1)S(1)} async-done(((bf16[8,144,128]{2,1,0:T(8,128)(2,1)}), bf16[8,144,128]{2,1,0:T(8,128)(2,1)S(1)}, u32[]{:S(2)}, u32[]{:S(2)}) %all-to-all-start) | async-done | bytes 294944 | tf_op jit(solution)/shard_map/all_to_all | solution.py:406
  61.6 0.8 line.1
  62.4 7.2 %all-to-all-start.1 = ((bf16[8,144,128]{2,1,0:T(8,128)(2,1)}), bf16[8,144,128]{2,1,0:T(8,128)(2,1)S(1)}, u32[]{:S(2)}, u32[]{:S(2)}) async-start(bf16[8,144,128]{2,1,0:T(8,128)(2,1)} %line.1), calls=%async_computation.1 | async-start | bytes 589824 | tf_op jit(solution)/shard_map/all_to_all | solution.py:406
  69.6 4.0 %rest_1.1 = (bf16[128,2048]{1,0:T(8,128)(2,1)}, bf16[128,2048]{1,0:T(8,128)(2,1)}, f32[8,2048]{1,0:T(8,128)}) custom-call(s32[1]{0:T(128)} %bitcast.place_ref, bf16[128,1024]{1,0:T(8,128)(2,1)} %get-tuple-element.52.sent_a_ref, bf16[128,1024]{1,0:T(8,128)(2,1)} %get-tuple-element.53.sent_b_ref, ...), custom_call_target="tpu_custom_call", output_to_operand_aliasing={{0}: (14, {}), {1}: (15, {}), {2}: (16, {})} | custom-call | flops 2000000000 | bytes 4000000 | tf_op jit(solution)/shard_map/rest_1/pallas_call | solution.py:332
  73.5 2.1 %all-to-all-done.1.arrived_ref = bf16[8,144,128]{2,1,0:T(8,128)(2,1)S(1)} async-done(((bf16[8,144,128]{2,1,0:T(8,128)(2,1)}), bf16[8,144,128]{2,1,0:T(8,128)(2,1)S(1)}, u32[]{:S(2)}, u32[]{:S(2)}) %all-to-all-start.1) | async-done | bytes 294944 | tf_op jit(solution)/shard_map/all_to_all | solution.py:406
  75.6 0.9 piece.1
  76.5 0.0 copy-start.7
  76.5 0.0 copy-start.6
  76.5 3.6 %all-to-all-start.2 = ((bf16[8,144,128]{2,1,0:T(8,128)(2,1)}), bf16[8,144,128]{2,1,0:T(8,128)(2,1)S(1)}, u32[]{:S(2)}, u32[]{:S(2)}) async-start(bf16[8,144,128]{2,1,0:T(8,128)(2,1)} %piece.1), calls=%async_computation.2 | async-start | bytes 589824 | tf_op jit(solution)/shard_map/all_to_all | solution.py:406
  80.1 0.0 copy-done.7
  80.1 10.0 %collective-permute-start.6 = (bf16[8,2048]{1,0:T(8,128)(2,1)S(1)}, bf16[8,2048]{1,0:T(8,128)(2,1)S(1)}, u32[]{:S(2)}, u32[]{:S(2)}) collective-permute-start(bf16[8,2048]{1,0:T(8,128)(2,1)S(1)} %copy-done.7), channel_id=1, source_target_pairs={{8,0},{16,8},{24,16},{32,24},{40,32},{48,40},{56,48},{64,56},{72,6... | collective-permute-start | bytes 98312 | tf_op jit(solution)/shard_map/ppermute | solution.py:312
  90.1 0.0 copy-done.6
  90.1 1.9 %collective-permute-start.5 = (bf16[8,2048]{1,0:T(8,128)(2,1)S(1)}, bf16[8,2048]{1,0:T(8,128)(2,1)S(1)}, u32[]{:S(2)}, u32[]{:S(2)}) collective-permute-start(bf16[8,2048]{1,0:T(8,128)(2,1)S(1)} %copy-done.6), channel_id=1, source_target_pairs={{0,8},{8,16},{16,24},{24,32},{32,40},{40,48},{48,56},{56,64},{64,7... | collective-permute-start | bytes 98312 | tf_op jit(solution)/shard_map/ppermute | solution.py:312
  92.0 0.0 collective-permute-done.6.rim_ref
  92.0 0.0 copy-start
  92.0 12.0 %collective-permute-done.5.before_ref = bf16[8,2048]{1,0:T(8,128)(2,1)S(1)} collective-permute-done((bf16[8,2048]{1,0:T(8,128)(2,1)S(1)}, bf16[8,2048]{1,0:T(8,128)(2,1)S(1)}, u32[]{:S(2)}, u32[]{:S(2)}) %collective-permute-start.5) | collective-permute-done | bytes 32800 | tf_op jit(solution)/shard_map/ppermute | solution.py:312
  104.0 0.0 copy-done
  104.0 0.0 copy-start.1
  104.0 0.6 copy-done.1
  104.6 2.0 %edge.1 = (bf16[128,2048]{1,0:T(8,128)(2,1)}, bf16[128,2048]{1,0:T(8,128)(2,1)}) custom-call(bf16[8,2048]{1,0:T(8,128)(2,1)} %copy-done.1, bf16[8,2048]{1,0:T(8,128)(2,1)} %copy-done, f32[8,2048]{1,0:T(8,128)} %get-tuple-element.80.long_top_ref, bf16[128,2048]{1,0:T(8,128)(2,1)} %bitcast.12, ...), custom_call_target="tpu_custom_call", output_to_operand_aliasing={{0}: (7, {}), {1}: (8, {})} | custom-call | flops 1000000 | bytes 500000 | tf_op jit(solution)/shard_map/edge/pallas_call | solution.py:425
  106.6 0.0 all-to-all-done.2.pieces_ref.mine_ref
  106.6 1.9 %collective-permute-start.7 = (bf16[8,144,128]{2,1,0:T(8,128)(2,1)S(1)}, bf16[8,144,128]{2,1,0:T(8,128)(2,1)S(1)}, u32[]{:S(2)}, u32[]{:S(2)}) collective-permute-start(bf16[8,144,128]{2,1,0:T(8,128)(2,1)S(1)} %all-to-all-done.2.pieces_ref.mine_ref), channel_id=1, source_target_pairs={{0,1},{1,0},{2,3},{3,2},{4,5},{5,4},{6,7},{7,6},{8,9},{9,8},{10,11... | collective-permute-start | bytes 884744 | tf_op jit(solution)/shard_map/ppermute | solution.py:450
  108.6 16.9 %all_to_all.20.norms_ref = f32[8,1,128]{2,1,0:T(1,128)S(1)} all-to-all(f32[8,1,128]{2,1,0:T(1,128)S(1)} %norm.1), channel_id=1, replica_groups=mesh['ctx'=64,'tp'=4,'dp'=2] {'tp','dp'}, dimensions={0} | all-to-all | bytes 8192 | tf_op jit(solution)/shard_map/all_to_all | solution.py:449
  125.4 0.0 collective-permute-done.7.other_ref
  125.4 0.9 scale.1
  (1 shorter events, 0.0 us)
Async XLA Ops:
  3.5 23.3 %collective-permute-start.2 = (bf16[128,1024]{1,0:T(8,128)(2,1)}, bf16[128,1024]{1,0:T(8,128)(2,1)S(1)}, u32[]{:S(2)}, u32[]{:S(2)}) collective-permute-start(bf16[128,1024]{1,0:T(8,128)(2,1)} %get-tuple-element.55.sent_a_ref), channel_id=1, source_target_pairs={{8,16},{24,32},{40,48},{56,64},{72,80},{88,96},{104,112},{120,128}... | collective-permute-start | bytes 786440 | tf_op jit(solution)/shard_map/ppermute | solution.py:307
  16.2 10.7 %collective-permute-start.3 = (bf16[128,1024]{1,0:T(8,128)(2,1)}, bf16[128,1024]{1,0:T(8,128)(2,1)S(1)}, u32[]{:S(2)}, u32[]{:S(2)}) collective-permute-start(bf16[128,1024]{1,0:T(8,128)(2,1)} %get-tuple-element.56.sent_b_ref), channel_id=1, source_target_pairs={{0,8},{16,24},{32,40},{48,56},{64,72},{80,88},{96,104},{112,120},{... | collective-permute-start | bytes 786440 | tf_op jit(solution)/shard_map/ppermute | solution.py:307
  21.0 18.1 %collective-permute-start = (bf16[128,1024]{1,0:T(8,128)(2,1)}, bf16[128,1024]{1,0:T(8,128)(2,1)S(1)}, u32[]{:S(2)}, u32[]{:S(2)}) collective-permute-start(bf16[128,1024]{1,0:T(8,128)(2,1)} %get-tuple-element.52.sent_a_ref), channel_id=1, source_target_pairs={{8,16},{24,32},{40,48},{56,64},{72,80},{88,96},{104,112},{120,128}... | collective-permute-start | bytes 786440 | tf_op jit(solution)/shard_map/ppermute | solution.py:307
  24.0 15.1 %collective-permute-start.1 = (bf16[128,1024]{1,0:T(8,128)(2,1)}, bf16[128,1024]{1,0:T(8,128)(2,1)S(1)}, u32[]{:S(2)}, u32[]{:S(2)}) collective-permute-start(bf16[128,1024]{1,0:T(8,128)(2,1)} %get-tuple-element.53.sent_b_ref), channel_id=1, source_target_pairs={{0,8},{16,24},{32,40},{48,56},{64,72},{80,88},{96,104},{112,120},{... | collective-permute-start | bytes 786440 | tf_op jit(solution)/shard_map/ppermute | solution.py:307
  26.9 0.7 copy-start.4
  26.9 0.8 copy-start.5
  32.5 12.3 %collective-permute-start.4 = (bf16[8,144,128]{2,1,0:T(8,128)(2,1)}, bf16[8,144,128]{2,1,0:T(8,128)(2,1)S(1)}, u32[]{:S(2)}, u32[]{:S(2)}) collective-permute-start(bf16[8,144,128]{2,1,0:T(8,128)(2,1)} %get-tuple-element.63), channel_id=1, source_target_pairs={{0,1},{1,0},{2,3},{3,2},{4,5},{5,4},{6,7},{7,6},{8,9},{9,8},{10,11... | collective-permute-start | bytes 884744 | tf_op jit(solution)/shard_map/ppermute | solution.py:396
  39.1 0.7 copy-start.2
  39.1 0.8 copy-start.3
  46.7 14.9 %all-to-all-start = ((bf16[8,144,128]{2,1,0:T(8,128)(2,1)}), bf16[8,144,128]{2,1,0:T(8,128)(2,1)S(1)}, u32[]{:S(2)}, u32[]{:S(2)}) async-start(bf16[8,144,128]{2,1,0:T(8,128)(2,1)} %add_convert_fusion), calls=%async_computation | async-start | bytes 589824 | tf_op jit(solution)/shard_map/all_to_all | solution.py:406
  62.4 13.3 %all-to-all-start.1 = ((bf16[8,144,128]{2,1,0:T(8,128)(2,1)}), bf16[8,144,128]{2,1,0:T(8,128)(2,1)S(1)}, u32[]{:S(2)}, u32[]{:S(2)}) async-start(bf16[8,144,128]{2,1,0:T(8,128)(2,1)} %line.1), calls=%async_computation.1 | async-start | bytes 589824 | tf_op jit(solution)/shard_map/all_to_all | solution.py:406
  76.5 3.6 %copy-start.7 = (bf16[8,2048]{1,0:T(8,128)(2,1)S(1)}, bf16[8,2048]{1,0:T(8,128)(2,1)}, u32[]{:S(2)}) copy-start(bf16[8,2048]{1,0:T(8,128)(2,1)} %get-tuple-element.79) | copy-start | bytes 98308
  76.5 13.6 %copy-start.6 = (bf16[8,2048]{1,0:T(8,128)(2,1)S(1)}, bf16[8,2048]{1,0:T(8,128)(2,1)}, u32[]{:S(2)}) copy-start(bf16[8,2048]{1,0:T(8,128)(2,1)} %get-tuple-element.71.gated_top_ref) | copy-start | bytes 98308
  76.5 30.1 %all-to-all-start.2 = ((bf16[8,144,128]{2,1,0:T(8,128)(2,1)}), bf16[8,144,128]{2,1,0:T(8,128)(2,1)S(1)}, u32[]{:S(2)}, u32[]{:S(2)}) async-start(bf16[8,144,128]{2,1,0:T(8,128)(2,1)} %piece.1), calls=%async_computation.2 | async-start | bytes 589824 | tf_op jit(solution)/shard_map/all_to_all | solution.py:406
  80.1 11.9 %collective-permute-start.6 = (bf16[8,2048]{1,0:T(8,128)(2,1)S(1)}, bf16[8,2048]{1,0:T(8,128)(2,1)S(1)}, u32[]{:S(2)}, u32[]{:S(2)}) collective-permute-start(bf16[8,2048]{1,0:T(8,128)(2,1)S(1)} %copy-done.7), channel_id=1, source_target_pairs={{8,0},{16,8},{24,16},{32,24},{40,32},{48,40},{56,48},{64,56},{72,6... | collective-permute-start | bytes 98312 | tf_op jit(solution)/shard_map/ppermute | solution.py:312
  90.1 13.9 %collective-permute-start.5 = (bf16[8,2048]{1,0:T(8,128)(2,1)S(1)}, bf16[8,2048]{1,0:T(8,128)(2,1)S(1)}, u32[]{:S(2)}, u32[]{:S(2)}) collective-permute-start(bf16[8,2048]{1,0:T(8,128)(2,1)S(1)} %copy-done.6), channel_id=1, source_target_pairs={{0,8},{8,16},{16,24},{24,32},{32,40},{40,48},{48,56},{56,64},{64,7... | collective-permute-start | bytes 98312 | tf_op jit(solution)/shard_map/ppermute | solution.py:312
  92.0 12.0 %copy-start = (bf16[8,2048]{1,0:T(8,128)(2,1)}, bf16[8,2048]{1,0:T(8,128)(2,1)S(1)}, u32[]{:S(2)}) copy-start(bf16[8,2048]{1,0:T(8,128)(2,1)S(1)} %collective-permute-done.6.rim_ref) | copy-start | bytes 98308
  104.0 0.6 copy-start.1
  106.6 18.8 %collective-permute-start.7 = (bf16[8,144,128]{2,1,0:T(8,128)(2,1)S(1)}, bf16[8,144,128]{2,1,0:T(8,128)(2,1)S(1)}, u32[]{:S(2)}, u32[]{:S(2)}) collective-permute-start(bf16[8,144,128]{2,1,0:T(8,128)(2,1)S(1)} %all-to-all-done.2.pieces_ref.mine_ref), channel_id=1, source_target_pairs={{0,1},{1,0},{2,3},{3,2},{4,5},{5,4},{6,7},{7,6},{8,9},{9,8},{10,11... | collective-permute-start | bytes 884744 | tf_op jit(solution)/shard_map/ppermute | solution.py:450

commit v7 on v6

--- a/solution.py
+++ b/solution.py
@@ -138,12 +138,13 @@
     place_ref, sent_a_ref, sent_b_ref, got_a_ref, got_b_ref, mixed_ref, key_ref, value_ref, short_ref, long_ref,
     hi_ref, lo_ref, near_ref, away_ref, inv_ref, *rest,
 ):
+    key_out, mixed_out, *tops, part_ref, wide_ref = rest[-6:]
     sent, arrived = (sent_a_ref, sent_b_ref), (got_a_ref, got_b_ref)
 
     def body(up_at, down_at):
         sums_body(
             sent[up_at], arrived[down_at], sent[down_at], arrived[up_at], mixed_ref, key_ref, value_ref, short_ref, long_ref,
-            hi_ref, lo_ref, near_ref, away_ref, inv_ref, *rest[-6:],
+            hi_ref, lo_ref, near_ref, away_ref, inv_ref, key_out, mixed_out, tops[up_at], tops[down_at], part_ref, wide_ref,
         )
 
     by_parity(place_ref, body)
@@ -194,7 +195,7 @@
 
 
 def rest_kernel(
-    place_ref, sent_a_ref, sent_b_ref, got_a_ref, got_b_ref, gated_top_ref, grad_ref, mixed_ref, short_ref, long_ref,
+    place_ref, sent_a_ref, sent_b_ref, got_a_ref, got_b_ref, top_a_ref, top_b_ref, grad_ref, mixed_ref, short_ref, long_ref,
     hi_ref, lo_ref, near_ref, inv_ref, *rest,
 ):
     query_out, value_out, long_top_out, wide_ref = rest[-4:]
@@ -203,7 +204,8 @@
     def body(up_at, down_at):
         up_ref, got_ref = sent[up_at], arrived[down_at]
         before = early_rows(wide_ref, got_ref[0:16, :].astype(F32)[0:8])
-        gated = with_heads(gated_top_ref[...].astype(F32), up_ref, before, got_ref)
+        gated_top = (top_a_ref, top_b_ref)[up_at][...].astype(F32)
+        gated = with_heads(gated_top, up_ref, before, got_ref)
         gated_spec = dot(hi_ref[...], gated) + dot(lo_ref[...], gated)
         taps_spec = dot(near_ref[...], twice(long_ref[...]))
         long_out = inverse(inv_ref, product(gated_spec, taps_spec, False))
@@ -220,28 +222,32 @@
 
 
 def edge_kernel(
-    before_ref, rim_ref, long_top_ref, grad_ref, taps_ref, mixed_ref, short_ref, query_ref, value_ref,
+    place_ref, got_a_ref, got_b_ref, long_top_ref, grad_ref, taps_ref, mixed_ref, short_ref, query_ref, value_ref,
     query_out, value_out, wide_ref,
 ):
-    width = wide_ref.shape[1]
-    before = before_ref[...].astype(F32)
-    ends = taps_ref[...].astype(F32)
-    lines = []
-    for t in range(5):
-        line = ends[15:16] * before[t + 1 : t + 2]
-        for r in range(t + 2, 6):
-            line = line + ends[16 - r + t : 17 - r + t] * before[r : r + 1]
-        lines.append(line)
-    lines.append(jnp.zeros((3, width), F32))
-    long_out = long_top_ref[...] + jnp.concatenate(lines, axis=0)
-    query = grad_ref[...].astype(F32)[0:8] * long_out
-    query_out[...] = jnp.concatenate([query, query_ref[...].astype(F32)[8:16]], axis=0).astype(BF)
-    wide_ref[0:16, :] = mixed_ref[...].astype(F32)
-    wide_ref[16:, :] = rim_ref[...].astype(F32)
-    total = short_ref[0:1, :] * wide_ref[0:16, :]
-    for lag in range(1, short_ref.shape[0]):
-        total = total + short_ref[lag : lag + 1, :] * wide_ref[lag : lag + 16, :]
-    value_out[...] = total.astype(BF)
+    arrived = (got_a_ref, got_b_ref)
+
+    def body(up_at, down_at):
+        before = arrived[down_at][...].astype(F32)
+        ends = taps_ref[...].astype(F32)
+        lines = []
+        for t in range(5):
+            line = ends[15:16] * before[t + 1 : t + 2]
+            for r in range(t + 2, 6):
+                line = line + ends[16 - r + t : 17 - r + t] * before[r : r + 1]
+            lines.append(line)
+        lines.append(jnp.zeros((3, wide_ref.shape[1]), F32))
+        long_out = long_top_ref[...] + jnp.concatenate(lines, axis=0)
+        query = grad_ref[...].astype(F32)[0:8] * long_out
+        query_out[...] = jnp.concatenate([query, query_ref[...].astype(F32)[8:16]], axis=0).astype(BF)
+        wide_ref[0:16, :] = mixed_ref[...].astype(F32)
+        wide_ref[16:, :] = arrived[up_at][...].astype(F32)
+        total = short_ref[0:1, :] * wide_ref[0:16, :]
+        for lag in range(1, short_ref.shape[0]):
+            total = total + short_ref[lag : lag + 1, :] * wide_ref[lag : lag + 16, :]
+        value_out[...] = total.astype(BF)
+
+    by_parity(place_ref, body)
 
 
 def line_kernel(arrived_ref, spread_ref):
@@ -305,11 +311,6 @@
     devices = lax.axis_size("ctx")
     starts = range(1 - phase, devices - 1, 2)
     return lax.ppermute(value, "ctx", [(i, i + 1) for i in starts] + [(i + 1, i) for i in starts])
-
-
-def shifted(value, by):
-    devices = lax.axis_size("ctx")
-    return lax.ppermute(value, "ctx", [(i, i + by) for i in range(devices) if 0 <= i + by < devices])
 
 
 def on_device(gate_query, gate_key, input_value, out_grad, short_taps, long_taps):
@@ -384,8 +385,8 @@
         part = half(slot)
         return call(
             rest_kernel, "rest", slot,
-            (*sent[slot], *got[slot], gated_top, grad_rows, mixed_grad, short_taps, long_taps, fwd_hi, fwd_lo, near, inv_both),
-            [held(ROWS)] * 4 + [part(8), part(ROWS), part(ROWS), part(short_len), part(long_len)] + [table] * 4,
+            (*sent[slot], *got[slot], *tops, grad_rows, mixed_grad, short_taps, long_taps, fwd_hi, fwd_lo, near, inv_both),
+            [held(ROWS)] * 4 + [part(8), part(8), part(ROWS), part(ROWS), part(short_len), part(long_len)] + [table] * 4,
             kept,
             (wide, wide, struct((8, chan_width), F32)),
             [part(ROWS), part(ROWS), part(8)],
@@ -394,7 +395,7 @@
 
     *kept, part_sent = run_sums(0, ())
     part_got = lax.ppermute(part_sent, "dp", [(0, 1), (1, 0)])
-    key_grad, mixed_grad, gated_top, mixed_top, part_own = run_sums(1, tuple(kept))
+    key_grad, mixed_grad, *tops, part_own = run_sums(1, tuple(kept))
 
     blocks = half_width // 128
     lines = devices // blocks
@@ -410,33 +411,35 @@
 
     total = (part_own + part_got.astype(F32)).astype(BF)
     scattered = swap(total, along)
-    scattered, gated_top, mixed_top, *grads = lax.optimization_barrier((scattered, gated_top, mixed_top, *run_rest(0, ())))
-    before = shifted(gated_top, 1)
-    rim = shifted(mixed_top, -1)
+    got_tops = [swapped(tops[phase], phase) for phase in range(2)]
+    scattered, got_tops, *grads = lax.optimization_barrier((scattered, got_tops, *run_rest(0, ())))
     crossed = swap(small_call(line_kernel, "line", lines)(scattered), across)
     crossed, *grads = lax.optimization_barrier((crossed, *run_rest(1, tuple(grads))))
     query_grad, value_grad, long_top = grads
     gathered = swap(small_call(piece_kernel, "piece", blocks)(crossed), along)
 
     def rows_at(rows, index):
-        return pl.BlockSpec((rows, chan_width), lambda i: (index, 0))
+        return pl.BlockSpec((rows, chan_width), lambda i, core: (index, 0))
 
     last = ROWS // 16 - 1
     query_grad, value_grad = pl.pallas_call(
         edge_kernel,
         out_shape=(wide, wide),
-        grid=(1,),
-        in_specs=[
-            rows_at(8, 0), rows_at(8, 0), rows_at(8, 0), rows_at(16, 0), rows_at(16, long_len // 16 - 1), rows_at(16, last),
-            rows_at(short_len, 0), rows_at(16, 0), pl.BlockSpec(memory_space=pl.ANY),
-        ],
-        out_specs=[rows_at(16, 0), rows_at(16, last)],
-        scratch_shapes=[pltpu.VMEM((24, chan_width), F32)],
-        input_output_aliases={7: 0, 8: 1},
+        grid_spec=pltpu.PrefetchScalarGridSpec(
+            num_scalar_prefetch=1,
+            grid=(1,),
+            in_specs=[
+                rows_at(8, 0), rows_at(8, 0), rows_at(8, 0), rows_at(16, 0), rows_at(16, long_len // 16 - 1), rows_at(16, last),
+                rows_at(short_len, 0), rows_at(16, 0), pl.BlockSpec(memory_space=pl.ANY),
+            ],
+            out_specs=[rows_at(16, 0), rows_at(16, last)],
+            scratch_shapes=[pltpu.VMEM((24, chan_width), F32)],
+        ),
+        input_output_aliases={8: 0, 9: 1},
         compiler_params=params(),
         cost_estimate=pl.CostEstimate(flops=1_000_000, bytes_accessed=500_000, transcendentals=0),
         name="edge",
-    )(before, rim, long_top, grad_rows, long_taps, mixed_grad, short_taps, query_grad, value_grad)
+    )(core, *got_tops, long_top, grad_rows, long_taps, mixed_grad, short_taps, query_grad, value_grad)
     gathered, query_grad, value_grad = lax.optimization_barrier((gathered, query_grad, value_grad))
 
     ways = lax.axis_size("tp")

time: 127 us -> 120 us (0.945)
  the two profiles are of different devices: /device:TPU:32 before, /device:TPU:1 now
where the time goes in v7:
time: 120 us; the launch traced here: 119 us
  starting transfers between devices  54.5 us (45%)
  Pallas kernels  28 us (23%)
  waiting for transfers between devices  16.3 us (14%)
  blocking collectives  16.2 us (14%)
  other arithmetic  1.84 us (2%)
  local copies, waits for them, and re-layouts  1.59 us (1%)
    ppermute x6, starting transfers between devices, swapped(): lax.ppermute(value, 'ctx', [(i, i + 1) for i in starts] + [(i + 1, i) for...  24.5 us
    pallas_call x6, Pallas kernels, call(): pl.pallas_call(kernel, out_shape=out_shape, grid_spec=pltpu.PrefetchScala...  23.4 us
    all_to_all x3, starting transfers between devices, swap(): lax.all_to_all(value, 'ctx', 0, 0, tiled=True, axis_index_groups=groups)  20.6 us
    all_to_all x3, waiting for transfers between devices, swap(): lax.all_to_all(value, 'ctx', 0, 0, tiled=True, axis_index_groups=groups)  16.3 us
    all_to_all x1, blocking collectives, on_device(): norms = lax.all_to_all(norms, ('tp', 'dp'), 0, 0, tiled=True)  16.2 us
    ppermute x1, starting transfers between devices, on_device(): other = lax.ppermute(gathered, 'dp', [(0, 1), (1, 0)])  5.71 us
    ppermute x1, starting transfers between devices, on_device(): part_got = lax.ppermute(part_sent, 'dp', [(0, 1), (1, 0)])  3.7 us
  transfers between devices with their start and end apart: 11, of which 3 were waited for; matrix products, arithmetic and copies ran while one was open for 0% of the time, Pallas kernels for 19%

profile of v7, /device:TPU:1, one launch (start us, length us, event | category | flops | bytes accessed | tf_op | source)
XLA Modules:
  0.0 119.2 jit_solution(1961264627644401087)
XLA Ops:
  0.6 2.9 %gates_0.1 = (bf16[128,1024]{1,0:T(8,128)(2,1)}, bf16[128,1024]{1,0:T(8,128)(2,1)}, bf16[128,1024]{1,0:T(8,128)(2,1)}) custom-call(s32[1]{0:T(128)} %bitcast.place_ref, bf16[128,2048]{1,0:T(8,128)(2,1)} %bitcast.13, bf16[128,2048]{1,0:T(8,128)(2,1)} %bitcast.15, bf16[128,2048]{1,0:T(8,128)(2,1)} %bitcast.19, bf16[128,2048]{1,0:T(8,128)(2,1)} %bitcast.8, ...), custom_call_target="tpu_custom_call" | custom-call | flops 1000 | bytes 1000 | tf_op jit(solution)/shard_map/gates_0/pallas_call | solution.py:333
  3.5 0.7 collective-permute-start.2
  4.2 8.2 %collective-permute-start.3 = (bf16[128,1024]{1,0:T(8,128)(2,1)}, bf16[128,1024]{1,0:T(8,128)(2,1)S(1)}, u32[]{:S(2)}, u32[]{:S(2)}) collective-permute-start(bf16[128,1024]{1,0:T(8,128)(2,1)} %get-tuple-element.56.sent_b_ref), channel_id=1, source_target_pairs={{0,8},{16,24},{32,40},{48,56},{64,72},{80,88},{96,104},{112,120},{... | collective-permute-start | bytes 786440 | tf_op jit(solution)/shard_map/ppermute | solution.py:313
  12.4 2.9 %gates_1.1 = (bf16[128,1024]{1,0:T(8,128)(2,1)}, bf16[128,1024]{1,0:T(8,128)(2,1)}, bf16[128,1024]{1,0:T(8,128)(2,1)}) custom-call(s32[1]{0:T(128)} %bitcast.place_ref, bf16[128,2048]{1,0:T(8,128)(2,1)} %bitcast.14, bf16[128,2048]{1,0:T(8,128)(2,1)} %bitcast.16, bf16[128,2048]{1,0:T(8,128)(2,1)} %bitcast.20, bf16[128,2048]{1,0:T(8,128)(2,1)} %bitcast.9, ...), custom_call_target="tpu_custom_call" | custom-call | flops 1000 | bytes 1000 | tf_op jit(solution)/shard_map/gates_1/pallas_call | solution.py:333
  15.2 0.7 collective-permute-start
  15.9 8.5 %collective-permute-start.1 = (bf16[128,1024]{1,0:T(8,128)(2,1)}, bf16[128,1024]{1,0:T(8,128)(2,1)S(1)}, u32[]{:S(2)}, u32[]{:S(2)}) collective-permute-start(bf16[128,1024]{1,0:T(8,128)(2,1)} %get-tuple-element.53.sent_b_ref), channel_id=1, source_target_pairs={{0,8},{16,24},{32,40},{48,56},{64,72},{80,88},{96,104},{112,120},{... | collective-permute-start | bytes 786440 | tf_op jit(solution)/shard_map/ppermute | solution.py:313
  24.4 0.0 collective-permute-done.2.got_a_ref
  24.4 0.0 copy-start.4
  24.4 0.0 collective-permute-done.3.got_b_ref
  24.5 0.0 copy-start.5
  24.5 0.7 copy-done.4
  25.2 0.1 copy-done.5
  25.2 4.8 %sums_0.1 = (bf16[128,2048]{1,0:T(8,128)(2,1)}, bf16[128,2048]{1,0:T(8,128)(2,1)}, bf16[8,2048]{1,0:T(8,128)(2,1)}, bf16[8,2048]{1,0:T(8,128)(2,1)}, bf16[8,144,128]{2,1,0:T(8,128)(2,1)}) custom-call(s32[1]{0:T(128)} %bitcast.place_ref, bf16[128,1024]{1,0:T(8,128)(2,1)} %get-tuple-element.55.sent_a_ref, bf16[128,1024]{1,0:T(8,128)(2,1)} %get-tuple-element.56.sent_b_ref, ...), custom_call_target="tpu_custom_call" | custom-call | flops 6000000000 | bytes 8000000 | tf_op jit(solution)/shard_map/sums_0/pallas_call | solution.py:333
  30.1 3.7 %collective-permute-start.4 = (bf16[8,144,128]{2,1,0:T(8,128)(2,1)}, bf16[8,144,128]{2,1,0:T(8,128)(2,1)S(1)}, u32[]{:S(2)}, u32[]{:S(2)}) collective-permute-start(bf16[8,144,128]{2,1,0:T(8,128)(2,1)} %get-tuple-element.63), channel_id=1, source_target_pairs={{0,1},{1,0},{2,3},{3,2},{4,5},{5,4},{6,7},{7,6},{8,9},{9,8},{10,11... | collective-permute-start | bytes 884744 | tf_op jit(solution)/shard_map/ppermute | solution.py:397
  33.8 0.0 collective-permute-done.got_a_ref
  33.8 0.0 copy-start.2
  33.8 0.0 collective-permute-done.1.got_b_ref
  33.8 0.0 copy-start.3
  33.8 0.7 copy-done.2
  34.5 0.1 copy-done.3
  34.6 4.9 %sums_1.1 = (bf16[128,2048]{1,0:T(8,128)(2,1)}, bf16[128,2048]{1,0:T(8,128)(2,1)}, bf16[8,2048]{1,0:T(8,128)(2,1)}, bf16[8,2048]{1,0:T(8,128)(2,1)}, f32[8,144,128]{2,1,0:T(8,128)}) custom-call(s32[1]{0:T(128)} %bitcast.place_ref, ...), custom_call_target="tpu_custom_call", output_to_operand_aliasing={{0}: (15, {}), {1}: (16, {}), {2}: (17, {}), {3}: (18, {})} | custom-call | flops 6000000000 | bytes 8000000 | tf_op jit(solution)/shard_map/sums_1/pallas_call | solution.py:333
  39.5 0.0 collective-permute-done.4
  39.5 1.8 %add_convert_fusion = bf16[8,144,128]{2,1,0:T(8,128)(2,1)} fusion(f32[8,144,128]{2,1,0:T(8,128)} %get-tuple-element.62, bf16[8,144,128]{2,1,0:T(8,128)(2,1)S(1)} %collective-permute-done.4), kind=kLoop, calls=%fused_computation | loop fusion | flops 442368 | bytes 1179648 | tf_op jit(solution)/shard_map/convert_element_type | solution.py:412
  41.4 0.0 copy-start.6
  41.4 0.0 copy-start.7
  41.4 5.1 %all-to-all-start = ((bf16[8,144,128]{2,1,0:T(8,128)(2,1)}), bf16[8,144,128]{2,1,0:T(8,128)(2,1)S(1)}, u32[]{:S(2)}, u32[]{:S(2)}) async-start(bf16[8,144,128]{2,1,0:T(8,128)(2,1)} %add_convert_fusion), calls=%async_computation | async-start | bytes 589824 | tf_op jit(solution)/shard_map/all_to_all | solution.py:407
  46.5 0.0 copy-done.6
  46.5 0.7 collective-permute-start.5
  47.2 0.0 copy-done.7
  47.2 5.8 %collective-permute-start.6 = (bf16[8,2048]{1,0:T(8,128)(2,1)S(1)}, bf16[8,2048]{1,0:T(8,128)(2,1)S(1)}, u32[]{:S(2)}, u32[]{:S(2)}) collective-permute-start(bf16[8,2048]{1,0:T(8,128)(2,1)S(1)} %copy-done.7), channel_id=1, source_target_pairs={{0,8},{16,24},{32,40},{48,56},{64,72},{80,88},{96,104},{112,120},{... | collective-permute-start | bytes 98312 | tf_op jit(solution)/shard_map/ppermute | solution.py:313
  53.0 4.0 %rest_0.1 = (bf16[128,2048]{1,0:T(8,128)(2,1)}, bf16[128,2048]{1,0:T(8,128)(2,1)}, f32[8,2048]{1,0:T(8,128)}) custom-call(s32[1]{0:T(128)} %bitcast.place_ref, bf16[128,1024]{1,0:T(8,128)(2,1)} %get-tuple-element.55.sent_a_ref, bf16[128,1024]{1,0:T(8,128)(2,1)} %get-tuple-element.56.sent_b_ref, bf16[128,1024]{1,0:T(8,128)(2,1)} %copy-done.4, ...), custom_call_target="tpu_custom_call" | custom-call | flops 2000000000 | bytes 4000000 | tf_op jit(solution)/shard_map/rest_0/pallas_call | solution.py:333
  57.0 0.0 collective-permute-done.5.got_a_ref
  57.0 0.0 copy-start
  57.0 0.0 collective-permute-done.6.got_b_ref
  57.0 0.0 copy-start.1
  57.0 2.5 %all-to-all-done.arrived_ref = bf16[8,144,128]{2,1,0:T(8,128)(2,1)S(1)} async-done(((bf16[8,144,128]{2,1,0:T(8,128)(2,1)}), bf16[8,144,128]{2,1,0:T(8,128)(2,1)S(1)}, u32[]{:S(2)}, u32[]{:S(2)}) %all-to-all-start) | async-done | bytes 294944 | tf_op jit(solution)/shard_map/all_to_all | solution.py:407
  59.6 0.8 line.1
  60.3 0.0 copy-done
  60.3 0.0 copy-done.1
  60.3 12.0 %all-to-all-start.1 = ((bf16[8,144,128]{2,1,0:T(8,128)(2,1)}), bf16[8,144,128]{2,1,0:T(8,128)(2,1)S(1)}, u32[]{:S(2)}, u32[]{:S(2)}) async-start(bf16[8,144,128]{2,1,0:T(8,128)(2,1)} %line.1), calls=%async_computation.1 | async-start | bytes 589824 | tf_op jit(solution)/shard_map/all_to_all | solution.py:407
  72.4 4.0 %rest_1.1 = (bf16[128,2048]{1,0:T(8,128)(2,1)}, bf16[128,2048]{1,0:T(8,128)(2,1)}, f32[8,2048]{1,0:T(8,128)}) custom-call(s32[1]{0:T(128)} %bitcast.place_ref, bf16[128,1024]{1,0:T(8,128)(2,1)} %get-tuple-element.52.sent_a_ref, bf16[128,1024]{1,0:T(8,128)(2,1)} %get-tuple-element.53.sent_b_ref, ...), custom_call_target="tpu_custom_call", output_to_operand_aliasing={{0}: (15, {}), {1}: (16, {}), {2}: (17, {})} | custom-call | flops 2000000000 | bytes 4000000 | tf_op jit(solution)/shard_map/rest_1/pallas_call | solution.py:333
  76.4 6.1 %all-to-all-done.1.arrived_ref = bf16[8,144,128]{2,1,0:T(8,128)(2,1)S(1)} async-done(((bf16[8,144,128]{2,1,0:T(8,128)(2,1)}), bf16[8,144,128]{2,1,0:T(8,128)(2,1)S(1)}, u32[]{:S(2)}, u32[]{:S(2)}) %all-to-all-start.1) | async-done | bytes 294944 | tf_op jit(solution)/shard_map/all_to_all | solution.py:407
  82.5 0.9 piece.1
  83.4 3.4 %all-to-all-start.2 = ((bf16[8,144,128]{2,1,0:T(8,128)(2,1)}), bf16[8,144,128]{2,1,0:T(8,128)(2,1)S(1)}, u32[]{:S(2)}, u32[]{:S(2)}) async-start(bf16[8,144,128]{2,1,0:T(8,128)(2,1)} %piece.1), calls=%async_computation.2 | async-start | bytes 589824 | tf_op jit(solution)/shard_map/all_to_all | solution.py:407
  86.8 2.0 %edge.1 = (bf16[128,2048]{1,0:T(8,128)(2,1)}, bf16[128,2048]{1,0:T(8,128)(2,1)}) custom-call(s32[1]{0:T(128)} %bitcast.place_ref, bf16[8,2048]{1,0:T(8,128)(2,1)} %copy-done, bf16[8,2048]{1,0:T(8,128)(2,1)} %copy-done.1, f32[8,2048]{1,0:T(8,128)} %get-tuple-element.80.long_top_ref, ...), custom_call_target="tpu_custom_call", output_to_operand_aliasing={{0}: (8, {}), {1}: (9, {})} | custom-call | flops 1000000 | bytes 500000 | tf_op jit(solution)/shard_map/edge/pallas_call | solution.py:425
  88.8 7.6 %all-to-all-done.2.pieces_ref.mine_ref = bf16[8,144,128]{2,1,0:T(8,128)(2,1)S(1)} async-done(((bf16[8,144,128]{2,1,0:T(8,128)(2,1)}), bf16[8,144,128]{2,1,0:T(8,128)(2,1)S(1)}, u32[]{:S(2)}, u32[]{:S(2)}) %all-to-all-start.2) | async-done | bytes 294944 | tf_op jit(solution)/shard_map/all_to_all | solution.py:407
  96.4 5.7 %collective-permute-start.7 = (bf16[8,144,128]{2,1,0:T(8,128)(2,1)S(1)}, bf16[8,144,128]{2,1,0:T(8,128)(2,1)S(1)}, u32[]{:S(2)}, u32[]{:S(2)}) collective-permute-start(bf16[8,144,128]{2,1,0:T(8,128)(2,1)S(1)} %all-to-all-done.2.pieces_ref.mine_ref), channel_id=1, source_target_pairs={{0,1},{1,0},{2,3},{3,2},{4,5},{5,4},{6,7},{7,6},{8,9},{9,8},{10,11... | collective-permute-start | bytes 884744 | tf_op jit(solution)/shard_map/ppermute | solution.py:453
  102.2 16.2 %all_to_all.20.norms_ref = f32[8,1,128]{2,1,0:T(1,128)S(1)} all-to-all(f32[8,1,128]{2,1,0:T(1,128)S(1)} %norm.1), channel_id=1, replica_groups=mesh['ctx'=64,'tp'=4,'dp'=2] {'tp','dp'}, dimensions={0} | all-to-all | bytes 8192 | tf_op jit(solution)/shard_map/all_to_all | solution.py:452
  118.3 0.0 collective-permute-done.7.other_ref
  118.3 0.9 scale.1
  (1 shorter events, 0.0 us)
Async XLA Ops:
  3.5 20.9 %collective-permute-start.2 = (bf16[128,1024]{1,0:T(8,128)(2,1)}, bf16[128,1024]{1,0:T(8,128)(2,1)S(1)}, u32[]{:S(2)}, u32[]{:S(2)}) collective-permute-start(bf16[128,1024]{1,0:T(8,128)(2,1)} %get-tuple-element.55.sent_a_ref), channel_id=1, source_target_pairs={{8,16},{24,32},{40,48},{56,64},{72,80},{88,96},{104,112},{120,128}... | collective-permute-start | bytes 786440 | tf_op jit(solution)/shard_map/ppermute | solution.py:313
  4.2 20.3 %collective-permute-start.3 = (bf16[128,1024]{1,0:T(8,128)(2,1)}, bf16[128,1024]{1,0:T(8,128)(2,1)S(1)}, u32[]{:S(2)}, u32[]{:S(2)}) collective-permute-start(bf16[128,1024]{1,0:T(8,128)(2,1)} %get-tuple-element.56.sent_b_ref), channel_id=1, source_target_pairs={{0,8},{16,24},{32,40},{48,56},{64,72},{80,88},{96,104},{112,120},{... | collective-permute-start | bytes 786440 | tf_op jit(solution)/shard_map/ppermute | solution.py:313
  15.2 18.6 %collective-permute-start = (bf16[128,1024]{1,0:T(8,128)(2,1)}, bf16[128,1024]{1,0:T(8,128)(2,1)S(1)}, u32[]{:S(2)}, u32[]{:S(2)}) collective-permute-start(bf16[128,1024]{1,0:T(8,128)(2,1)} %get-tuple-element.52.sent_a_ref), channel_id=1, source_target_pairs={{8,16},{24,32},{40,48},{56,64},{72,80},{88,96},{104,112},{120,128}... | collective-permute-start | bytes 786440 | tf_op jit(solution)/shard_map/ppermute | solution.py:313
  15.9 17.9 %collective-permute-start.1 = (bf16[128,1024]{1,0:T(8,128)(2,1)}, bf16[128,1024]{1,0:T(8,128)(2,1)S(1)}, u32[]{:S(2)}, u32[]{:S(2)}) collective-permute-start(bf16[128,1024]{1,0:T(8,128)(2,1)} %get-tuple-element.53.sent_b_ref), channel_id=1, source_target_pairs={{0,8},{16,24},{32,40},{48,56},{64,72},{80,88},{96,104},{112,120},{... | collective-permute-start | bytes 786440 | tf_op jit(solution)/shard_map/ppermute | solution.py:313
  24.4 0.7 copy-start.4
  24.5 0.8 copy-start.5
  30.1 9.5 %collective-permute-start.4 = (bf16[8,144,128]{2,1,0:T(8,128)(2,1)}, bf16[8,144,128]{2,1,0:T(8,128)(2,1)S(1)}, u32[]{:S(2)}, u32[]{:S(2)}) collective-permute-start(bf16[8,144,128]{2,1,0:T(8,128)(2,1)} %get-tuple-element.63), channel_id=1, source_target_pairs={{0,1},{1,0},{2,3},{3,2},{4,5},{5,4},{6,7},{7,6},{8,9},{9,8},{10,11... | collective-permute-start | bytes 884744 | tf_op jit(solution)/shard_map/ppermute | solution.py:397
  33.8 0.7 copy-start.2
  33.8 0.8 copy-start.3
  41.4 5.1 %copy-start.6 = (bf16[8,2048]{1,0:T(8,128)(2,1)S(1)}, bf16[8,2048]{1,0:T(8,128)(2,1)}, u32[]{:S(2)}) copy-start(bf16[8,2048]{1,0:T(8,128)(2,1)} %get-tuple-element.64.top_a_ref) | copy-start | bytes 98308
  41.4 5.8 %copy-start.7 = (bf16[8,2048]{1,0:T(8,128)(2,1)S(1)}, bf16[8,2048]{1,0:T(8,128)(2,1)}, u32[]{:S(2)}) copy-start(bf16[8,2048]{1,0:T(8,128)(2,1)} %get-tuple-element.65.top_b_ref) | copy-start | bytes 98308
  41.4 18.2 %all-to-all-start = ((bf16[8,144,128]{2,1,0:T(8,128)(2,1)}), bf16[8,144,128]{2,1,0:T(8,128)(2,1)S(1)}, u32[]{:S(2)}, u32[]{:S(2)}) async-start(bf16[8,144,128]{2,1,0:T(8,128)(2,1)} %add_convert_fusion), calls=%async_computation | async-start | bytes 589824 | tf_op jit(solution)/shard_map/all_to_all | solution.py:407
  46.5 10.5 %collective-permute-start.5 = (bf16[8,2048]{1,0:T(8,128)(2,1)S(1)}, bf16[8,2048]{1,0:T(8,128)(2,1)S(1)}, u32[]{:S(2)}, u32[]{:S(2)}) collective-permute-start(bf16[8,2048]{1,0:T(8,128)(2,1)S(1)} %copy-done.6), channel_id=1, source_target_pairs={{8,16},{24,32},{40,48},{56,64},{72,80},{88,96},{104,112},{120,128}... | collective-permute-start | bytes 98312 | tf_op jit(solution)/shard_map/ppermute | solution.py:313
  47.2 9.8 %collective-permute-start.6 = (bf16[8,2048]{1,0:T(8,128)(2,1)S(1)}, bf16[8,2048]{1,0:T(8,128)(2,1)S(1)}, u32[]{:S(2)}, u32[]{:S(2)}) collective-permute-start(bf16[8,2048]{1,0:T(8,128)(2,1)S(1)} %copy-done.7), channel_id=1, source_target_pairs={{0,8},{16,24},{32,40},{48,56},{64,72},{80,88},{96,104},{112,120},{... | collective-permute-start | bytes 98312 | tf_op jit(solution)/shard_map/ppermute | solution.py:313
  57.0 3.3 %copy-start = (bf16[8,2048]{1,0:T(8,128)(2,1)}, bf16[8,2048]{1,0:T(8,128)(2,1)S(1)}, u32[]{:S(2)}) copy-start(bf16[8,2048]{1,0:T(8,128)(2,1)S(1)} %collective-permute-done.5.got_a_ref) | copy-start | bytes 98308
  57.0 3.3 %copy-start.1 = (bf16[8,2048]{1,0:T(8,128)(2,1)}, bf16[8,2048]{1,0:T(8,128)(2,1)S(1)}, u32[]{:S(2)}) copy-start(bf16[8,2048]{1,0:T(8,128)(2,1)S(1)} %collective-permute-done.6.got_b_ref) | copy-start | bytes 98308
  60.3 22.2 %all-to-all-start.1 = ((bf16[8,144,128]{2,1,0:T(8,128)(2,1)}), bf16[8,144,128]{2,1,0:T(8,128)(2,1)S(1)}, u32[]{:S(2)}, u32[]{:S(2)}) async-start(bf16[8,144,128]{2,1,0:T(8,128)(2,1)} %line.1), calls=%async_computation.1 | async-start | bytes 589824 | tf_op jit(solution)/shard_map/all_to_all | solution.py:407
  83.4 13.1 %all-to-all-start.2 = ((bf16[8,144,128]{2,1,0:T(8,128)(2,1)}), bf16[8,144,128]{2,1,0:T(8,128)(2,1)S(1)}, u32[]{:S(2)}, u32[]{:S(2)}) async-start(bf16[8,144,128]{2,1,0:T(8,128)(2,1)} %piece.1), calls=%async_computation.2 | async-start | bytes 589824 | tf_op jit(solution)/shard_map/all_to_all | solution.py:407
  96.4 21.9 %collective-permute-start.7 = (bf16[8,144,128]{2,1,0:T(8,128)(2,1)S(1)}, bf16[8,144,128]{2,1,0:T(8,128)(2,1)S(1)}, u32[]{:S(2)}, u32[]{:S(2)}) collective-permute-start(bf16[8,144,128]{2,1,0:T(8,128)(2,1)S(1)} %all-to-all-done.2.pieces_ref.mine_ref), channel_id=1, source_target_pairs={{0,1},{1,0},{2,3},{3,2},{4,5},{5,4},{6,7},{7,6},{8,9},{9,8},{10,11... | collective-permute-start | bytes 884744 | tf_op jit(solution)/shard_map/ppermute | solution.py:453

commit v8 on v7

--- a/solution.py
+++ b/solution.py
@@ -376,7 +376,7 @@
             ),
             [held(ROWS)] * 5 + [part(ROWS), part(ROWS), part(short_len), part(long_len)] + [table] * 5,
             kept,
-            (wide, wide, top, top, struct((half_width // 128, ROWS + 16, 128), BF if slot == 0 else F32)),
+            (wide, wide, top, top, struct((half_width // 128, ROWS + 16, 128), BF)),
             [part(ROWS), part(ROWS), part(8), part(8), pl.BlockSpec((WIDTH // 128, ROWS + 16, 128), lambda i, core: (i, 0, 0))],
             pl.CostEstimate(flops=6_000_000_000, bytes_accessed=8_000_000, transcendentals=0),
         )
@@ -409,14 +409,15 @@
     def small_call(kernel, name, count):
         return pl.pallas_call(kernel, out_shape=struct((count, depth, 128), BF), compiler_params=params(SMALL), name=name)
 
-    total = (part_own + part_got.astype(F32)).astype(BF)
+    total = (part_own.astype(F32) + part_got.astype(F32)).astype(BF)
     scattered = swap(total, along)
     got_tops = [swapped(tops[phase], phase) for phase in range(2)]
-    scattered, got_tops, *grads = lax.optimization_barrier((scattered, got_tops, *run_rest(0, ())))
+    scattered, got_tops, sent = lax.optimization_barrier((scattered, got_tops, sent))
     crossed = swap(small_call(line_kernel, "line", lines)(scattered), across)
-    crossed, *grads = lax.optimization_barrier((crossed, *run_rest(1, tuple(grads))))
-    query_grad, value_grad, long_top = grads
+    crossed, *grads = lax.optimization_barrier((crossed, *run_rest(0, ())))
+    query_grad, value_grad, long_top = run_rest(1, tuple(grads))
     gathered = swap(small_call(piece_kernel, "piece", blocks)(crossed), along)
+    gathered, query_grad, value_grad, long_top = lax.optimization_barrier((gathered, query_grad, value_grad, long_top))
 
     def rows_at(rows, index):
         return pl.BlockSpec((rows, chan_width), lambda i, core: (index, 0))
@@ -437,11 +438,9 @@
         ),
         input_output_aliases={8: 0, 9: 1},
         compiler_params=params(),
-        cost_estimate=pl.CostEstimate(flops=1_000_000, bytes_accessed=500_000, transcendentals=0),
+        cost_estimate=pl.CostEstimate(flops=4_000_000_000, bytes_accessed=8_000_000, transcendentals=0),
         name="edge",
     )(core, *got_tops, long_top, grad_rows, long_taps, mixed_grad, short_taps, query_grad, value_grad)
-    gathered, query_grad, value_grad = lax.optimization_barrier((gathered, query_grad, value_grad))
-
     ways = lax.axis_size("tp")
     norms = pl.pallas_call(
         norm_kernel,
@@ -449,6 +448,7 @@
         compiler_params=params(SMALL),
         name="norm",
     )(gathered)
+    norms, gathered = lax.optimization_barrier((norms, gathered))
     norms = lax.all_to_all(norms, ("tp", "dp"), 0, 0, tiled=True)
     other = lax.ppermute(gathered, "dp", [(0, 1), (1, 0)])
     limit = math.sqrt((long_len + short_len) * chan_width * ways)

time: 120 us -> 118 us (0.983)
  blocking collectives: 16.2 us -> 0 us
  starting transfers between devices: 54.5 us -> 65.2 us
  waiting for transfers between devices: 16.3 us -> 19.2 us
    all_to_all x1 -> x0, blocking collectives: 16.2 us -> none  [on_device(): norms = lax.all_to_all(norms, ('tp', 'dp'), 0, 0, tiled=True)]
    all_to_all x0 -> x1, starting transfers between devices: none -> 15.6 us  [on_device(): norms = lax.all_to_all(norms, ('tp', 'dp'), 0, 0, tiled=True)]
    ppermute x1, starting transfers between devices: 5.71 us -> 1.91 us  [on_device(): other = lax.ppermute(gathered, 'dp', [(0, 1), (1, 0)])]
    ppermute x6, waiting for transfers between devices: 0.02 us -> 3.01 us  [swapped(): lax.ppermute(value, 'ctx', [(i, i + 1) for i in starts] + [(i + 1, i) for...]
  transfers between devices with their start and end apart: 11 -> 12, of which waited for: 3 -> 5; matrix products, arithmetic and copies ran while one was open for 0% -> 0% of each run, Pallas kernels for 19% -> 19%
where the time goes in v8:
time: 118 us; the launch traced here: 117 us
  starting transfers between devices  65.2 us (55%)
  Pallas kernels  28.6 us (24%)
  waiting for transfers between devices  19.2 us (16%)
  other arithmetic  1.76 us (1%)
  local copies, waits for them, and re-layouts  1.6 us (1%)
    ppermute x6, starting transfers between devices, swapped(): lax.ppermute(value, 'ctx', [(i, i + 1) for i in starts] + [(i + 1, i) for...  24.5 us
    pallas_call x6, Pallas kernels, call(): pl.pallas_call(kernel, out_shape=out_shape, grid_spec=pltpu.PrefetchScala...  23.4 us
    all_to_all x3, starting transfers between devices, swap(): lax.all_to_all(value, 'ctx', 0, 0, tiled=True, axis_index_groups=groups)  19.6 us
    all_to_all x1, starting transfers between devices, on_device(): norms = lax.all_to_all(norms, ('tp', 'dp'), 0, 0, tiled=True)  15.6 us
    all_to_all x3, waiting for transfers between devices, swap(): lax.all_to_all(value, 'ctx', 0, 0, tiled=True, axis_index_groups=groups)  15.4 us
    ppermute x1, starting transfers between devices, on_device(): part_got = lax.ppermute(part_sent, 'dp', [(0, 1), (1, 0)])  3.69 us
    ppermute x6, waiting for transfers between devices, swapped(): lax.ppermute(value, 'ctx', [(i, i + 1) for i in starts] + [(i + 1, i) for...  3.01 us
  transfers between devices with their start and end apart: 12, of which 5 were waited for; matrix products, arithmetic and copies ran while one was open for 0% of the time, Pallas kernels for 19%

profile of v8, /device:TPU:1, one launch (start us, length us, event | category | flops | bytes accessed | tf_op | source)
XLA Modules:
  0.0 117.2 jit_solution(8433127061988902303)
XLA Ops:
  0.6 2.9 %gates_0.1 = (bf16[128,1024]{1,0:T(8,128)(2,1)}, bf16[128,1024]{1,0:T(8,128)(2,1)}, bf16[128,1024]{1,0:T(8,128)(2,1)}) custom-call(s32[1]{0:T(128)} %bitcast.place_ref, bf16[128,2048]{1,0:T(8,128)(2,1)} %bitcast.8, bf16[128,2048]{1,0:T(8,128)(2,1)} %bitcast.10, bf16[128,2048]{1,0:T(8,128)(2,1)} %bitcast.14, bf16[128,2048]{1,0:T(8,128)(2,1)} %bitcast.18, ...), custom_call_target="tpu_custom_call" | custom-call | flops 1000 | bytes 1000 | tf_op jit(solution)/shard_map/gates_0/pallas_call | solution.py:333
  3.5 0.7 collective-permute-start.2
  4.2 8.2 %collective-permute-start.3 = (bf16[128,1024]{1,0:T(8,128)(2,1)}, bf16[128,1024]{1,0:T(8,128)(2,1)S(1)}, u32[]{:S(2)}, u32[]{:S(2)}) collective-permute-start(bf16[128,1024]{1,0:T(8,128)(2,1)} %get-tuple-element.74.sent_b_ref), channel_id=1, source_target_pairs={{0,8},{16,24},{32,40},{48,56},{64,72},{80,88},{96,104},{112,120},{... | collective-permute-start | bytes 786440 | tf_op jit(solution)/shard_map/ppermute | solution.py:313
  12.3 2.9 %gates_1.1 = (bf16[128,1024]{1,0:T(8,128)(2,1)}, bf16[128,1024]{1,0:T(8,128)(2,1)}, bf16[128,1024]{1,0:T(8,128)(2,1)}) custom-call(s32[1]{0:T(128)} %bitcast.place_ref, bf16[128,2048]{1,0:T(8,128)(2,1)} %bitcast.9, bf16[128,2048]{1,0:T(8,128)(2,1)} %bitcast.11, bf16[128,2048]{1,0:T(8,128)(2,1)} %bitcast.15, bf16[128,2048]{1,0:T(8,128)(2,1)} %bitcast.19, ...), custom_call_target="tpu_custom_call" | custom-call | flops 1000 | bytes 1000 | tf_op jit(solution)/shard_map/gates_1/pallas_call | solution.py:333
  15.2 0.7 collective-permute-start
  15.9 8.5 %collective-permute-start.1 = (bf16[128,1024]{1,0:T(8,128)(2,1)}, bf16[128,1024]{1,0:T(8,128)(2,1)S(1)}, u32[]{:S(2)}, u32[]{:S(2)}) collective-permute-start(bf16[128,1024]{1,0:T(8,128)(2,1)} %get-tuple-element.81.sent_b_ref), channel_id=1, source_target_pairs={{0,8},{16,24},{32,40},{48,56},{64,72},{80,88},{96,104},{112,120},{... | collective-permute-start | bytes 786440 | tf_op jit(solution)/shard_map/ppermute | solution.py:313
  24.4 0.0 collective-permute-done.2.got_a_ref
  24.5 0.0 copy-start.2
  24.5 0.0 collective-permute-done.3.got_b_ref
  24.5 0.0 copy-start.3
  24.5 0.7 copy-done.2
  25.2 0.1 copy-done.3
  25.3 4.8 %sums_0.1 = (bf16[128,2048]{1,0:T(8,128)(2,1)}, bf16[128,2048]{1,0:T(8,128)(2,1)}, bf16[8,2048]{1,0:T(8,128)(2,1)}, bf16[8,2048]{1,0:T(8,128)(2,1)}, bf16[8,144,128]{2,1,0:T(8,128)(2,1)}) custom-call(s32[1]{0:T(128)} %bitcast.place_ref, bf16[128,1024]{1,0:T(8,128)(2,1)} %get-tuple-element.73.sent_a_ref, bf16[128,1024]{1,0:T(8,128)(2,1)} %get-tuple-element.74.sent_b_ref, ...), custom_call_target="tpu_custom_call" | custom-call | flops 6000000000 | bytes 8000000 | tf_op jit(solution)/shard_map/sums_0/pallas_call | solution.py:333
  30.1 3.7 %collective-permute-start.4 = (bf16[8,144,128]{2,1,0:T(8,128)(2,1)}, bf16[8,144,128]{2,1,0:T(8,128)(2,1)S(1)}, u32[]{:S(2)}, u32[]{:S(2)}) collective-permute-start(bf16[8,144,128]{2,1,0:T(8,128)(2,1)} %get-tuple-element.67), channel_id=1, source_target_pairs={{0,1},{1,0},{2,3},{3,2},{4,5},{5,4},{6,7},{7,6},{8,9},{9,8},{10,11... | collective-permute-start | bytes 884744 | tf_op jit(solution)/shard_map/ppermute | solution.py:397
  33.8 0.0 collective-permute-done.got_a_ref
  33.8 0.0 copy-start
  33.8 0.0 collective-permute-done.1.got_b_ref
  33.9 0.0 copy-start.1
  33.9 0.7 copy-done
  34.6 0.1 copy-done.1
  34.7 4.8 %sums_1.1 = (bf16[128,2048]{1,0:T(8,128)(2,1)}, bf16[128,2048]{1,0:T(8,128)(2,1)}, bf16[8,2048]{1,0:T(8,128)(2,1)}, bf16[8,2048]{1,0:T(8,128)(2,1)}, bf16[8,144,128]{2,1,0:T(8,128)(2,1)}) custom-call(s32[1]{0:T(128)} %bitcast.place_ref, ...), custom_call_target="tpu_custom_call", output_to_operand_aliasing={{0}: (15, {}), {1}: (16, {}), {2}: (17, {}), {3}: (18, {})} | custom-call | flops 6000000000 | bytes 8000000 | tf_op jit(solution)/shard_map/sums_1/pallas_call | solution.py:333
  39.5 0.0 collective-permute-done.4
  39.5 1.8 %add_convert_fusion = bf16[8,144,128]{2,1,0:T(8,128)(2,1)} fusion(bf16[8,144,128]{2,1,0:T(8,128)(2,1)S(1)} %collective-permute-done.4, bf16[8,144,128]{2,1,0:T(8,128)(2,1)} %get-tuple-element.66), kind=kLoop, calls=%fused_computation | loop fusion | flops 589824 | bytes 884736 | tf_op jit(solution)/shard_map/convert_element_type | solution.py:412
  41.3 0.0 copy-start.6
  41.3 0.0 copy-start.7
  41.3 5.1 %all-to-all-start = ((bf16[8,144,128]{2,1,0:T(8,128)(2,1)}), bf16[8,144,128]{2,1,0:T(8,128)(2,1)S(1)}, u32[]{:S(2)}, u32[]{:S(2)}) async-start(bf16[8,144,128]{2,1,0:T(8,128)(2,1)} %add_convert_fusion), calls=%async_computation | async-start | bytes 589824 | tf_op jit(solution)/shard_map/all_to_all | solution.py:407
  46.4 0.0 copy-done.6
  46.4 0.7 collective-permute-start.5
  47.0 0.0 copy-done.7
  47.0 5.8 %collective-permute-start.6 = (bf16[8,2048]{1,0:T(8,128)(2,1)S(1)}, bf16[8,2048]{1,0:T(8,128)(2,1)S(1)}, u32[]{:S(2)}, u32[]{:S(2)}) collective-permute-start(bf16[8,2048]{1,0:T(8,128)(2,1)S(1)} %copy-done.7), channel_id=1, source_target_pairs={{0,8},{16,24},{32,40},{48,56},{64,72},{80,88},{96,104},{112,120},{... | collective-permute-start | bytes 98312 | tf_op jit(solution)/shard_map/ppermute | solution.py:313
  52.8 0.0 collective-permute-done.5.got_a_ref
  52.8 0.0 copy-start.4
  52.9 3.0 %collective-permute-done.6.got_b_ref = bf16[8,2048]{1,0:T(8,128)(2,1)S(1)} collective-permute-done((bf16[8,2048]{1,0:T(8,128)(2,1)S(1)}, bf16[8,2048]{1,0:T(8,128)(2,1)S(1)}, u32[]{:S(2)}, u32[]{:S(2)}) %collective-permute-start.6) | collective-permute-done | bytes 32800 | tf_op jit(solution)/shard_map/ppermute | solution.py:313
  55.9 0.0 copy-start.5
  55.9 3.6 %all-to-all-done.arrived_ref = bf16[8,144,128]{2,1,0:T(8,128)(2,1)S(1)} async-done(((bf16[8,144,128]{2,1,0:T(8,128)(2,1)}), bf16[8,144,128]{2,1,0:T(8,128)(2,1)S(1)}, u32[]{:S(2)}, u32[]{:S(2)}) %all-to-all-start) | async-done | bytes 294944 | tf_op jit(solution)/shard_map/all_to_all | solution.py:407
  59.4 0.8 line.1
  60.2 0.0 copy-done.4
  60.2 0.0 copy-done.5
  60.2 11.1 %all-to-all-start.1 = ((bf16[8,144,128]{2,1,0:T(8,128)(2,1)}), bf16[8,144,128]{2,1,0:T(8,128)(2,1)S(1)}, u32[]{:S(2)}, u32[]{:S(2)}) async-start(bf16[8,144,128]{2,1,0:T(8,128)(2,1)} %line.1), calls=%async_computation.1 | async-start | bytes 589824 | tf_op jit(solution)/shard_map/all_to_all | solution.py:407
  71.3 4.0 %rest_0.1 = (bf16[128,2048]{1,0:T(8,128)(2,1)}, bf16[128,2048]{1,0:T(8,128)(2,1)}, f32[8,2048]{1,0:T(8,128)}) custom-call(s32[1]{0:T(128)} %bitcast.place_ref, bf16[128,1024]{1,0:T(8,128)(2,1)} %get-tuple-element.73.sent_a_ref, bf16[128,1024]{1,0:T(8,128)(2,1)} %get-tuple-element.74.sent_b_ref, bf16[128,1024]{1,0:T(8,128)(2,1)} %copy-done.2, ...), custom_call_target="tpu_custom_call" | custom-call | flops 2000000000 | bytes 4000000 | tf_op jit(solution)/shard_map/rest_0/pallas_call | solution.py:333
  75.2 6.1 %all-to-all-done.1.arrived_ref = bf16[8,144,128]{2,1,0:T(8,128)(2,1)S(1)} async-done(((bf16[8,144,128]{2,1,0:T(8,128)(2,1)}), bf16[8,144,128]{2,1,0:T(8,128)(2,1)S(1)}, u32[]{:S(2)}, u32[]{:S(2)}) %all-to-all-start.1) | async-done | bytes 294944 | tf_op jit(solution)/shard_map/all_to_all | solution.py:407
  81.4 0.8 piece.1
  82.2 3.4 %all-to-all-start.2 = ((bf16[8,144,128]{2,1,0:T(8,128)(2,1)}), bf16[8,144,128]{2,1,0:T(8,128)(2,1)S(1)}, u32[]{:S(2)}, u32[]{:S(2)}) async-start(bf16[8,144,128]{2,1,0:T(8,128)(2,1)} %piece.1), calls=%async_computation.2 | async-start | bytes 589824 | tf_op jit(solution)/shard_map/all_to_all | solution.py:407
  85.6 4.0 %rest_1.1 = (bf16[128,2048]{1,0:T(8,128)(2,1)}, bf16[128,2048]{1,0:T(8,128)(2,1)}, f32[8,2048]{1,0:T(8,128)}) custom-call(s32[1]{0:T(128)} %bitcast.place_ref, bf16[128,1024]{1,0:T(8,128)(2,1)} %get-tuple-element.80.sent_a_ref, bf16[128,1024]{1,0:T(8,128)(2,1)} %get-tuple-element.81.sent_b_ref, ...), custom_call_target="tpu_custom_call", output_to_operand_aliasing={{0}: (15, {}), {1}: (16, {}), {2}: (17, {})} | custom-call | flops 2000000000 | bytes 4000000 | tf_op jit(solution)/shard_map/rest_1/pallas_call | solution.py:333
  89.6 5.7 %all-to-all-done.2.pieces_ref.mine_ref = bf16[8,144,128]{2,1,0:T(8,128)(2,1)S(1)} async-done(((bf16[8,144,128]{2,1,0:T(8,128)(2,1)}), bf16[8,144,128]{2,1,0:T(8,128)(2,1)S(1)}, u32[]{:S(2)}, u32[]{:S(2)}) %all-to-all-start.2) | async-done | bytes 294944 | tf_op jit(solution)/shard_map/all_to_all | solution.py:407
  95.3 0.6 norm.1
  95.9 15.6 %all-to-all-start.3 = ((f32[8,1,128]{2,1,0:T(1,128)}), f32[8,1,128]{2,1,0:T(1,128)S(1)}, u32[]{:S(2)}, u32[]{:S(2)}) async-start(f32[8,1,128]{2,1,0:T(1,128)} %norm.1), calls=%async_computation.3 | async-start | bytes 8192 | tf_op jit(solution)/shard_map/all_to_all | solution.py:452
  111.5 1.9 %collective-permute-start.7 = (bf16[8,144,128]{2,1,0:T(8,128)(2,1)S(1)}, bf16[8,144,128]{2,1,0:T(8,128)(2,1)S(1)}, u32[]{:S(2)}, u32[]{:S(2)}) collective-permute-start(bf16[8,144,128]{2,1,0:T(8,128)(2,1)S(1)} %all-to-all-done.2.pieces_ref.mine_ref), channel_id=1, source_target_pairs={{0,1},{1,0},{2,3},{3,2},{4,5},{5,4},{6,7},{7,6},{8,9},{9,8},{10,11... | collective-permute-start | bytes 884744 | tf_op jit(solution)/shard_map/ppermute | solution.py:453
  113.4 2.0 %edge.1 = (bf16[128,2048]{1,0:T(8,128)(2,1)}, bf16[128,2048]{1,0:T(8,128)(2,1)}) custom-call(s32[1]{0:T(128)} %bitcast.place_ref, bf16[8,2048]{1,0:T(8,128)(2,1)} %copy-done.4, bf16[8,2048]{1,0:T(8,128)(2,1)} %copy-done.5, f32[8,2048]{1,0:T(8,128)} %get-tuple-element.88.long_top_ref, ...), custom_call_target="tpu_custom_call", output_to_operand_aliasing={{0}: (8, {}), {1}: (9, {})} | custom-call | flops 4000000000 | bytes 8000000 | tf_op jit(solution)/shard_map/edge/pallas_call | solution.py:426
  115.4 0.8 all-to-all-done.3.norms_ref
  116.3 0.0 collective-permute-done.7.other_ref
  116.3 0.9 scale.1
Async XLA Ops:
  3.5 21.0 %collective-permute-start.2 = (bf16[128,1024]{1,0:T(8,128)(2,1)}, bf16[128,1024]{1,0:T(8,128)(2,1)S(1)}, u32[]{:S(2)}, u32[]{:S(2)}) collective-permute-start(bf16[128,1024]{1,0:T(8,128)(2,1)} %get-tuple-element.73.sent_a_ref), channel_id=1, source_target_pairs={{8,16},{24,32},{40,48},{56,64},{72,80},{88,96},{104,112},{120,128}... | collective-permute-start | bytes 786440 | tf_op jit(solution)/shard_map/ppermute | solution.py:313
  4.2 20.3 %collective-permute-start.3 = (bf16[128,1024]{1,0:T(8,128)(2,1)}, bf16[128,1024]{1,0:T(8,128)(2,1)S(1)}, u32[]{:S(2)}, u32[]{:S(2)}) collective-permute-start(bf16[128,1024]{1,0:T(8,128)(2,1)} %get-tuple-element.74.sent_b_ref), channel_id=1, source_target_pairs={{0,8},{16,24},{32,40},{48,56},{64,72},{80,88},{96,104},{112,120},{... | collective-permute-start | bytes 786440 | tf_op jit(solution)/shard_map/ppermute | solution.py:313
  15.2 18.6 %collective-permute-start = (bf16[128,1024]{1,0:T(8,128)(2,1)}, bf16[128,1024]{1,0:T(8,128)(2,1)S(1)}, u32[]{:S(2)}, u32[]{:S(2)}) collective-permute-start(bf16[128,1024]{1,0:T(8,128)(2,1)} %get-tuple-element.80.sent_a_ref), channel_id=1, source_target_pairs={{8,16},{24,32},{40,48},{56,64},{72,80},{88,96},{104,112},{120,128}... | collective-permute-start | bytes 786440 | tf_op jit(solution)/shard_map/ppermute | solution.py:313
  15.9 17.9 %collective-permute-start.1 = (bf16[128,1024]{1,0:T(8,128)(2,1)}, bf16[128,1024]{1,0:T(8,128)(2,1)S(1)}, u32[]{:S(2)}, u32[]{:S(2)}) collective-permute-start(bf16[128,1024]{1,0:T(8,128)(2,1)} %get-tuple-element.81.sent_b_ref), channel_id=1, source_target_pairs={{0,8},{16,24},{32,40},{48,56},{64,72},{80,88},{96,104},{112,120},{... | collective-permute-start | bytes 786440 | tf_op jit(solution)/shard_map/ppermute | solution.py:313
  24.5 0.7 copy-start.2
  24.5 0.8 copy-start.3
  30.1 9.4 %collective-permute-start.4 = (bf16[8,144,128]{2,1,0:T(8,128)(2,1)}, bf16[8,144,128]{2,1,0:T(8,128)(2,1)S(1)}, u32[]{:S(2)}, u32[]{:S(2)}) collective-permute-start(bf16[8,144,128]{2,1,0:T(8,128)(2,1)} %get-tuple-element.67), channel_id=1, source_target_pairs={{0,1},{1,0},{2,3},{3,2},{4,5},{5,4},{6,7},{7,6},{8,9},{9,8},{10,11... | collective-permute-start | bytes 884744 | tf_op jit(solution)/shard_map/ppermute | solution.py:397
  33.8 0.7 copy-start
  33.9 0.8 copy-start.1
  41.3 5.1 %copy-start.6 = (bf16[8,2048]{1,0:T(8,128)(2,1)S(1)}, bf16[8,2048]{1,0:T(8,128)(2,1)}, u32[]{:S(2)}) copy-start(bf16[8,2048]{1,0:T(8,128)(2,1)} %get-tuple-element.68.top_a_ref) | copy-start | bytes 98308
  41.3 5.8 %copy-start.7 = (bf16[8,2048]{1,0:T(8,128)(2,1)S(1)}, bf16[8,2048]{1,0:T(8,128)(2,1)}, u32[]{:S(2)}) copy-start(bf16[8,2048]{1,0:T(8,128)(2,1)} %get-tuple-element.69.top_b_ref) | copy-start | bytes 98308
  41.3 18.2 %all-to-all-start = ((bf16[8,144,128]{2,1,0:T(8,128)(2,1)}), bf16[8,144,128]{2,1,0:T(8,128)(2,1)S(1)}, u32[]{:S(2)}, u32[]{:S(2)}) async-start(bf16[8,144,128]{2,1,0:T(8,128)(2,1)} %add_convert_fusion), calls=%async_computation | async-start | bytes 589824 | tf_op jit(solution)/shard_map/all_to_all | solution.py:407
  46.4 6.5 %collective-permute-start.5 = (bf16[8,2048]{1,0:T(8,128)(2,1)S(1)}, bf16[8,2048]{1,0:T(8,128)(2,1)S(1)}, u32[]{:S(2)}, u32[]{:S(2)}) collective-permute-start(bf16[8,2048]{1,0:T(8,128)(2,1)S(1)} %copy-done.6), channel_id=1, source_target_pairs={{8,16},{24,32},{40,48},{56,64},{72,80},{88,96},{104,112},{120,128}... | collective-permute-start | bytes 98312 | tf_op jit(solution)/shard_map/ppermute | solution.py:313
  47.0 8.8 %collective-permute-start.6 = (bf16[8,2048]{1,0:T(8,128)(2,1)S(1)}, bf16[8,2048]{1,0:T(8,128)(2,1)S(1)}, u32[]{:S(2)}, u32[]{:S(2)}) collective-permute-start(bf16[8,2048]{1,0:T(8,128)(2,1)S(1)} %copy-done.7), channel_id=1, source_target_pairs={{0,8},{16,24},{32,40},{48,56},{64,72},{80,88},{96,104},{112,120},{... | collective-permute-start | bytes 98312 | tf_op jit(solution)/shard_map/ppermute | solution.py:313
  52.8 7.3 %copy-start.4 = (bf16[8,2048]{1,0:T(8,128)(2,1)}, bf16[8,2048]{1,0:T(8,128)(2,1)S(1)}, u32[]{:S(2)}) copy-start(bf16[8,2048]{1,0:T(8,128)(2,1)S(1)} %collective-permute-done.5.got_a_ref) | copy-start | bytes 98308
  55.9 4.3 %copy-start.5 = (bf16[8,2048]{1,0:T(8,128)(2,1)}, bf16[8,2048]{1,0:T(8,128)(2,1)S(1)}, u32[]{:S(2)}) copy-start(bf16[8,2048]{1,0:T(8,128)(2,1)S(1)} %collective-permute-done.6.got_b_ref) | copy-start | bytes 98308
  60.2 21.2 %all-to-all-start.1 = ((bf16[8,144,128]{2,1,0:T(8,128)(2,1)}), bf16[8,144,128]{2,1,0:T(8,128)(2,1)S(1)}, u32[]{:S(2)}, u32[]{:S(2)}) async-start(bf16[8,144,128]{2,1,0:T(8,128)(2,1)} %line.1), calls=%async_computation.1 | async-start | bytes 589824 | tf_op jit(solution)/shard_map/all_to_all | solution.py:407
  82.2 13.1 %all-to-all-start.2 = ((bf16[8,144,128]{2,1,0:T(8,128)(2,1)}), bf16[8,144,128]{2,1,0:T(8,128)(2,1)S(1)}, u32[]{:S(2)}, u32[]{:S(2)}) async-start(bf16[8,144,128]{2,1,0:T(8,128)(2,1)} %piece.1), calls=%async_computation.2 | async-start | bytes 589824 | tf_op jit(solution)/shard_map/all_to_all | solution.py:407
  95.9 20.3 %all-to-all-start.3 = ((f32[8,1,128]{2,1,0:T(1,128)}), f32[8,1,128]{2,1,0:T(1,128)S(1)}, u32[]{:S(2)}, u32[]{:S(2)}) async-start(f32[8,1,128]{2,1,0:T(1,128)} %norm.1), calls=%async_computation.3 | async-start | bytes 8192 | tf_op jit(solution)/shard_map/all_to_all | solution.py:452
  111.5 4.8 %collective-permute-start.7 = (bf16[8,144,128]{2,1,0:T(8,128)(2,1)S(1)}, bf16[8,144,128]{2,1,0:T(8,128)(2,1)S(1)}, u32[]{:S(2)}, u32[]{:S(2)}) collective-permute-start(bf16[8,144,128]{2,1,0:T(8,128)(2,1)S(1)} %all-to-all-done.2.pieces_ref.mine_ref), channel_id=1, source_target_pairs={{0,1},{1,0},{2,3},{3,2},{4,5},{5,4},{6,7},{7,6},{8,9},{9,8},{10,11... | collective-permute-start | bytes 884744 | tf_op jit(solution)/shard_map/ppermute | solution.py:453
